TPU v7x, 512 devices: a whole 4x4x16 slice. The times are simulated.
512 devices in a mesh: dp: 32 (over x, y, core), ctx: 16 (over z).
Axes of the slice: x: 4, y: 4, z: 16, core: 2. Of those that a mesh axis runs over, the one named last changes fastest.
Arguments:
- query_rows: bfloat16 [65536, 1024], P(('dp', 'ctx')), may hold values from -6 to 6
- key_rows: bfloat16 [65536, 1024], P(('dp', 'ctx')), may hold values from -6 to 6
- value_rows: bfloat16 [65536, 1024], P(('dp', 'ctx')), may hold values from -6 to 6
- gate_rows: bfloat16 [65536, 1024], P(('dp', 'ctx')), may hold values from -6 to 6
- out_grad: bfloat16 [65536, 1024], P(('dp', 'ctx')), may hold values from -24 to 24
- proj_weight: bfloat16 [1024, 1024], P(('dp', 'ctx')), may hold values from -0.1875 to 0.1875
- user_lengths: int32 [32, 4], P('dp'), may hold values from 1 to 1024, 2048 in all within a row
Outputs:
- query_grad: bfloat16 [65536, 1024], P(('dp', 'ctx'))
- key_grad: bfloat16 [65536, 1024], P(('dp', 'ctx'))
- value_grad: bfloat16 [65536, 1024], P(('dp', 'ctx'))
- gate_grad: bfloat16 [65536, 1024], P(('dp', 'ctx'))
- proj_grad: float32 [1024, 1024], P('dp')
Inputs may be any that keep to these rules, and one draw needn't show every extreme that they name: `user_lengths`: each row sums to 2048; its largest entry is exactly 1024.
All inputs are finite; a program needn't handle non-finite values.
Results may differ from a plain program's by a relative error of at most 0.013.
Values may be sent and summed in bfloat16 or wider, within the bound.
No kernel may reach another device: no remote copies, remote signals or barrier semaphores. Data moves between devices by JAX's collectives and lax.ppermute only.
A program may use at most 128 MiB of HBM per device.

v0:
```python
import math

import jax
import jax.numpy as jnp
from jax import lax
from jax.sharding import PartitionSpec as P

DH = 64


def silu_slope(scores):
    sigmoid = jax.nn.sigmoid(scores)
    return sigmoid * (1.0 + scores * (1.0 - sigmoid))


def user_tables(lengths_row, group_size):
    ends = jnp.cumsum(lengths_row)
    starts = ends - lengths_row
    position = jnp.arange(group_size, dtype=jnp.int32)
    member = (position[:, None] >= starts[None, :]) & (position[:, None] < ends[None, :])
    user_ids = jnp.sum((position[:, None] >= ends[None, :]).astype(jnp.int32), axis=1)
    inverse = jnp.sum(
        jnp.where(member, 1.0 / lengths_row.astype(jnp.float32)[None, :], jnp.float32(0.0)), axis=1
    )
    return (user_ids, inverse)


def tile_weight(user_ids, inverse, row_block, col_block, block_size):
    row_pos = row_block * block_size + jnp.arange(block_size, dtype=jnp.int32)
    col_pos = col_block * block_size + jnp.arange(block_size, dtype=jnp.int32)
    row_users = user_ids[row_block * block_size : (row_block + 1) * block_size]
    col_users = user_ids[col_block * block_size : (col_block + 1) * block_size]
    row_inverse = inverse[row_block * block_size : (row_block + 1) * block_size]
    allowed = (row_users[:, None] == col_users[None, :]) & (col_pos[None, :] <= row_pos[:, None])
    return jnp.where(allowed, row_inverse[:, None], jnp.float32(0.0))


def tile_scores(query_tile, key_tile, scale):
    return (
        jnp.einsum("qhd,khd->hqk", query_tile, key_tile, preferred_element_type=jnp.float32) * scale
    )


def local(query_rows, key_rows, value_rows, gate_rows, out_grad, proj_weight, user_lengths):
    ctx_devices = lax.axis_size("ctx")
    tok_count = query_rows.shape[0]
    width = query_rows.shape[1]
    group_size = tok_count * ctx_devices
    head_cols = width // ctx_devices
    heads_here = head_cols // DH
    scale = 1.0 / math.sqrt(DH)
    block_size = tok_count * min(ctx_devices, 2)
    block_count = group_size // block_size
    query_heads, key_heads, value_heads = (
        lax.all_to_all(query_rows, "ctx", split_axis=1, concat_axis=0, tiled=True),
        lax.all_to_all(key_rows, "ctx", split_axis=1, concat_axis=0, tiled=True),
        lax.all_to_all(value_rows, "ctx", split_axis=1, concat_axis=0, tiled=True),
    )
    query_heads = query_heads.reshape(group_size, heads_here, DH)
    key_heads = key_heads.reshape(group_size, heads_here, DH)
    value_heads = value_heads.reshape(group_size, heads_here, DH)
    user_ids, inverse = user_tables(user_lengths[0], group_size)
    forward_blocks = []
    for row_block in range(block_count):
        query_tile = query_heads[row_block * block_size : (row_block + 1) * block_size]
        accum_out = jnp.zeros((block_size, heads_here, DH), jnp.float32)
        for col_block in range(row_block + 1):
            key_tile = key_heads[col_block * block_size : (col_block + 1) * block_size]
            value_tile = value_heads[col_block * block_size : (col_block + 1) * block_size]
            weight = tile_weight(user_ids, inverse, row_block, col_block, block_size)

            def forward_tile(
                total,
                query_tile=query_tile,
                key_tile=key_tile,
                value_tile=value_tile,
                weight=weight,
            ):
                scores = tile_scores(query_tile, key_tile, scale)
                attn = (jax.nn.silu(scores) * weight[None]).astype(jnp.bfloat16)
                return total + jnp.einsum(
                    "hqk,khd->qhd", attn, value_tile, preferred_element_type=jnp.float32
                )

            accum_out = forward_tile(accum_out)
        forward_blocks.append(accum_out.astype(jnp.bfloat16))
    attn_heads = jnp.concatenate(forward_blocks, axis=0).reshape(group_size, head_cols)
    attn_out = lax.all_to_all(attn_heads, "ctx", split_axis=0, concat_axis=1, tiled=True)
    centred = attn_out.astype(jnp.float32)
    centred = centred - jnp.mean(centred, axis=1, keepdims=True)
    rstd = lax.rsqrt(jnp.mean(centred * centred, axis=1, keepdims=True) + 1e-05)
    normed = centred * rstd
    gates = gate_rows.astype(jnp.float32)
    gated = (normed * gates).astype(jnp.bfloat16)
    gated_grad = jnp.einsum(
        "te,re->tr",
        out_grad,
        lax.all_gather(proj_weight, ("dp", "ctx"), axis=0, tiled=True),
        preferred_element_type=jnp.float32,
    )
    gate_grad = (gated_grad * normed).astype(jnp.bfloat16)
    normed_grad = gated_grad * gates
    out_grad_attn = (
        normed_grad
        - jnp.mean(normed_grad, axis=1, keepdims=True)
        - normed * jnp.mean(normed_grad * normed, axis=1, keepdims=True)
    ) * rstd
    out_grad_attn = out_grad_attn.astype(jnp.bfloat16)
    grad_heads = lax.all_to_all(
        out_grad_attn, "ctx", split_axis=1, concat_axis=0, tiled=True
    ).reshape(group_size, heads_here, DH)
    query_acc = [jnp.zeros((block_size, heads_here, DH), jnp.float32) for _ in range(block_count)]
    key_acc = [jnp.zeros((block_size, heads_here, DH), jnp.float32) for _ in range(block_count)]
    value_acc = [jnp.zeros((block_size, heads_here, DH), jnp.float32) for _ in range(block_count)]
    for row_block in range(block_count):
        query_tile = query_heads[row_block * block_size : (row_block + 1) * block_size]
        grad_tile = grad_heads[row_block * block_size : (row_block + 1) * block_size]
        for col_block in range(row_block + 1):
            key_tile = key_heads[col_block * block_size : (col_block + 1) * block_size]
            value_tile = value_heads[col_block * block_size : (col_block + 1) * block_size]
            weight = tile_weight(user_ids, inverse, row_block, col_block, block_size)

            def backward_tile(
                totals,
                query_tile=query_tile,
                key_tile=key_tile,
                value_tile=value_tile,
                grad_tile=grad_tile,
                weight=weight,
            ):
                scores = tile_scores(query_tile, key_tile, scale)
                attn = (jax.nn.silu(scores) * weight[None]).astype(jnp.bfloat16)
                value_part = jnp.einsum(
                    "hqk,qhd->khd", attn, grad_tile, preferred_element_type=jnp.float32
                )
                attn_grad = jnp.einsum(
                    "qhd,khd->hqk", grad_tile, value_tile, preferred_element_type=jnp.float32
                )
                score_grad = (attn_grad * weight[None] * silu_slope(scores) * scale).astype(
                    jnp.bfloat16
                )
                query_part = jnp.einsum(
                    "hqk,khd->qhd", score_grad, key_tile, preferred_element_type=jnp.float32
                )
                key_part = jnp.einsum(
                    "hqk,qhd->khd", score_grad, query_tile, preferred_element_type=jnp.float32
                )
                return (totals[0] + query_part, totals[1] + key_part, totals[2] + value_part)

            current = (query_acc[row_block], key_acc[col_block], value_acc[col_block])
            updated = backward_tile(current)
            query_acc[row_block] = updated[0]
            key_acc[col_block] = updated[1]
            value_acc[col_block] = updated[2]
    query_back = (
        jnp.concatenate(query_acc, axis=0).astype(jnp.bfloat16).reshape(group_size, head_cols)
    )
    key_back = jnp.concatenate(key_acc, axis=0).astype(jnp.bfloat16).reshape(group_size, head_cols)
    value_back = (
        jnp.concatenate(value_acc, axis=0).astype(jnp.bfloat16).reshape(group_size, head_cols)
    )
    query_grad, key_grad, value_grad = (
        lax.all_to_all(query_back, "ctx", split_axis=0, concat_axis=1, tiled=True),
        lax.all_to_all(key_back, "ctx", split_axis=0, concat_axis=1, tiled=True),
        lax.all_to_all(value_back, "ctx", split_axis=0, concat_axis=1, tiled=True),
    )
    summed = lax.psum_scatter(
        jnp.einsum("tr,te->re", gated, out_grad, preferred_element_type=jnp.float32),
        ("dp", "ctx"),
        scatter_dimension=0,
        tiled=True,
    )
    proj_grad = lax.all_gather(summed, "ctx", axis=0, tiled=True)
    return (query_grad, key_grad, value_grad, gate_grad, proj_grad)


def solution(mesh):
    in_specs = (
        P(("dp", "ctx"), None),
        P(("dp", "ctx"), None),
        P(("dp", "ctx"), None),
        P(("dp", "ctx"), None),
        P(("dp", "ctx"), None),
        P(("dp", "ctx"), None),
        P("dp", None),
    )
    out_specs = (
        P(("dp", "ctx"), None),
        P(("dp", "ctx"), None),
        P(("dp", "ctx"), None),
        P(("dp", "ctx"), None),
        P("dp", None),
    )
    return jax.shard_map(local, mesh=mesh, in_specs=in_specs, out_specs=out_specs, check_vma=False)
```

profile of v0, /device:TPU:6, one launch (start us, length us, event | category | flops | bytes accessed | tf_op | source)
XLA Modules:
  0.0 790.7 jit_solution(1413111546133356601)
XLA Ops:
  7.2 1.8 copy.104
  9.0 15.2 %all-to-all-start = ((bf16[128,16,64]{0,2,1:T(8,128)(2,1)}), bf16[128,16,64]{0,2,1:T(8,128)(2,1)S(1)}, u32[]{:S(2)}, u32[]{:S(2)}) async-start(bf16[128,16,64]{0,2,1:T(8,128)(2,1)} %bitcast.1), calls=%async_computation | async-start | bytes 524288 | tf_op jit(solution)/shard_map/all_to_all | solution.py:55
  25.0 1.8 copy.106
  26.8 1.8 copy.108
  31.1 11.5 %all-to-all-done = bf16[128,16,64]{0,2,1:T(8,128)(2,1)S(1)} async-done(((bf16[128,16,64]{0,2,1:T(8,128)(2,1)}), bf16[128,16,64]{0,2,1:T(8,128)(2,1)S(1)}, u32[]{:S(2)}, u32[]{:S(2)}) %all-to-all-start) | async-done | bytes 262176 | tf_op jit(solution)/shard_map/all_to_all | solution.py:55
  42.6 5.8 all-to-all-start.1
  49.8 17.0 %all-to-all-done.1 = bf16[128,16,64]{0,2,1:T(8,128)(2,1)S(1)} async-done(((bf16[128,16,64]{0,2,1:T(8,128)(2,1)}), bf16[128,16,64]{0,2,1:T(8,128)(2,1)S(1)}, u32[]{:S(2)}, u32[]{:S(2)}) %all-to-all-start.1) | async-done | bytes 262176 | tf_op jit(solution)/shard_map/all_to_all | solution.py:56
  66.8 5.7 all-to-all-start.2
  94.7 1.6 fusion.200
  97.1 2.6 fusion.199
  100.7 2.6 fusion.220
  103.8 2.4 fusion.218
  107.0 2.5 fusion.219
  110.5 2.0 fusion.212
  121.7 30.1 %all_to_all.125 = bf16[16,128,64]{1,2,0:T(8,128)(2,1)S(1)} all-to-all(bf16[16,128,64]{1,2,0:T(8,128)(2,1)S(1)} %copy.131), channel_id=1, replica_groups=mesh['dp'=32,'ctx'=16] {'ctx'}, dimensions={0} | all-to-all | bytes 524288 | tf_op jit(solution)/shard_map/all_to_all | solution.py:88
  152.4 77.3 %all-gather.4.cloned.1.call-done = bf16[512,2,1024]{2,1,0:T(2,128)(2,1)} async-done(((bf16[1,2,1024]{2,1,0:T(2,128)(2,1)}), bf16[512,2,1024]{2,1,0:T(2,128)(2,1)}) %all-gather.4.cloned.1.call-update) | async-done | bytes 2097168 | tf_op jit(solution)/shard_map/all_gather | solution.py:98
  229.7 2.7 reshape.2236
  235.3 6.7 all-to-all-start.4
  242.2 2.9 fusion.221
  245.1 15.5 %all-to-all-done.4 = bf16[128,16,64]{0,2,1:T(8,128)(2,1)S(1)} async-done(((bf16[128,16,64]{0,2,1:T(8,128)(2,1)}), bf16[128,16,64]{0,2,1:T(8,128)(2,1)S(1)}, u32[]{:S(2)}, u32[]{:S(2)}) %all-to-all-start.4) | async-done | bytes 262176 | tf_op jit(solution)/shard_map/all_to_all | solution.py:109
  265.7 1.1 fusion.98
  283.4 1.3 fusion.79
  293.2 1.1 fusion.106
  294.3 1.1 fusion.105
  295.4 1.1 fusion.99
  315.1 5.9 all-to-all-start.7
  328.2 12.5 %all-to-all-done.7 = bf16[16,128,64]{1,2,0:T(8,128)(2,1)S(1)} async-done(((bf16[16,128,64]{1,2,0:T(8,128)(2,1)}), bf16[16,128,64]{1,2,0:T(8,128)(2,1)S(1)}, u32[]{:S(2)}, u32[]{:S(2)}) %all-to-all-start.7) | async-done | bytes 262176 | tf_op jit(solution)/shard_map/all_to_all | solution.py:165
  340.8 5.8 all-to-all-start.6
  348.1 17.6 %all-to-all-done.6 = bf16[16,128,64]{1,2,0:T(8,128)(2,1)S(1)} async-done(((bf16[16,128,64]{1,2,0:T(8,128)(2,1)}), bf16[16,128,64]{1,2,0:T(8,128)(2,1)S(1)}, u32[]{:S(2)}, u32[]{:S(2)}) %all-to-all-start.6) | async-done | bytes 262176 | tf_op jit(solution)/shard_map/all_to_all | solution.py:164
  365.8 6.3 all-to-all-start.5
  372.1 380.8 %all-reduce.3.cloned.1.call-done = f32[1024,1024]{1,0:T(8,128)} async-done(((f32[1024,1024]{1,0:T(8,128)}), f32[1024,1024]{1,0:T(8,128)}) %all-reduce.3.cloned.1.call-update) | async-done | bytes 4194320
  753.6 27.0 %all-gather.1 = f32[16,2,1024]{2,1,0:T(2,128)S(1)} all-gather(f32[1,2,1024]{2,1,0:T(2,128)S(1)} %dynamic-slice_bitcast_fusion), channel_id=1, replica_groups=mesh['dp'=32,'ctx'=16] {'ctx'}, dimensions={0}, use_global_device_ids=true | all-gather | bytes 139264 | tf_op jit(solution)/shard_map/all_gather | solution.py:173
  (573 shorter events, 102.7 us)
Async XLA Ops:
  7.2 225.3 %copy-start = (bf16[128,1024]{1,0:T(8,128)(2,1)S(1)}, bf16[128,1024]{1,0:T(8,128)(2,1)}, u32[]{:S(2)}) copy-start(bf16[128,1024]{1,0:T(8,128)(2,1)} %param.11) | copy-start | bytes 786436
  7.2 21.4 %copy-start.156 = (s32[1,4]{1,0:T(1,128)S(1)}, s32[1,4]{1,0:T(1,128)}, u32[]{:S(2)}) copy-start(s32[1,4]{1,0:T(1,128)} %param.13) | copy-start | bytes 52
  9.0 33.6 %all-to-all-start = ((bf16[128,16,64]{0,2,1:T(8,128)(2,1)}), bf16[128,16,64]{0,2,1:T(8,128)(2,1)S(1)}, u32[]{:S(2)}, u32[]{:S(2)}) async-start(bf16[128,16,64]{0,2,1:T(8,128)(2,1)} %bitcast.1), calls=%async_computation | async-start | bytes 524288 | tf_op jit(solution)/shard_map/all_to_all | solution.py:55
  24.2 205.5 %all-gather.4.cloned.1.call-start = ((), (), s32[]{:S(2)}) async-start(), calls=%async_computation.8 | async-start | bytes 2101248 | tf_op jit(solution)/shard_map/all_gather | solution.py:98
  42.6 24.2 %all-to-all-start.1 = ((bf16[128,16,64]{0,2,1:T(8,128)(2,1)}), bf16[128,16,64]{0,2,1:T(8,128)(2,1)S(1)}, u32[]{:S(2)}, u32[]{:S(2)}) async-start(bf16[128,16,64]{0,2,1:T(8,128)(2,1)} %bitcast.3), calls=%async_computation.1 | async-start | bytes 524288 | tf_op jit(solution)/shard_map/all_to_all | solution.py:56
  49.1 47.9 %copy-start.150 = (f32[256]{0:T(256)}, f32[256]{0:T(256)S(1)}, u32[]{:S(2)}) copy-start(f32[256]{0:T(256)S(1)} %get-tuple-element.71) | copy-start | bytes 3076
  49.1 51.4 %copy-start.152 = (f32[256]{0:T(256)}, f32[256]{0:T(256)S(1)}, u32[]{:S(2)}) copy-start(f32[256]{0:T(256)S(1)} %get-tuple-element.70) | copy-start | bytes 3076
  49.1 51.4 %copy-start.154 = (f32[256]{0:T(256)}, f32[256]{0:T(256)S(1)}, u32[]{:S(2)}) copy-start(f32[256]{0:T(256)S(1)} %get-tuple-element.69) | copy-start | bytes 3076
  49.7 50.8 %copy-start.148 = (s32[256]{0:T(256)}, s32[256]{0:T(256)S(1)}, u32[]{:S(2)}) copy-start(s32[256]{0:T(256)S(1)} %get-tuple-element.63) | copy-start | bytes 3076
  49.7 43.4 %copy-start.2 = (bf16[2,8,8,128]{3,2,1,0:T(8,128)(2,1)}, bf16[2,8,8,128]{3,2,1,0:T(8,128)(2,1)S(1)}, u32[]{:S(2)}) copy-start(bf16[2,8,8,128]{3,2,1,0:T(8,128)(2,1)S(1)} %get-tuple-element.53) | copy-start | bytes 98308
  49.8 43.8 %copy-start.10 = (bf16[2,8,8,128]{3,2,1,0:T(8,128)(2,1)}, bf16[2,8,8,128]{3,2,1,0:T(8,128)(2,1)S(1)}, u32[]{:S(2)}) copy-start(bf16[2,8,8,128]{3,2,1,0:T(8,128)(2,1)S(1)} %get-tuple-element.54) | copy-start | bytes 98308
  49.8 44.1 %copy-start.86 = (bf16[2,8,8,128]{3,2,1,0:T(8,128)(2,1)}, bf16[2,8,8,128]{3,2,1,0:T(8,128)(2,1)S(1)}, u32[]{:S(2)}) copy-start(bf16[2,8,8,128]{3,2,1,0:T(8,128)(2,1)S(1)} %get-tuple-element.55) | copy-start | bytes 98308
  66.8 27.3 %all-to-all-start.2 = ((bf16[128,16,64]{0,2,1:T(8,128)(2,1)}), bf16[128,16,64]{0,2,1:T(8,128)(2,1)S(1)}, u32[]{:S(2)}, u32[]{:S(2)}) async-start(bf16[128,16,64]{0,2,1:T(8,128)(2,1)} %bitcast.10), calls=%async_computation.2 | async-start | bytes 524288 | tf_op jit(solution)/shard_map/all_to_all | solution.py:57
  72.6 28.0 %copy-start.146 = (bf16[2,8,8,128]{3,2,1,0:T(8,128)(2,1)}, bf16[2,8,8,128]{3,2,1,0:T(8,128)(2,1)S(1)}, u32[]{:S(2)}) copy-start(bf16[2,8,8,128]{3,2,1,0:T(8,128)(2,1)S(1)} %get-tuple-element.40) | copy-start | bytes 98308
  72.6 31.2 %copy-start.6 = (bf16[2,8,8,128]{3,2,1,0:T(8,128)(2,1)}, bf16[2,8,8,128]{3,2,1,0:T(8,128)(2,1)S(1)}, u32[]{:S(2)}) copy-start(bf16[2,8,8,128]{3,2,1,0:T(8,128)(2,1)S(1)} %get-tuple-element.42) | copy-start | bytes 98308
  72.6 37.9 %copy-start.88 = (bf16[2,8,8,128]{3,2,1,0:T(8,128)(2,1)}, bf16[2,8,8,128]{3,2,1,0:T(8,128)(2,1)S(1)}, u32[]{:S(2)}) copy-start(bf16[2,8,8,128]{3,2,1,0:T(8,128)(2,1)S(1)} %get-tuple-element.41) | copy-start | bytes 98308
  85.0 21.9 %copy-start.102 = (f32[256,256]{1,0:T(8,128)}, f32[256,256]{1,0:T(8,128)S(1)}, u32[]{:S(2)}) copy-start(f32[256,256]{1,0:T(8,128)S(1)} %convolution_multiply_fusion.63) | copy-start | bytes 786436
  94.7 23.4 %copy-start.4 = (bf16[2,8,8,128]{3,2,1,0:T(8,128)(2,1)}, bf16[2,8,8,128]{3,2,1,0:T(8,128)(2,1)S(1)}, u32[]{:S(2)}) copy-start(bf16[2,8,8,128]{3,2,1,0:T(8,128)(2,1)S(1)} %get-tuple-element.37) | copy-start | bytes 98308
  94.7 23.6 %copy-start.8 = (bf16[2,8,8,128]{3,2,1,0:T(8,128)(2,1)}, bf16[2,8,8,128]{3,2,1,0:T(8,128)(2,1)S(1)}, u32[]{:S(2)}) copy-start(bf16[2,8,8,128]{3,2,1,0:T(8,128)(2,1)S(1)} %get-tuple-element.36) | copy-start | bytes 98308
  94.7 23.8 %copy-start.12 = (bf16[2,8,8,128]{3,2,1,0:T(8,128)(2,1)}, bf16[2,8,8,128]{3,2,1,0:T(8,128)(2,1)S(1)}, u32[]{:S(2)}) copy-start(bf16[2,8,8,128]{3,2,1,0:T(8,128)(2,1)S(1)} %get-tuple-element.35) | copy-start | bytes 98308
  103.4 17.3 %copy-start.42 = (bf16[256,256]{1,0:T(8,128)(2,1)}, bf16[256,256]{1,0:T(8,128)(2,1)S(1)}, u32[]{:S(2)}) copy-start(bf16[256,256]{1,0:T(8,128)(2,1)S(1)} %get-tuple-element.72) | copy-start | bytes 393220
  152.4 80.1 %copy-start.1 = (bf16[128,1024]{1,0:T(8,128)(2,1)S(1)}, bf16[128,1024]{1,0:T(8,128)(2,1)}, u32[]{:S(2)}) copy-start(bf16[128,1024]{1,0:T(8,128)(2,1)} %param.10) | copy-start | bytes 786436
  235.3 25.3 %all-to-all-start.4 = ((bf16[128,16,64]{0,2,1:T(8,128)(2,1)}), bf16[128,16,64]{0,2,1:T(8,128)(2,1)S(1)}, u32[]{:S(2)}, u32[]{:S(2)}) async-start(bf16[128,16,64]{0,2,1:T(8,128)(2,1)} %bitcast.38), calls=%async_computation.4 | async-start | bytes 524288 | tf_op jit(solution)/shard_map/all_to_all | solution.py:109
  241.9 510.9 %all-reduce.3.cloned.1.call-start = ((), (), s32[]{:S(2)}) async-start(), calls=%async_computation.9 | async-start | bytes 8388608
  245.1 15.6 %copy-start.139 = (f32[256,256]{1,0:T(8,128)S(1)}, f32[256,256]{1,0:T(8,128)}, u32[]{:S(2)}) copy-start(f32[256,256]{1,0:T(8,128)} %convolution_multiply_fusion.39) | copy-start | bytes 786436
  245.1 16.6 %copy-start.9 = (bf16[2,8,8,128]{3,2,1,0:T(8,128)(2,1)S(1)}, bf16[2,8,8,128]{3,2,1,0:T(8,128)(2,1)}, u32[]{:S(2)}) copy-start(bf16[2,8,8,128]{3,2,1,0:T(8,128)(2,1)} %copy-done.8) | copy-start | bytes 98308
  245.1 16.6 %copy-start.136 = (f32[256,256]{1,0:T(8,128)S(1)}, f32[256,256]{1,0:T(8,128)}, u32[]{:S(2)}) copy-start(f32[256,256]{1,0:T(8,128)} %convolution_multiply_fusion.40) | copy-start | bytes 786436
  315.1 25.7 %all-to-all-start.7 = ((bf16[16,128,64]{1,2,0:T(8,128)(2,1)}), bf16[16,128,64]{1,2,0:T(8,128)(2,1)S(1)}, u32[]{:S(2)}, u32[]{:S(2)}) async-start(bf16[16,128,64]{1,2,0:T(8,128)(2,1)} %copy_bitcast_fusion), calls=%async_computation.7 | async-start | bytes 524288 | tf_op jit(solution)/shard_map/all_to_all | solution.py:165
  322.9 23.7 %copy-start.89 = (bf16[2,8,8,128]{3,2,1,0:T(8,128)(2,1)S(1)}, bf16[2,8,8,128]{3,2,1,0:T(8,128)(2,1)}, u32[]{:S(2)}) copy-start(bf16[2,8,8,128]{3,2,1,0:T(8,128)(2,1)} %copy-done.88) | copy-start | bytes 98308
  323.4 23.8 %copy-start.147 = (bf16[2,8,8,128]{3,2,1,0:T(8,128)(2,1)S(1)}, bf16[2,8,8,128]{3,2,1,0:T(8,128)(2,1)}, u32[]{:S(2)}) copy-start(bf16[2,8,8,128]{3,2,1,0:T(8,128)(2,1)} %copy-done.146) | copy-start | bytes 98308
  340.8 25.0 %all-to-all-start.6 = ((bf16[16,128,64]{1,2,0:T(8,128)(2,1)}), bf16[16,128,64]{1,2,0:T(8,128)(2,1)S(1)}, u32[]{:S(2)}, u32[]{:S(2)}) async-start(bf16[16,128,64]{1,2,0:T(8,128)(2,1)} %copy_bitcast_fusion.1), calls=%async_computation.6 | async-start | bytes 524288 | tf_op jit(solution)/shard_map/all_to_all | solution.py:164
  365.8 417.3 %all-to-all-start.5 = ((bf16[16,128,64]{1,2,0:T(8,128)(2,1)}), bf16[16,128,64]{1,2,0:T(8,128)(2,1)S(1)}, u32[]{:S(2)}, u32[]{:S(2)}) async-start(bf16[16,128,64]{1,2,0:T(8,128)(2,1)} %copy_bitcast_fusion.2), calls=%async_computation.5 | async-start | bytes 524288 | tf_op jit(solution)/shard_map/all_to_all | solution.py:163
  (140 other events, 551.8 us)
Sparse Core Ops, SparseCore 0:
  29.7 200.0 all-gather.3
  248.2 504.5 all-reduce.2
where the time goes:
time: 793 us; the launch traced here: 791 us
  waiting for transfers between devices  533 us (67%)
  matrix products  108 us (14%)
  blocking collectives  57 us (7%)
  starting transfers between devices  51.7 us (7%)
  local copies, waits for them, and re-layouts  20.2 us (3%)
  between operations  17 us (2%)
    unnamed x3, waiting for transfers between devices  381 us
    all_gather x1, waiting for transfers between devices, local(): lax.all_gather(proj_weight, ('dp', 'ctx'), axis=0, tiled=True)  77.3 us
    dot_general x36, matrix products, backward_tile(): jnp.einsum('qhd,khd->hqk', grad_tile, value_tile, preferred_element_type=...  35.3 us
    dot_general x36, matrix products, tile_scores(): jnp.einsum('qhd,khd->hqk', query_tile, key_tile, preferred_element_type=j...  35 us
    all_to_all x1, blocking collectives, local(): lax.all_to_all(attn_heads, 'ctx', split_axis=0, concat_axis=1, tiled=True)  30.1 us
    all_gather x1, blocking collectives, local(): proj_grad = lax.all_gather(summed, 'ctx', axis=0, tiled=True)  27 us
    all_to_all x1, waiting for transfers between devices, local(): lax.all_to_all(key_back, 'ctx', split_axis=0, concat_axis=1, tiled=True)  17.6 us
    all_to_all x1, waiting for transfers between devices, local(): lax.all_to_all(key_rows, 'ctx', split_axis=1, concat_axis=0, tiled=True)  17 us
  transfers between devices with their start and end apart: 9, of which 7 were waited for; matrix products, arithmetic and copies ran while one was open for 15% of the time, Pallas kernels for 0%

commit v1 on v0

v1 whole, which is shorter than its diff:
```python
import functools
import math

import jax
import jax.numpy as jnp
from jax import lax
from jax.experimental import pallas as pl
from jax.experimental.pallas import tpu as pltpu
from jax.sharding import PartitionSpec as P

DH = 64
LANES = 128
TILE = 256
BF16 = jnp.bfloat16
F32 = jnp.float32
VMEM = pl.BlockSpec(memory_space=pltpu.VMEM)
SMEM = pl.BlockSpec(memory_space=pltpu.SMEM)
LIMIT = 48 * 1024 * 1024


def call(kernel, out_shape, in_specs, scratch=(), flops=0, nbytes=0):
    single = not isinstance(out_shape, (list, tuple))
    out_specs = VMEM if single else [VMEM] * len(out_shape)
    return pl.pallas_call(
        kernel,
        out_shape=out_shape,
        in_specs=in_specs,
        out_specs=out_specs,
        scratch_shapes=list(scratch),
        compiler_params=pltpu.CompilerParams(vmem_limit_bytes=LIMIT),
        cost_estimate=pl.CostEstimate(flops=flops, bytes_accessed=nbytes, transcendentals=0),
    )


def pack_kernel(q_ref, k_ref, v_ref, w_ref, first_ref, second_ref):
    heads = first_ref.shape[0]
    for pair in range(heads // 2):
        cols = slice(pair * 2 * DH, (pair + 1) * 2 * DH)
        q_t = q_ref[:, cols].T
        k_t = k_ref[:, cols].T
        v_t = v_ref[:, cols].T
        for half in range(2):
            rows = slice(half * DH, (half + 1) * DH)
            first_ref[2 * pair + half, 0:DH, :] = q_t[rows]
            first_ref[2 * pair + half, DH : 2 * DH, :] = k_t[rows]
            second_ref[2 * pair + half] = v_t[rows]
    for head in range(heads):
        first_ref[head, 2 * DH :, :] = w_ref[...]


def unpack_kernel(count, x_ref, *out_refs):
    heads = x_ref.shape[0]
    for pair in range(heads // 2):
        for i in range(count):
            rows = slice(i * DH, (i + 1) * DH)
            both = jnp.concatenate([x_ref[2 * pair, rows, :], x_ref[2 * pair + 1, rows, :]], axis=0)
            out_refs[i][:, pair * 2 * DH : (pair + 1) * 2 * DH] = both.T


def user_edges(len_ref):
    ends = []
    total = 0
    for i in range(len_ref.shape[1]):
        total = total + len_ref[0, i]
        ends.append(total)
    return ends


def user_start(position, ends):
    start = jnp.zeros_like(position)
    for end in ends[:-1]:
        start = jnp.where(position >= end, end, start)
    return start


def user_inverse(position, ends, len_ref):
    length = jnp.full(position.shape, len_ref[0, 0], jnp.int32)
    for i, end in enumerate(ends[:-1]):
        length = jnp.where(position >= end, len_ref[0, i + 1], length)
    return 1.0 / length.astype(F32)


def lane_pair(ref, block, rows):
    return jnp.concatenate([ref[2 * block, rows, :], ref[2 * block + 1, rows, :]], axis=1)


def tile_allowed(row_block, col_block, starts, positions):
    key_pos = col_block * TILE + lax.broadcasted_iota(jnp.int32, (TILE, TILE), 0)
    return (key_pos >= starts) & (key_pos <= positions)


def block_rows(row_block, ends):
    positions = row_block * TILE + lax.broadcasted_iota(jnp.int32, (1, TILE), 1)
    return positions, user_start(positions, ends)


def first_block(row_block, ends):
    return lax.div(user_start(row_block * TILE, ends), TILE)


def natural(source_ref, rows, target_ref):
    for block in range(target_ref.shape[0]):
        for half in range(2):
            target_ref[block, half * LANES : (half + 1) * LANES, :] = source_ref[
                2 * block + half, rows, :
            ].T


Q_ROWS = slice(0, DH)
K_ROWS = slice(DH, 2 * DH)
V_ROWS = slice(0, DH)


def forward_kernel(len_ref, qk_ref, v_ref, out_ref, k_nat):
    blocks = k_nat.shape[0]
    ends = user_edges(len_ref)
    natural(qk_ref, K_ROWS, k_nat)
    for row_block in range(blocks):
        q_t = lane_pair(qk_ref, row_block, Q_ROWS)
        positions, starts = block_rows(row_block, ends)

        def step(col_block, total, q_t=q_t, positions=positions, starts=starts, row_block=row_block):
            raw = jnp.dot(k_nat[col_block], q_t, preferred_element_type=F32)
            half = raw * (0.5 / math.sqrt(DH))
            gate = 0.5 * jnp.tanh(half) + 0.5
            silu = (half + half) * gate
            allowed = tile_allowed(row_block, col_block, starts, positions)
            attn = jnp.where(allowed, silu, 0.0).astype(BF16)
            return total + jnp.dot(
                lane_pair(v_ref, col_block, V_ROWS), attn, preferred_element_type=F32
            )

        total = lax.fori_loop(
            first_block(row_block, ends), row_block + 1, step, jnp.zeros((DH, TILE), F32)
        )
        total = total * user_inverse(positions, ends, len_ref)
        out_ref[2 * row_block] = total[:, :LANES].astype(BF16)
        out_ref[2 * row_block + 1] = total[:, LANES:].astype(BF16)


def backward_kernel(len_ref, qk_ref, v_ref, g_ref, out_ref, k_nat, v_nat, k_acc, v_acc):
    blocks = k_nat.shape[0]
    scale = 1.0 / math.sqrt(DH)
    ends = user_edges(len_ref)
    natural(qk_ref, K_ROWS, k_nat)
    natural(v_ref, V_ROWS, v_nat)
    k_acc[...] = jnp.zeros_like(k_acc)
    v_acc[...] = jnp.zeros_like(v_acc)
    contract_lanes = (((1,), (1,)), ((), ()))
    for row_block in range(blocks):
        q_t = lane_pair(qk_ref, row_block, Q_ROWS)
        g_t = lane_pair(g_ref, row_block, slice(0, DH))
        positions, starts = block_rows(row_block, ends)

        def step(
            col_block, total, q_t=q_t, g_t=g_t, positions=positions, starts=starts, row_block=row_block
        ):
            raw = jnp.dot(k_nat[col_block], q_t, preferred_element_type=F32)
            attn_grad = jnp.dot(v_nat[col_block], g_t, preferred_element_type=F32)
            half = raw * (0.5 * scale)
            gate = 0.5 * jnp.tanh(half) + 0.5
            silu = (half + half) * gate
            slope = gate + silu * (1.0 - gate)
            allowed = tile_allowed(row_block, col_block, starts, positions)
            attn = jnp.where(allowed, silu, 0.0).astype(BF16)
            score_grad = jnp.where(allowed, attn_grad * slope, 0.0).astype(BF16)
            v_acc[col_block] += lax.dot_general(
                g_t, attn, contract_lanes, preferred_element_type=F32
            )
            k_acc[col_block] += lax.dot_general(
                q_t, score_grad, contract_lanes, preferred_element_type=F32
            )
            return total + jnp.dot(
                lane_pair(qk_ref, col_block, K_ROWS), score_grad, preferred_element_type=F32
            )

        total = lax.fori_loop(
            first_block(row_block, ends), row_block + 1, step, jnp.zeros((DH, TILE), F32)
        )
        total = (total * scale).astype(BF16)
        out_ref[2 * row_block, 0:DH, :] = total[:, :LANES]
        out_ref[2 * row_block + 1, 0:DH, :] = total[:, LANES:]
    for block in range(blocks):
        k_grad = (k_acc[block] * scale).astype(BF16)
        v_grad = v_acc[block].astype(BF16)
        for half in range(2):
            lanes = slice(half * LANES, (half + 1) * LANES)
            out_ref[2 * block + half, DH : 2 * DH, :] = k_grad[:, lanes]
            out_ref[2 * block + half, 2 * DH : 3 * DH, :] = v_grad[:, lanes]


def norm_kernel(
    len_ref, place_ref, o_ref, w_ref, out_grad_ref, gate_ref, grad_ref, gated_ref, gate_grad_ref, proj_acc
):
    width = w_ref.shape[0]
    tokens = out_grad_ref.shape[0]
    block = 256
    contract_lanes = (((1,), (1,)), ((), ()))
    out_grad = out_grad_ref[...]
    attn = o_ref[...].reshape(width, tokens).astype(F32)
    mean = jnp.sum(attn, axis=0, keepdims=True) * (1.0 / width)
    centred = attn - mean
    var = jnp.sum(centred * centred, axis=0, keepdims=True) * (1.0 / width)
    rstd = lax.rsqrt(var + 1e-05)
    sum_first = jnp.zeros((1, tokens), F32)
    sum_second = jnp.zeros((1, tokens), F32)
    for i in range(width // block):
        rows = slice(i * block, (i + 1) * block)
        gated_grad = lax.dot_general(
            w_ref[rows, :], out_grad, contract_lanes, preferred_element_type=F32
        )
        normed = (o_ref[i * block // DH : (i + 1) * block // DH].reshape(block, tokens).astype(F32) - mean) * rstd
        gates = gate_ref[:, rows].T.astype(F32)
        gated_ref[rows, :] = (normed * gates).astype(BF16)
        gate_grad_ref[:, rows] = (gated_grad * normed).astype(BF16).T
        normed_grad = gated_grad * gates
        sum_first = sum_first + jnp.sum(normed_grad, axis=0, keepdims=True)
        sum_second = sum_second + jnp.sum(normed_grad * normed, axis=0, keepdims=True)
        proj_acc[rows, :] = normed_grad
    sum_first = sum_first * (1.0 / width)
    sum_second = sum_second * (1.0 / width)
    position = place_ref[0] * tokens + lax.broadcasted_iota(jnp.int32, (1, tokens), 1)
    weight = rstd * user_inverse(position, user_edges(len_ref), len_ref)
    for i in range(width // block):
        rows = slice(i * block, (i + 1) * block)
        normed = (o_ref[i * block // DH : (i + 1) * block // DH].reshape(block, tokens).astype(F32) - mean) * rstd
        grad = (proj_acc[rows, :] - sum_first - normed * sum_second) * weight
        grad_ref[i * block // DH : (i + 1) * block // DH] = grad.astype(BF16).reshape(
            block // DH, DH, tokens
        )


def proj_kernel(mine_ref, other_ref, out_grad_ref, other_grad_ref, out_ref):
    chips, rows, width = out_ref.shape
    tokens = out_grad_ref.shape[0]
    step = 8
    for i in range(chips // step):
        part = slice(i * step, (i + 1) * step)
        mine = mine_ref[part].reshape(step * rows, tokens)
        other = other_ref[part].reshape(step * rows, tokens)
        left = jnp.concatenate([mine, other], axis=1)
        for j in range(width // 256):
            cols = slice(j * 256, (j + 1) * 256)
            right = jnp.concatenate([out_grad_ref[:, cols], other_grad_ref[:, cols]], axis=0)
            product = jnp.dot(left, right, preferred_element_type=F32)
            out_ref[part, :, cols] = product.astype(BF16).reshape(step, rows, 256)


def sum_kernel(x_ref, out_ref):
    out_ref[...] = jnp.sum(x_ref[...].astype(F32), axis=0).astype(BF16)


def exchange(array, axis, groups=None):
    return lax.all_to_all(
        array, axis, split_axis=0, concat_axis=0, tiled=True, axis_index_groups=groups
    )


def local(query_rows, key_rows, value_rows, gate_rows, out_grad, proj_weight, user_lengths):
    ctx = lax.axis_size("ctx")
    dp = lax.axis_size("dp")
    tokens, width = query_rows.shape
    heads = width // DH
    group = tokens * ctx
    blocks = group // TILE
    w_rows = proj_weight.size // LANES
    shape = jax.ShapeDtypeStruct
    partner = [(i, i ^ 1) for i in range(dp)]
    same_core = [[2 * i + core for i in range(dp // 2)] for core in range(2)]

    other_grad = lax.ppermute(out_grad, "dp", partner)
    first, second = call(
        pack_kernel,
        [
            shape((heads, 2 * DH + w_rows, tokens), BF16),
            shape((heads, DH, tokens), BF16),
        ],
        [VMEM] * 4,
        nbytes=6 * tokens * width * 2,
    )(query_rows, key_rows, value_rows, proj_weight.reshape(w_rows, LANES))
    first = exchange(first, "ctx")
    weight_part = first[:, 2 * DH :, :].reshape(ctx * proj_weight.shape[0], width)
    weights = lax.all_gather(weight_part, "dp", axis=0, tiled=True)
    second, first = lax.optimization_barrier((second, first))
    second = exchange(second, "ctx")

    attn_out = call(
        forward_kernel,
        shape((ctx, DH, tokens), BF16),
        [SMEM, VMEM, VMEM],
        [pltpu.VMEM((blocks, TILE, DH), BF16)],
        flops=group * group * DH * 2,
        nbytes=5 * group * DH * 2,
    )(user_lengths, first, second)
    attn_out = exchange(attn_out, "ctx")

    place = lax.axis_index("ctx").astype(jnp.int32).reshape(1)
    grad, gated, gate_grad = call(
        norm_kernel,
        [
            shape((heads, DH, tokens), BF16),
            shape((width, tokens), BF16),
            shape((tokens, width), BF16),
        ],
        [SMEM, SMEM, VMEM, VMEM, VMEM, VMEM],
        [pltpu.VMEM((width, tokens), F32)],
        flops=2 * tokens * width * width,
        nbytes=2 * width * width + 12 * tokens * width,
    )(user_lengths, place, attn_out, weights, out_grad, gate_rows)
    grad_heads = exchange(grad, "ctx")

    core = lax.rem(lax.axis_index("dp"), 2)
    gated = gated.reshape(dp // 2, 2, width // dp, tokens)
    mine = lax.dynamic_index_in_dim(gated, core, 1, keepdims=False)
    other = lax.dynamic_index_in_dim(gated, 1 - core, 1, keepdims=False)
    other = lax.ppermute(other, "dp", partner)
    partial = call(
        proj_kernel,
        shape((dp // 2, width // dp, width), BF16),
        [VMEM] * 4,
        flops=2 * tokens * width * width,
        nbytes=2 * width * width,
    )(mine, other, out_grad, other_grad)
    partial = exchange(partial, "dp", same_core)

    grads = call(
        backward_kernel,
        shape((ctx, 3 * DH, tokens), BF16),
        [SMEM, VMEM, VMEM, VMEM],
        [
            pltpu.VMEM((blocks, TILE, DH), BF16),
            pltpu.VMEM((blocks, TILE, DH), BF16),
            pltpu.VMEM((blocks, DH, TILE), F32),
            pltpu.VMEM((blocks, DH, TILE), F32),
        ],
        flops=3 * group * group * DH * 2,
        nbytes=7 * group * DH * 2,
    )(user_lengths, first, second, grad_heads)
    own = call(sum_kernel, shape((width // dp, width), BF16), [VMEM], nbytes=width * width)(partial)
    own = own.reshape(ctx, w_rows, LANES)
    grads = exchange(jnp.concatenate([grads, own], axis=1), "ctx")
    summed = jnp.sum(grads[:, 3 * DH :, :].astype(F32), axis=0).astype(BF16)
    proj = exchange(jnp.broadcast_to(summed[None], (ctx, w_rows, LANES)), "ctx")
    proj_grad = proj.reshape(width // dp, width).astype(F32)

    query_grad, key_grad, value_grad = call(
        functools.partial(unpack_kernel, 3),
        [shape((tokens, width), BF16)] * 3,
        [VMEM],
        nbytes=6 * tokens * width * 2,
    )(grads)
    return (query_grad, key_grad, value_grad, gate_grad, proj_grad)


def solution(mesh):
    rows = P(("dp", "ctx"), None)
    in_specs = (rows,) * 6 + (P("dp", None),)
    out_specs = (rows,) * 4 + (P("dp", None),)
    return jax.shard_map(local, mesh=mesh, in_specs=in_specs, out_specs=out_specs, check_vma=False)
```

time: 793 us -> 245 us (0.31)
  waiting for transfers between devices: 533 us -> 43.5 us
  matrix products: 108 us -> 0 us
  blocking collectives: 57 us -> 124 us
  Pallas kernels: 0 us -> 25 us
  starting transfers between devices: 51.7 us -> 30.4 us
  local copies, waits for them, and re-layouts: 20.2 us -> 7.2 us
    unnamed x3 -> x1, waiting for transfers between devices: 381 us -> 0.02 us
    dot_general x218 -> x0, matrix products: 108 us -> none  [the longest x36 35.3 us: backward_tile(): jnp.einsum('qhd,khd->hqk', grad_tile, value_tile, preferred_element_type=...]
    all_to_all x1 -> x3, blocking collectives: 30.1 us -> 124 us  [exchange(): lax.all_to_all(array, axis, split_axis=0, concat_axis=0, tiled=True, axis...]
    all_gather x1, waiting for transfers between devices: 77.3 us -> 0.01 us  [local(): weights = lax.all_gather(weight_part, 'dp', axis=0, tiled=True)]
    all_to_all x7 -> x4, waiting for transfers between devices: 74.1 us -> 42.5 us  [exchange(): lax.all_to_all(array, axis, split_axis=0, concat_axis=0, tiled=True, axis...]
    all_gather x1 -> x0, blocking collectives: 27 us -> none  [local(): proj_grad = lax.all_gather(summed, 'ctx', axis=0, tiled=True)]
    all_to_all x7 -> x4, starting transfers between devices: 51.4 us -> 26.1 us  [exchange(): lax.all_to_all(array, axis, split_axis=0, concat_axis=0, tiled=True, axis...]
    pallas_call x0 -> x7, Pallas kernels: none -> 25 us  [the longest x1 10.5 us: local(): call(backward_kernel, shape((ctx, 3 * DH, tokens), BF16), [SMEM, VMEM, VM...]
  transfers between devices with their start and end apart: 9 -> 7, of which waited for: 7 -> 5; matrix products, arithmetic and copies ran while one was open for 15% -> 0% of each run, Pallas kernels for 0% -> 9%
where the time goes in v1:
time: 245 us; the launch traced here: 244 us
  blocking collectives  124 us (51%)
  waiting for transfers between devices  43.5 us (18%)
  starting transfers between devices  30.4 us (12%)
  Pallas kernels  25 us (10%)
  between operations  14.2 us (6%)
  local copies, waits for them, and re-layouts  7.2 us (3%)
    all_to_all x3, blocking collectives, exchange(): lax.all_to_all(array, axis, split_axis=0, concat_axis=0, tiled=True, axis...  124 us
    all_to_all x4, waiting for transfers between devices, exchange(): lax.all_to_all(array, axis, split_axis=0, concat_axis=0, tiled=True, axis...  42.5 us
    all_to_all x4, starting transfers between devices, exchange(): lax.all_to_all(array, axis, split_axis=0, concat_axis=0, tiled=True, axis...  26.1 us
    pallas_call x1, Pallas kernels, local(): call(backward_kernel, shape((ctx, 3 * DH, tokens), BF16), [SMEM, VMEM, VM...  10.5 us
    pallas_call x1, Pallas kernels, local(): call(forward_kernel, shape((ctx, DH, tokens), BF16), [SMEM, VMEM, VMEM],...  9.29 us
  transfers between devices with their start and end apart: 7, of which 5 were waited for; matrix products, arithmetic and copies ran while one was open for 0% of the time, Pallas kernels for 9%

profile of v1, /device:TPU:6, one launch (start us, length us, event | category | flops | bytes accessed | tf_op | source)
XLA Modules:
  0.0 243.9 jit_solution(3217193532588768126)
XLA Ops:
  7.2 0.0 all-gather.2.cloned.1.call-start
  7.2 0.7 reshape.29.w_ref
  7.9 0.9 copy-done.2
  8.9 0.9 copy-done.3
  9.8 0.9 copy-done.4
  10.8 0.3 shard_map.110
  11.0 49.9 %all_to_all.35.qk_ref = bf16[16,144,128]{2,1,0:T(8,128)(2,1)S(1)} all-to-all(bf16[16,144,128]{2,1,0:T(8,128)(2,1)S(1)} %get-tuple-element.16), channel_id=1, replica_groups=mesh['dp'=32,'ctx'=16] {'ctx'}, dimensions={0} | all-to-all | bytes 1179648 | tf_op jit(solution)/shard_map/all_to_all | solution.py:254
  61.0 0.7 reshape.31
  61.6 0.0 all-gather.2.cloned.1.call-update
  61.7 21.4 %all_to_all.36.v_ref = bf16[16,64,128]{2,1,0:T(8,128)(2,1)S(1)} all-to-all(bf16[16,64,128]{2,1,0:T(8,128)(2,1)S(1)} %get-tuple-element.18), channel_id=1, replica_groups=mesh['dp'=32,'ctx'=16] {'ctx'}, dimensions={0} | all-to-all | bytes 524288 | tf_op jit(solution)/shard_map/all_to_all | solution.py:254
  83.1 9.3 %shard_map.111 = bf16[16,64,128]{2,1,0:T(8,128)(2,1)} custom-call(s32[1,4]{1,0:T(1,128)S(1)} %copy-done.6, bf16[16,144,128]{2,1,0:T(8,128)(2,1)S(1)} %all_to_all.35.qk_ref, bf16[16,64,128]{2,1,0:T(8,128)(2,1)S(1)} %all_to_all.36.v_ref), custom_call_target="tpu_custom_call" | custom-call | flops 536870912 | bytes 1310720 | tf_op jit(solution)/shard_map/pallas_call | solution.py:287
  92.4 5.6 %all-to-all-start.2 = ((bf16[16,64,128]{2,1,0:T(8,128)(2,1)}), bf16[16,64,128]{2,1,0:T(8,128)(2,1)S(1)}, u32[]{:S(2)}, u32[]{:S(2)}) async-start(bf16[16,64,128]{2,1,0:T(8,128)(2,1)} %shard_map.111), calls=%async_computation.2 | async-start | bytes 524288 | tf_op jit(solution)/shard_map/all_to_all | solution.py:254
  98.0 18.4 %all-to-all-done.2.o_ref = bf16[16,64,128]{2,1,0:T(8,128)(2,1)S(1)} async-done(((bf16[16,64,128]{2,1,0:T(8,128)(2,1)}), bf16[16,64,128]{2,1,0:T(8,128)(2,1)S(1)}, u32[]{:S(2)}, u32[]{:S(2)}) %all-to-all-start.2) | async-done | bytes 262176 | tf_op jit(solution)/shard_map/all_to_all | solution.py:254
  116.4 1.6 copy-done
  118.0 2.3 shard_map.112
  120.3 9.0 %all-to-all-start.3 = ((bf16[16,64,128]{2,1,0:T(8,128)(2,1)}), bf16[16,64,128]{2,1,0:T(8,128)(2,1)S(1)}, u32[]{:S(2)}, u32[]{:S(2)}) async-start(bf16[16,64,128]{2,1,0:T(8,128)(2,1)} %get-tuple-element.19), calls=%async_computation.3 | async-start | bytes 524288 | tf_op jit(solution)/shard_map/all_to_all | solution.py:254
  129.3 1.9 collective-permute-start.1
  131.3 2.4 collective-permute-start
  133.7 1.0 collective-permute-done.other_ref
  134.7 1.4 shard_map.114
  136.1 11.9 %all-to-all-done.3.g_ref = bf16[16,64,128]{2,1,0:T(8,128)(2,1)S(1)} async-done(((bf16[16,64,128]{2,1,0:T(8,128)(2,1)}), bf16[16,64,128]{2,1,0:T(8,128)(2,1)S(1)}, u32[]{:S(2)}, u32[]{:S(2)}) %all-to-all-start.3) | async-done | bytes 262176 | tf_op jit(solution)/shard_map/all_to_all | solution.py:254
  147.9 5.7 %all-to-all-start.4 = ((bf16[16,32,1024]{2,1,0:T(8,128)(2,1)}), bf16[16,32,1024]{2,1,0:T(8,128)(2,1)S(1)}, u32[]{:S(2)}, u32[]{:S(2)}) async-start(bf16[16,32,1024]{2,1,0:T(8,128)(2,1)} %shard_map.114), calls=%async_computation.4 | async-start | bytes 2097152 | tf_op jit(solution)/shard_map/all_to_all | solution.py:254
  153.7 10.5 %shard_map.113 = bf16[16,192,128]{2,1,0:T(8,128)(2,1)S(1)} custom-call(s32[1,4]{1,0:T(1,128)S(1)} %copy-done.6, bf16[16,144,128]{2,1,0:T(8,128)(2,1)S(1)} %all_to_all.35.qk_ref, bf16[16,64,128]{2,1,0:T(8,128)(2,1)S(1)} %all_to_all.36.v_ref, bf16[16,64,128]{2,1,0:T(8,128)(2,1)S(1)} %all-to-all-done.3.g_ref), custom_call_target="tpu_custom_call" | custom-call | flops 1610612736 | bytes 1835008 | tf_op jit(solution)/shard_map/pallas_call | solution.py:326
  164.2 0.5 all-to-all-done.4.x_ref
  164.7 0.1 shard_map.115
  164.9 0.1 pad_maximum_fusion
  164.9 52.1 %all_to_all.37.x_ref = bf16[16,208,128]{2,1,0:T(8,128)(2,1)S(1)} all-to-all(bf16[16,208,128]{2,1,0:T(8,128)(2,1)S(1)} %pad_maximum_fusion), channel_id=1, replica_groups=mesh['dp'=32,'ctx'=16] {'ctx'}, dimensions={0} | all-to-all | bytes 1703936 | tf_op jit(solution)/shard_map/all_to_all | solution.py:254
  217.1 0.6 broadcast_in_dim.2
  217.7 5.7 %all-to-all-start.6 = ((bf16[16,16,128]{2,1,0:T(8,128)(2,1)}), bf16[16,16,128]{2,1,0:T(8,128)(2,1)S(1)}, u32[]{:S(2)}, u32[]{:S(2)}) async-start(bf16[16,16,128]{2,1,0:T(8,128)(2,1)} %broadcast_in_dim.2), calls=%async_computation.6 | async-start | bytes 131072 | tf_op jit(solution)/shard_map/all_to_all | solution.py:254
  223.5 1.1 shard_map.116
  224.6 11.7 %all-to-all-done.6 = bf16[16,16,128]{2,1,0:T(8,128)(2,1)S(1)} async-done(((bf16[16,16,128]{2,1,0:T(8,128)(2,1)}), bf16[16,16,128]{2,1,0:T(8,128)(2,1)S(1)}, u32[]{:S(2)}, u32[]{:S(2)}) %all-to-all-start.6) | async-done | bytes 65568 | tf_op jit(solution)/shard_map/all_to_all | solution.py:254
  236.4 0.7 reshape.34
  (16 shorter events, 0.1 us)
Async XLA Ops:
  7.2 75.9 %copy-start.6 = (s32[1,4]{1,0:T(1,128)S(1)}, s32[1,4]{1,0:T(1,128)}, u32[]{:S(2)}) copy-start(s32[1,4]{1,0:T(1,128)} %len_ref.5) | copy-start | bytes 52
  7.2 109.3 %all-gather.2.cloned.1.call-start = ((), (), s32[]{:S(2)}) async-start(), calls=%async_computation.7 | async-start | bytes 2162688 | tf_op jit(solution)/shard_map/all_gather | solution.py:283
  7.9 0.9 copy-start.2
  8.9 0.9 copy-start.3
  9.8 0.9 copy-start.4
  61.0 55.5 %copy-start.1 = (bf16[128,1024]{1,0:T(8,128)(2,1)S(1)}, bf16[128,1024]{1,0:T(8,128)(2,1)}, u32[]{:S(2)}) copy-start(bf16[128,1024]{1,0:T(8,128)(2,1)} %out_grad_ref.3) | copy-start | bytes 786436
  61.0 55.5 %copy-start.5 = (bf16[128,1024]{1,0:T(8,128)(2,1)S(1)}, bf16[128,1024]{1,0:T(8,128)(2,1)}, u32[]{:S(2)}) copy-start(bf16[128,1024]{1,0:T(8,128)(2,1)} %gate_ref.1) | copy-start | bytes 786436
  92.4 24.0 %all-to-all-start.2 = ((bf16[16,64,128]{2,1,0:T(8,128)(2,1)}), bf16[16,64,128]{2,1,0:T(8,128)(2,1)S(1)}, u32[]{:S(2)}, u32[]{:S(2)}) async-start(bf16[16,64,128]{2,1,0:T(8,128)(2,1)} %shard_map.111), calls=%async_computation.2 | async-start | bytes 524288 | tf_op jit(solution)/shard_map/all_to_all | solution.py:254
  116.4 1.6 copy-start
  120.3 27.6 %all-to-all-start.3 = ((bf16[16,64,128]{2,1,0:T(8,128)(2,1)}), bf16[16,64,128]{2,1,0:T(8,128)(2,1)S(1)}, u32[]{:S(2)}, u32[]{:S(2)}) async-start(bf16[16,64,128]{2,1,0:T(8,128)(2,1)} %get-tuple-element.19), calls=%async_computation.3 | async-start | bytes 524288 | tf_op jit(solution)/shard_map/all_to_all | solution.py:254
  129.3 4.4 %collective-permute-start.1 = (bf16[128,1024]{1,0:T(8,128)(2,1)S(1)}, bf16[128,1024]{1,0:T(8,128)(2,1)S(1)}, u32[]{:S(2)}, u32[]{:S(2)}) collective-permute-start(bf16[128,1024]{1,0:T(8,128)(2,1)S(1)} %copy-done.1), channel_id=1, source_target_pairs={{0,16},{16,0},{32,48},{48,32},{64,80},{80,64},{96,112},{112,96},{1... | collective-permute-start | bytes 786440 | tf_op jit(solution)/shard_map/ppermute | solution.py:271
  131.3 3.4 %collective-permute-start = (bf16[16,32,128]{2,1,0:T(8,128)(2,1)S(1)}, bf16[16,32,128]{2,1,0:T(8,128)(2,1)S(1)}, u32[]{:S(2)}, u32[]{:S(2)}) collective-permute-start(bf16[16,32,128]{2,1,0:T(8,128)(2,1)S(1)} %get-tuple-element.25), channel_id=1, source_target_pairs={{0,16},{16,0},{32,48},{48,32},{64,80},{80,64},{96,112},{112,96},{1... | collective-permute-start | bytes 393224 | tf_op jit(solution)/shard_map/ppermute | solution.py:316
  147.9 16.8 %all-to-all-start.4 = ((bf16[16,32,1024]{2,1,0:T(8,128)(2,1)}), bf16[16,32,1024]{2,1,0:T(8,128)(2,1)S(1)}, u32[]{:S(2)}, u32[]{:S(2)}) async-start(bf16[16,32,1024]{2,1,0:T(8,128)(2,1)} %shard_map.114), calls=%async_computation.4 | async-start | bytes 2097152 | tf_op jit(solution)/shard_map/all_to_all | solution.py:254
  217.7 18.6 %all-to-all-start.6 = ((bf16[16,16,128]{2,1,0:T(8,128)(2,1)}), bf16[16,16,128]{2,1,0:T(8,128)(2,1)S(1)}, u32[]{:S(2)}, u32[]{:S(2)}) async-start(bf16[16,16,128]{2,1,0:T(8,128)(2,1)} %broadcast_in_dim.2), calls=%async_computation.6 | async-start | bytes 131072 | tf_op jit(solution)/shard_map/all_to_all | solution.py:254
Sparse Core Ops, SparseCore 0:
  61.8 51.2 all-gather.1

commit v2 on v1

v2 whole, which is shorter than its diff:
```python
import functools
import math

import jax
import jax.numpy as jnp
from jax import lax
from jax.experimental import pallas as pl
from jax.experimental.pallas import tpu as pltpu
from jax.sharding import PartitionSpec as P

DH = 64
LANES = 128
TILE = 256
BF16 = jnp.bfloat16
F32 = jnp.float32
VMEM = pl.BlockSpec(memory_space=pltpu.VMEM)
SMEM = pl.BlockSpec(memory_space=pltpu.SMEM)
LIMIT = 48 * 1024 * 1024


def call(kernel, out_shape, in_specs, scratch=(), flops=0, nbytes=0):
    single = not isinstance(out_shape, (list, tuple))
    out_specs = VMEM if single else [VMEM] * len(out_shape)
    return pl.pallas_call(
        kernel,
        out_shape=out_shape,
        in_specs=in_specs,
        out_specs=out_specs,
        scratch_shapes=list(scratch),
        compiler_params=pltpu.CompilerParams(vmem_limit_bytes=LIMIT),
        cost_estimate=pl.CostEstimate(flops=flops, bytes_accessed=nbytes, transcendentals=0),
    )


def pack_kernel(q_hbm, k_hbm, v_hbm, out_ref, rows_ref, sems):
    heads = out_ref.shape[0]
    copies = [
        pltpu.make_async_copy(source, rows_ref.at[i], sems.at[i])
        for i, source in enumerate((q_hbm, k_hbm, v_hbm))
    ]
    for copy in copies:
        copy.start()
    for i, copy in enumerate(copies):
        copy.wait()
        for pair in range(heads // 2):
            both = rows_ref[i, :, pair * 2 * DH : (pair + 1) * 2 * DH].T
            out_ref[2 * pair, i * DH : (i + 1) * DH, :] = both[:DH]
            out_ref[2 * pair + 1, i * DH : (i + 1) * DH, :] = both[DH:]


def unpack_kernel(count, x_ref, *out_refs):
    heads = x_ref.shape[0]
    for pair in range(heads // 2):
        for i in range(count):
            rows = slice(i * DH, (i + 1) * DH)
            both = jnp.concatenate([x_ref[2 * pair, rows, :], x_ref[2 * pair + 1, rows, :]], axis=0)
            out_refs[i][:, pair * 2 * DH : (pair + 1) * 2 * DH] = both.T


def user_edges(len_ref):
    ends = []
    total = 0
    for i in range(len_ref.shape[1]):
        total = total + len_ref[0, i]
        ends.append(total)
    return ends


def user_start(position, ends):
    start = jnp.zeros_like(position)
    for end in ends[:-1]:
        start = jnp.where(position >= end, end, start)
    return start


def user_inverse(position, ends, len_ref):
    length = jnp.full(position.shape, len_ref[0, 0], jnp.int32)
    for i, end in enumerate(ends[:-1]):
        length = jnp.where(position >= end, len_ref[0, i + 1], length)
    return 1.0 / length.astype(F32)


def lane_pair(ref, block, rows):
    return jnp.concatenate([ref[2 * block, rows, :], ref[2 * block + 1, rows, :]], axis=1)


def tile_allowed(diagonal, col_block, starts, positions):
    key_pos = lax.broadcasted_iota(jnp.int32, (TILE, TILE), 0)
    shift = col_block * TILE
    allowed = key_pos >= starts - shift
    return allowed & (key_pos <= positions - shift) if diagonal else allowed


def block_rows(row_block, ends):
    positions = row_block * TILE + lax.broadcasted_iota(jnp.int32, (1, TILE), 1)
    return positions, user_start(positions, ends)


def first_block(row_block, ends):
    return lax.div(user_start(row_block * TILE, ends), TILE)


def natural(source_ref, rows, target_ref):
    for block in range(target_ref.shape[0]):
        for half in range(2):
            target_ref[block, half * LANES : (half + 1) * LANES, :] = source_ref[
                2 * block + half, rows, :
            ].T


Q_ROWS = slice(0, DH)
K_ROWS = slice(DH, 2 * DH)
V_ROWS = slice(2 * DH, 3 * DH)
CONTRACT_LANES = (((1,), (1,)), ((), ()))


def gate_and_silu(raw):
    half = raw * (0.5 / math.sqrt(DH))
    gate = 0.5 * jnp.tanh(half) + 0.5
    return gate, (half + half) * gate


def forward_kernel(len_ref, qkv_ref, out_ref, k_nat, attn_ref):
    ends = user_edges(len_ref)
    natural(qkv_ref, K_ROWS, k_nat)
    for row_block in range(k_nat.shape[0]):
        q_t = lane_pair(qkv_ref, row_block, Q_ROWS)
        positions, starts = block_rows(row_block, ends)
        first = first_block(row_block, ends)

        def score(col, diagonal, q_t=q_t, positions=positions, starts=starts):
            raw = jnp.dot(k_nat[col], q_t, preferred_element_type=F32)
            _, silu = gate_and_silu(raw)
            allowed = tile_allowed(diagonal, col, starts, positions)
            return jnp.where(allowed, silu, 0.0).astype(BF16)

        def product(col, attn):
            return jnp.dot(lane_pair(qkv_ref, col, V_ROWS), attn, preferred_element_type=F32)

        def step(i, total, row_block=row_block, score=score):
            col = row_block - 1 - i
            before = attn_ref[...]
            attn = score(col, False)
            total = total + product(col + 1, before)
            attn_ref[...] = attn
            return total

        attn_ref[...] = score(row_block, True)
        total = lax.fori_loop(0, row_block - first, step, jnp.zeros((DH, TILE), F32))
        total = total + product(first, attn_ref[...])
        total = total * user_inverse(positions, ends, len_ref)
        out_ref[2 * row_block] = total[:, :LANES].astype(BF16)
        out_ref[2 * row_block + 1] = total[:, LANES:].astype(BF16)


def backward_kernel(len_ref, qkv_ref, g_ref, out_ref, k_nat, v_nat, k_acc, v_acc, attn_ref, slope_ref):
    blocks = k_nat.shape[0]
    scale = 1.0 / math.sqrt(DH)
    ends = user_edges(len_ref)
    natural(qkv_ref, K_ROWS, k_nat)
    natural(qkv_ref, V_ROWS, v_nat)
    k_acc[...] = jnp.zeros_like(k_acc)
    v_acc[...] = jnp.zeros_like(v_acc)
    for row_block in range(blocks):
        q_t = lane_pair(qkv_ref, row_block, Q_ROWS)
        g_t = lane_pair(g_ref, row_block, slice(0, DH))
        positions, starts = block_rows(row_block, ends)
        first = first_block(row_block, ends)

        def score(col, diagonal, q_t=q_t, g_t=g_t, positions=positions, starts=starts):
            raw = jnp.dot(k_nat[col], q_t, preferred_element_type=F32)
            attn_grad = jnp.dot(v_nat[col], g_t, preferred_element_type=F32)
            gate, silu = gate_and_silu(raw)
            score_grad = attn_grad * (gate + silu * (1.0 - gate))
            allowed = tile_allowed(diagonal, col, starts, positions)
            return (
                jnp.where(allowed, silu, 0.0).astype(BF16),
                jnp.where(allowed, score_grad, 0.0).astype(BF16),
            )

        def product(col, attn, score_grad, q_t=q_t, g_t=g_t):
            v_acc[col] += lax.dot_general(g_t, attn, CONTRACT_LANES, preferred_element_type=F32)
            k_acc[col] += lax.dot_general(
                q_t, score_grad, CONTRACT_LANES, preferred_element_type=F32
            )
            return jnp.dot(lane_pair(qkv_ref, col, K_ROWS), score_grad, preferred_element_type=F32)

        def step(i, total, row_block=row_block, score=score, product=product):
            col = row_block - 1 - i
            before = attn_ref[...], slope_ref[...]
            attn, score_grad = score(col, False)
            total = total + product(col + 1, *before)
            attn_ref[...] = attn
            slope_ref[...] = score_grad
            return total

        attn, score_grad = score(row_block, True)
        attn_ref[...] = attn
        slope_ref[...] = score_grad
        total = lax.fori_loop(0, row_block - first, step, jnp.zeros((DH, TILE), F32))
        total = total + product(first, attn_ref[...], slope_ref[...])
        total = (total * scale).astype(BF16)
        out_ref[2 * row_block, 0:DH, :] = total[:, :LANES]
        out_ref[2 * row_block + 1, 0:DH, :] = total[:, LANES:]
    for block in range(blocks):
        k_grad = (k_acc[block] * scale).astype(BF16)
        v_grad = v_acc[block].astype(BF16)
        for half in range(2):
            lanes = slice(half * LANES, (half + 1) * LANES)
            out_ref[2 * block + half, DH : 2 * DH, :] = k_grad[:, lanes]
            out_ref[2 * block + half, 2 * DH : 3 * DH, :] = v_grad[:, lanes]


def project_kernel(
    place_ref, w0_ref, w1_ref, w2_low_ref, w2_high_ref, w3_ref, out_grad_ref, other_grad_ref, mine_ref, theirs_ref
):
    side, rows, width = w0_ref.shape
    tokens = out_grad_ref.shape[0]
    both = jnp.concatenate([out_grad_ref[...], other_grad_ref[...]], axis=0)
    pieces = [(w0_ref, 0, 0), (w1_ref, 1, 0), (w2_low_ref, 2, 0), (w2_high_ref, 2, side // 2), (w3_ref, 3, 0)]
    for ref, y_back, x_first in pieces:
        count = ref.shape[0]
        product = lax.dot_general(
            ref[...].reshape(count * rows, width), both, CONTRACT_LANES, preferred_element_type=F32
        )
        y = lax.rem(place_ref[3] + side - y_back, side)
        for i in range(count):
            x = lax.rem(place_ref[2] + side - x_first - i, side)
            mine_ref[x * side + y] = product[i * rows : (i + 1) * rows, :tokens]
            theirs_ref[x * side + y] = product[i * rows : (i + 1) * rows, tokens:]


def norm_kernel(
    len_ref,
    place_ref,
    o_ref,
    mine_ref,
    recv_ref,
    gate_ref,
    grad_ref,
    gated_mine_ref,
    gated_other_ref,
    gate_grad_ref,
    normed_grad_ref,
):
    heads, _, tokens = o_ref.shape
    width = heads * DH
    half = DH // 2
    even = place_ref[1] == 0
    total = jnp.zeros((DH, tokens), F32)
    for head in range(heads):
        total = total + o_ref[head].astype(F32)
    mean = jnp.sum(total, axis=0, keepdims=True) * (1.0 / width)
    total = jnp.zeros((DH, tokens), F32)
    for head in range(heads):
        centred = o_ref[head].astype(F32) - mean
        total = total + centred * centred
    var = jnp.sum(total, axis=0, keepdims=True) * (1.0 / width)
    rstd = lax.rsqrt(var + 1e-05)
    first = jnp.zeros((DH, tokens), F32)
    second = jnp.zeros((DH, tokens), F32)
    for pair in range(heads // 2):
        cols = slice(pair * 2 * DH, (pair + 1) * 2 * DH)
        gates = gate_ref[:, cols].T.astype(F32)
        gate_grads = []
        for i in range(2):
            head = 2 * pair + i
            normed = (o_ref[head].astype(F32) - mean) * rstd
            mine, recv = mine_ref[head], recv_ref[head]
            gated_grad = jnp.concatenate(
                [jnp.where(even, mine, recv), jnp.where(even, recv, mine)], axis=0
            )
            gate = gates[i * DH : (i + 1) * DH]
            gated = normed * gate
            low, high = gated[:half], gated[half:]
            gated_mine_ref[head] = jnp.where(even, low, high).astype(BF16)
            gated_other_ref[head] = jnp.where(even, high, low).astype(BF16)
            gate_grads.append((gated_grad * normed).astype(BF16))
            normed_grad = gated_grad * gate
            first = first + normed_grad
            second = second + normed_grad * normed
            normed_grad_ref[head] = normed_grad
        gate_grad_ref[:, cols] = jnp.concatenate(gate_grads, axis=0).T
    first = jnp.sum(first, axis=0, keepdims=True) * (1.0 / width)
    second = jnp.sum(second, axis=0, keepdims=True) * (1.0 / width)
    position = place_ref[0] * tokens + lax.broadcasted_iota(jnp.int32, (1, tokens), 1)
    weight = rstd * user_inverse(position, user_edges(len_ref), len_ref)
    for head in range(heads):
        normed = (o_ref[head].astype(F32) - mean) * rstd
        grad_ref[head] = ((normed_grad_ref[head] - first - normed * second) * weight).astype(BF16)


def proj_kernel(mine_ref, other_ref, out_grad_ref, other_grad_ref, out_ref):
    chips, rows, width = out_ref.shape
    tokens = out_grad_ref.shape[0]
    step = 8
    for i in range(chips // step):
        part = slice(i * step, (i + 1) * step)
        mine = mine_ref[part].reshape(step * rows, tokens)
        other = other_ref[part].reshape(step * rows, tokens)
        left = jnp.concatenate([mine, other], axis=1)
        for j in range(width // 256):
            cols = slice(j * 256, (j + 1) * 256)
            right = jnp.concatenate([out_grad_ref[:, cols], other_grad_ref[:, cols]], axis=0)
            product = jnp.dot(left, right, preferred_element_type=F32)
            out_ref[part, :, cols] = product.astype(BF16).reshape(step, rows, 256)


def sum_kernel(x_ref, out_ref):
    out_ref[...] = jnp.sum(x_ref[...].astype(F32), axis=0).astype(BF16)


def exchange(array, axis, groups=None):
    return lax.all_to_all(
        array, axis, split_axis=0, concat_axis=0, tiled=True, axis_index_groups=groups
    )


SIDE = 4


def plane_shift(axis, step):
    moves = []
    for i in range(2 * SIDE * SIDE):
        x, y, core = i // (2 * SIDE), i // 2 % SIDE, i % 2
        if axis == "x":
            x = (x + step) % SIDE
        else:
            y = (y + step) % SIDE
        moves.append((i, (x * SIDE + y) * 2 + core))
    return moves


def ring_blocks(block, axis):
    up, down = plane_shift(axis, 1), plane_shift(axis, -1)
    back_one = lax.ppermute(block, "dp", up)
    back_three = lax.ppermute(block, "dp", down)
    half = block.shape[0] // 2
    low = lax.ppermute(back_one[:half], "dp", up)
    high = lax.ppermute(back_three[half:], "dp", down)
    return block, back_one, low, high, back_three


def local(query_rows, key_rows, value_rows, gate_rows, out_grad, proj_weight, user_lengths):
    ctx = lax.axis_size("ctx")
    dp = lax.axis_size("dp")
    tokens, width = query_rows.shape
    heads = width // DH
    group = tokens * ctx
    blocks = group // TILE
    chips = dp // 2
    out_rows = width // dp
    w_rows = proj_weight.size // LANES
    shape = jax.ShapeDtypeStruct
    partner = [(i, i ^ 1) for i in range(dp)]
    same_core = [[2 * i + core for i in range(chips)] for core in range(2)]
    chip = lax.axis_index("dp") // 2
    place = jnp.stack(
        [lax.axis_index("ctx"), lax.rem(lax.axis_index("dp"), 2), chip // SIDE, lax.rem(chip, SIDE)]
    ).astype(jnp.int32)
    in_hbm = pl.BlockSpec(memory_space=pltpu.HBM)

    block = proj_weight.reshape(1, w_rows, LANES)
    block = exchange(jnp.broadcast_to(block, (ctx, w_rows, LANES)), "ctx")
    qkv = call(
        pack_kernel,
        shape((heads, 3 * DH, tokens), BF16),
        [in_hbm] * 3,
        [pltpu.VMEM((3, tokens, width), BF16), pltpu.SemaphoreType.DMA((3,))],
        nbytes=6 * tokens * width * 2,
    )(query_rows, key_rows, value_rows)
    block, qkv = lax.optimization_barrier((block, qkv))
    qkv = exchange(qkv, "ctx")

    block = block.reshape(out_rows, width)
    column = jnp.concatenate(ring_blocks(block, "x"), axis=0).reshape(SIDE, out_rows, width)
    weights = ring_blocks(column, "y")
    qkv, weights = lax.optimization_barrier((qkv, weights))
    other_grad = lax.ppermute(out_grad, "dp", partner)
    mine, theirs = call(
        project_kernel,
        [shape((heads, DH // 2, tokens), F32)] * 2,
        [SMEM] + [VMEM] * 7,
        flops=2 * tokens * width * width,
        nbytes=2 * width * width,
    )(place, *weights, out_grad, other_grad)
    received = lax.ppermute(theirs, "dp", partner)

    attn_out = call(
        forward_kernel,
        shape((ctx, DH, tokens), BF16),
        [SMEM, VMEM],
        [pltpu.VMEM((blocks, TILE, DH), BF16), pltpu.VMEM((TILE, TILE), BF16)],
        flops=group * group * DH * 2,
        nbytes=5 * group * DH * 2,
    )(user_lengths, qkv)
    attn_out = exchange(attn_out, "ctx")

    grad, gated_mine, gated_other, gate_grad = call(
        norm_kernel,
        [
            shape((heads, DH, tokens), BF16),
            shape((heads, DH // 2, tokens), BF16),
            shape((heads, DH // 2, tokens), BF16),
            shape((tokens, width), BF16),
        ],
        [SMEM, SMEM, VMEM, VMEM, VMEM, VMEM],
        [pltpu.VMEM((heads, DH, tokens), F32)],
        nbytes=18 * tokens * width,
    )(user_lengths, place, attn_out, mine, received, gate_rows)
    grad = exchange(grad, "ctx")

    other = lax.ppermute(gated_other, "dp", partner)
    partial = call(
        proj_kernel,
        shape((chips, out_rows, width), BF16),
        [VMEM] * 4,
        flops=2 * tokens * width * width,
        nbytes=2 * width * width,
    )(gated_mine, other, out_grad, other_grad)
    partial = exchange(partial, "dp", same_core)

    grads = call(
        backward_kernel,
        shape((ctx, 3 * DH, tokens), BF16),
        [SMEM, VMEM, VMEM],
        [
            pltpu.VMEM((blocks, TILE, DH), BF16),
            pltpu.VMEM((blocks, TILE, DH), BF16),
            pltpu.VMEM((blocks, DH, TILE), F32),
            pltpu.VMEM((blocks, DH, TILE), F32),
            pltpu.VMEM((TILE, TILE), BF16),
            pltpu.VMEM((TILE, TILE), BF16),
        ],
        flops=3 * group * group * DH * 2,
        nbytes=7 * group * DH * 2,
    )(user_lengths, qkv, grad)
    own = call(sum_kernel, shape((out_rows, width), BF16), [VMEM], nbytes=width * width)(partial)
    own = own.reshape(ctx, w_rows, LANES)
    grads = exchange(jnp.concatenate([grads, own], axis=1), "ctx")
    summed = jnp.sum(grads[:, 3 * DH :, :].astype(F32), axis=0).astype(BF16)
    proj = exchange(jnp.broadcast_to(summed[None], (ctx, w_rows, LANES)), "ctx")
    proj_grad = proj.reshape(out_rows, width).astype(F32)

    query_grad, key_grad, value_grad = call(
        functools.partial(unpack_kernel, 3),
        [shape((tokens, width), BF16)] * 3,
        [VMEM],
        nbytes=6 * tokens * width * 2,
    )(grads)
    return (query_grad, key_grad, value_grad, gate_grad, proj_grad)


def solution(mesh):
    rows = P(("dp", "ctx"), None)
    in_specs = (rows,) * 6 + (P("dp", None),)
    out_specs = (rows,) * 4 + (P("dp", None),)
    return jax.shard_map(local, mesh=mesh, in_specs=in_specs, out_specs=out_specs, check_vma=False)
```

time: 245 us -> 223 us (0.910)
  blocking collectives: 124 us -> 52.5 us
  starting transfers between devices: 30.4 us -> 83.6 us
  waiting for transfers between devices: 43.5 us -> 57.5 us
  between operations: 14.2 us -> 0.95 us
  Pallas kernels: 25 us -> 21.2 us
    all_to_all x3 -> x1, blocking collectives: 124 us -> 52.5 us  [exchange(): lax.all_to_all(array, axis, split_axis=0, concat_axis=0, tiled=True, axis...]
    ppermute x1 -> x10, starting transfers between devices: 2.41 us -> 32.6 us  [the longest x2 7.66 us: ring_blocks(): back_three = lax.ppermute(block, 'dp', down)]
    all_to_all x4 -> x6, starting transfers between devices: 26.1 us -> 49.1 us  [exchange(): lax.all_to_all(array, axis, split_axis=0, concat_axis=0, tiled=True, axis...]
    ppermute x1 -> x10, waiting for transfers between devices: 0.95 us -> 12.6 us  [the longest x2 7.31 us: ring_blocks(): low = lax.ppermute(back_one[:half], 'dp', up)]
    pallas_call x1, Pallas kernels: 10.5 us -> 7.5 us  [local(): call(backward_kernel, shape((ctx, 3 * DH, tokens), BF16), [SMEM, VMEM, VM...]
    all_to_all x4 -> x6, waiting for transfers between devices: 42.5 us -> 43.5 us  [exchange(): lax.all_to_all(array, axis, split_axis=0, concat_axis=0, tiled=True, axis...]
    pallas_call x5 -> x6, Pallas kernels: 13.4 us -> 12.6 us  [the longest x1 6.27 us: local(): call(forward_kernel, shape((ctx, DH, tokens), BF16), [SMEM, VMEM], [pltpu...]
  transfers between devices with their start and end apart: 7 -> 17, of which waited for: 5 -> 13; matrix products, arithmetic and copies ran while one was open for 0% -> 0% of each run, Pallas kernels for 9% -> 6%
where the time goes in v2:
time: 223 us; the launch traced here: 222 us
  starting transfers between devices  83.6 us (37%)
  waiting for transfers between devices  57.5 us (26%)
  blocking collectives  52.5 us (24%)
  Pallas kernels  21.2 us (10%)
  local copies, waits for them, and re-layouts  5.64 us (3%)
    all_to_all x1, blocking collectives, exchange(): lax.all_to_all(array, axis, split_axis=0, concat_axis=0, tiled=True, axis...  52.5 us
    all_to_all x6, starting transfers between devices, exchange(): lax.all_to_all(array, axis, split_axis=0, concat_axis=0, tiled=True, axis...  49.1 us
    all_to_all x6, waiting for transfers between devices, exchange(): lax.all_to_all(array, axis, split_axis=0, concat_axis=0, tiled=True, axis...  43.5 us
    ppermute x2, starting transfers between devices, ring_blocks(): back_three = lax.ppermute(block, 'dp', down)  7.66 us
    ppermute x2, starting transfers between devices, ring_blocks(): high = lax.ppermute(back_three[half:], 'dp', down)  7.51 us
    pallas_call x1, Pallas kernels, local(): call(backward_kernel, shape((ctx, 3 * DH, tokens), BF16), [SMEM, VMEM, VM...  7.5 us
    ppermute x2, waiting for transfers between devices, ring_blocks(): low = lax.ppermute(back_one[:half], 'dp', up)  7.31 us
    ppermute x2, starting transfers between devices, ring_blocks(): low = lax.ppermute(back_one[:half], 'dp', up)  7.18 us
  transfers between devices with their start and end apart: 17, of which 13 were waited for; matrix products, arithmetic and copies ran while one was open for 0% of the time, Pallas kernels for 6%

profile of v2, /device:TPU:6, one launch (start us, length us, event | category | flops | bytes accessed | tf_op | source)
XLA Modules:
  0.0 221.5 jit_solution(839026490451340485)
XLA Ops:
  2.0 15.2 %all-to-all-start = ((bf16[16,16,128]{2,1,0:T(8,128)(2,1)}), bf16[16,16,128]{2,1,0:T(8,128)(2,1)S(1)}, u32[]{:S(2)}, u32[]{:S(2)}) async-start(bf16[16,16,128]{2,1,0:T(8,128)(2,1)} %broadcast_in_dim.14), calls=%async_computation | async-start | bytes 131072 | tf_op jit(solution)/shard_map/all_to_all | solution.py:314
  21.4 8.5 %all-to-all-done = bf16[16,16,128]{2,1,0:T(8,128)(2,1)S(1)} async-done(((bf16[16,16,128]{2,1,0:T(8,128)(2,1)}), bf16[16,16,128]{2,1,0:T(8,128)(2,1)S(1)}, u32[]{:S(2)}, u32[]{:S(2)}) %all-to-all-start) | async-done | bytes 65568 | tf_op jit(solution)/shard_map/all_to_all | solution.py:314
  29.9 3.6 %all-to-all-start.1 = ((bf16[16,192,128]{2,1,0:T(8,128)(2,1)}), bf16[16,192,128]{2,1,0:T(8,128)(2,1)S(1)}, u32[]{:S(2)}, u32[]{:S(2)}) async-start(bf16[16,192,128]{2,1,0:T(8,128)(2,1)} %shard_map.110), calls=%async_computation.1 | async-start | bytes 1572864 | tf_op jit(solution)/shard_map/all_to_all | solution.py:314
  33.6 2.7 %collective-permute-start.2 = (bf16[32,1024]{1,0:T(8,128)(2,1)S(1)}, bf16[32,1024]{1,0:T(8,128)(2,1)S(1)}, u32[]{:S(2)}, u32[]{:S(2)}) collective-permute-start(bf16[32,1024]{1,0:T(8,128)(2,1)S(1)} %reshape.25), channel_id=1, source_target_pairs={{0,384},{16,400},{32,416},{48,432},{64,448},{80,464},{96,480},{112... | collective-permute-start | bytes 196616 | tf_op jit(solution)/shard_map/ppermute | solution.py:337
  36.3 4.3 %collective-permute-start = (bf16[32,1024]{1,0:T(8,128)(2,1)S(1)}, bf16[32,1024]{1,0:T(8,128)(2,1)S(1)}, u32[]{:S(2)}, u32[]{:S(2)}) collective-permute-start(bf16[32,1024]{1,0:T(8,128)(2,1)S(1)} %reshape.25), channel_id=1, source_target_pairs={{0,128},{16,144},{32,160},{48,176},{64,192},{80,208},{96,224},{112... | collective-permute-start | bytes 196616 | tf_op jit(solution)/shard_map/ppermute | solution.py:336
  40.9 1.9 collective-permute-start.3
  42.9 5.1 %collective-permute-start.1 = (bf16[16,1024]{1,0:T(8,128)(2,1)S(1)}, bf16[16,1024]{1,0:T(8,128)(2,1)S(1)}, u32[]{:S(2)}, u32[]{:S(2)}) collective-permute-start(bf16[16,1024]{1,0:T(8,128)(2,1)S(1)} %slice.20), channel_id=1, source_target_pairs={{0,128},{16,144},{32,160},{48,176},{64,192},{80,208},{96,224},{112... | collective-permute-start | bytes 98312 | tf_op jit(solution)/shard_map/ppermute | solution.py:339
  48.0 1.6 collective-permute-done.1
  49.6 4.9 %collective-permute-start.6 = (bf16[4,32,1024]{2,1,0:T(8,128)(2,1)S(1)}, bf16[4,32,1024]{2,1,0:T(8,128)(2,1)S(1)}, u32[]{:S(2)}, u32[]{:S(2)}) collective-permute-start(bf16[4,32,1024]{2,1,0:T(8,128)(2,1)S(1)} %bitcast.5), channel_id=1, source_target_pairs={{0,96},{16,112},{32,0},{48,16},{64,32},{80,48},{96,64},{112,80},{1... | collective-permute-start | bytes 786440 | tf_op jit(solution)/shard_map/ppermute | solution.py:337
  54.6 1.9 collective-permute-start.4
  56.5 1.9 collective-permute-done.6.w3_ref
  58.4 5.6 %collective-permute-start.7 = (bf16[2,32,1024]{2,1,0:T(8,128)(2,1)S(1)}, bf16[2,32,1024]{2,1,0:T(8,128)(2,1)S(1)}, u32[]{:S(2)}, u32[]{:S(2)}) collective-permute-start(bf16[2,32,1024]{2,1,0:T(8,128)(2,1)S(1)} %slice.23), channel_id=1, source_target_pairs={{0,96},{16,112},{32,0},{48,16},{64,32},{80,48},{96,64},{112,80},{1... | collective-permute-start | bytes 393224 | tf_op jit(solution)/shard_map/ppermute | solution.py:340
  64.1 2.1 collective-permute-start.5
  66.6 5.7 %collective-permute-done.5.w2_low_ref = bf16[2,32,1024]{2,1,0:T(8,128)(2,1)S(1)} collective-permute-done((bf16[2,32,1024]{2,1,0:T(8,128)(2,1)S(1)}, bf16[2,32,1024]{2,1,0:T(8,128)(2,1)S(1)}, u32[]{:S(2)}, u32[]{:S(2)}) %collective-permute-start.5) | collective-permute-done | bytes 131104 | tf_op jit(solution)/shard_map/ppermute | solution.py:339
  72.3 6.3 %shard_map.111 = bf16[16,64,128]{2,1,0:T(8,128)(2,1)} custom-call(s32[1,4]{1,0:T(1,128)S(1)} %copy-done.5, bf16[16,192,128]{2,1,0:T(8,128)(2,1)S(1)} %all-to-all-done.1.qkv_ref), custom_call_target="tpu_custom_call" | custom-call | flops 536870912 | bytes 1310720 | tf_op jit(solution)/shard_map/pallas_call | solution.py:389
  78.6 12.1 %all-to-all-start.2 = ((bf16[16,64,128]{2,1,0:T(8,128)(2,1)}), bf16[16,64,128]{2,1,0:T(8,128)(2,1)S(1)}, u32[]{:S(2)}, u32[]{:S(2)}) async-start(bf16[16,64,128]{2,1,0:T(8,128)(2,1)} %shard_map.111), calls=%async_computation.2 | async-start | bytes 524288 | tf_op jit(solution)/shard_map/all_to_all | solution.py:314
  90.7 1.9 collective-permute-start.8
  92.7 1.4 collective-permute-done.8.other_grad_ref
  94.1 1.5 shard_map.112
  95.6 2.0 collective-permute-start.9
  99.0 5.8 %all-to-all-done.2.o_ref = bf16[16,64,128]{2,1,0:T(8,128)(2,1)S(1)} async-done(((bf16[16,64,128]{2,1,0:T(8,128)(2,1)}), bf16[16,64,128]{2,1,0:T(8,128)(2,1)S(1)}, u32[]{:S(2)}, u32[]{:S(2)}) %all-to-all-start.2) | async-done | bytes 262176 | tf_op jit(solution)/shard_map/all_to_all | solution.py:314
  104.9 1.9 shard_map.113
  106.8 6.2 %all-to-all-start.3 = ((bf16[16,64,128]{2,1,0:T(8,128)(2,1)}), bf16[16,64,128]{2,1,0:T(8,128)(2,1)S(1)}, u32[]{:S(2)}, u32[]{:S(2)}) async-start(bf16[16,64,128]{2,1,0:T(8,128)(2,1)} %get-tuple-element.32), calls=%async_computation.3 | async-start | bytes 524288 | tf_op jit(solution)/shard_map/all_to_all | solution.py:314
  113.0 1.9 collective-permute-start.10
  116.2 1.4 shard_map.115
  117.6 13.8 %all-to-all-done.3.g_ref = bf16[16,64,128]{2,1,0:T(8,128)(2,1)S(1)} async-done(((bf16[16,64,128]{2,1,0:T(8,128)(2,1)}), bf16[16,64,128]{2,1,0:T(8,128)(2,1)S(1)}, u32[]{:S(2)}, u32[]{:S(2)}) %all-to-all-start.3) | async-done | bytes 262176 | tf_op jit(solution)/shard_map/all_to_all | solution.py:314
  131.5 6.4 %all-to-all-start.4 = ((bf16[16,32,1024]{2,1,0:T(8,128)(2,1)}), bf16[16,32,1024]{2,1,0:T(8,128)(2,1)S(1)}, u32[]{:S(2)}, u32[]{:S(2)}) async-start(bf16[16,32,1024]{2,1,0:T(8,128)(2,1)} %shard_map.115), calls=%async_computation.4 | async-start | bytes 2097152 | tf_op jit(solution)/shard_map/all_to_all | solution.py:314
  137.9 7.5 %shard_map.114 = bf16[16,192,128]{2,1,0:T(8,128)(2,1)S(1)} custom-call(s32[1,4]{1,0:T(1,128)S(1)} %copy-done.5, bf16[16,192,128]{2,1,0:T(8,128)(2,1)S(1)} %all-to-all-done.1.qkv_ref, bf16[16,64,128]{2,1,0:T(8,128)(2,1)S(1)} %all-to-all-done.3.g_ref), custom_call_target="tpu_custom_call" | custom-call | flops 1610612736 | bytes 1835008 | tf_op jit(solution)/shard_map/pallas_call | solution.py:423
  145.4 3.5 %all-to-all-done.4.x_ref = bf16[16,32,1024]{2,1,0:T(8,128)(2,1)S(1)} async-done(((bf16[16,32,1024]{2,1,0:T(8,128)(2,1)}), bf16[16,32,1024]{2,1,0:T(8,128)(2,1)S(1)}, u32[]{:S(2)}, u32[]{:S(2)}) %all-to-all-start.4) | async-done | bytes 1048608 | tf_op jit(solution)/shard_map/all_to_all | solution.py:314
  149.1 52.5 %all_to_all.35.x_ref = bf16[16,208,128]{2,1,0:T(8,128)(2,1)S(1)} all-to-all(bf16[16,208,128]{2,1,0:T(8,128)(2,1)S(1)} %pad_maximum_fusion), channel_id=1, replica_groups=mesh['dp'=32,'ctx'=16] {'ctx'}, dimensions={0} | all-to-all | bytes 1703936 | tf_op jit(solution)/shard_map/all_to_all | solution.py:314
  202.3 5.6 %all-to-all-start.6 = ((bf16[16,16,128]{2,1,0:T(8,128)(2,1)}), bf16[16,16,128]{2,1,0:T(8,128)(2,1)S(1)}, u32[]{:S(2)}, u32[]{:S(2)}) async-start(bf16[16,16,128]{2,1,0:T(8,128)(2,1)} %broadcast_in_dim.15), calls=%async_computation.6 | async-start | bytes 131072 | tf_op jit(solution)/shard_map/all_to_all | solution.py:314
  209.1 11.7 %all-to-all-done.6 = bf16[16,16,128]{2,1,0:T(8,128)(2,1)S(1)} async-done(((bf16[16,16,128]{2,1,0:T(8,128)(2,1)}), bf16[16,16,128]{2,1,0:T(8,128)(2,1)S(1)}, u32[]{:S(2)}, u32[]{:S(2)}) %all-to-all-start.6) | async-done | bytes 65568 | tf_op jit(solution)/shard_map/all_to_all | solution.py:314
  (41 shorter events, 11.8 us)
Async XLA Ops:
  2.0 27.9 %all-to-all-start = ((bf16[16,16,128]{2,1,0:T(8,128)(2,1)}), bf16[16,16,128]{2,1,0:T(8,128)(2,1)S(1)}, u32[]{:S(2)}, u32[]{:S(2)}) async-start(bf16[16,16,128]{2,1,0:T(8,128)(2,1)} %broadcast_in_dim.14), calls=%async_computation | async-start | bytes 131072 | tf_op jit(solution)/shard_map/all_to_all | solution.py:314
  17.2 1.0 copy-start.2
  18.1 0.9 copy-start.3
  19.1 0.9 copy-start.4
  29.9 42.4 %all-to-all-start.1 = ((bf16[16,192,128]{2,1,0:T(8,128)(2,1)}), bf16[16,192,128]{2,1,0:T(8,128)(2,1)S(1)}, u32[]{:S(2)}, u32[]{:S(2)}) async-start(bf16[16,192,128]{2,1,0:T(8,128)(2,1)} %shard_map.110), calls=%async_computation.1 | async-start | bytes 1572864 | tf_op jit(solution)/shard_map/all_to_all | solution.py:314
  33.5 38.8 %copy-start.5 = (s32[1,4]{1,0:T(1,128)S(1)}, s32[1,4]{1,0:T(1,128)}, u32[]{:S(2)}) copy-start(s32[1,4]{1,0:T(1,128)} %len_ref.5) | copy-start | bytes 52
  33.6 7.4 %collective-permute-start.2 = (bf16[32,1024]{1,0:T(8,128)(2,1)S(1)}, bf16[32,1024]{1,0:T(8,128)(2,1)S(1)}, u32[]{:S(2)}, u32[]{:S(2)}) collective-permute-start(bf16[32,1024]{1,0:T(8,128)(2,1)S(1)} %reshape.25), channel_id=1, source_target_pairs={{0,384},{16,400},{32,416},{48,432},{64,448},{80,464},{96,480},{112... | collective-permute-start | bytes 196616 | tf_op jit(solution)/shard_map/ppermute | solution.py:337
  36.3 6.5 %collective-permute-start = (bf16[32,1024]{1,0:T(8,128)(2,1)S(1)}, bf16[32,1024]{1,0:T(8,128)(2,1)S(1)}, u32[]{:S(2)}, u32[]{:S(2)}) collective-permute-start(bf16[32,1024]{1,0:T(8,128)(2,1)S(1)} %reshape.25), channel_id=1, source_target_pairs={{0,128},{16,144},{32,160},{48,176},{64,192},{80,208},{96,224},{112... | collective-permute-start | bytes 196616 | tf_op jit(solution)/shard_map/ppermute | solution.py:336
  40.9 8.7 %collective-permute-start.3 = (bf16[16,1024]{1,0:T(8,128)(2,1)S(1)}, bf16[16,1024]{1,0:T(8,128)(2,1)S(1)}, u32[]{:S(2)}, u32[]{:S(2)}) collective-permute-start(bf16[16,1024]{1,0:T(8,128)(2,1)S(1)} %slice.21), channel_id=1, source_target_pairs={{0,384},{16,400},{32,416},{48,432},{64,448},{80,464},{96,480},{112... | collective-permute-start | bytes 98312 | tf_op jit(solution)/shard_map/ppermute | solution.py:340
  42.9 6.7 %collective-permute-start.1 = (bf16[16,1024]{1,0:T(8,128)(2,1)S(1)}, bf16[16,1024]{1,0:T(8,128)(2,1)S(1)}, u32[]{:S(2)}, u32[]{:S(2)}) collective-permute-start(bf16[16,1024]{1,0:T(8,128)(2,1)S(1)} %slice.20), channel_id=1, source_target_pairs={{0,128},{16,144},{32,160},{48,176},{64,192},{80,208},{96,224},{112... | collective-permute-start | bytes 98312 | tf_op jit(solution)/shard_map/ppermute | solution.py:339
  49.6 8.8 %collective-permute-start.6 = (bf16[4,32,1024]{2,1,0:T(8,128)(2,1)S(1)}, bf16[4,32,1024]{2,1,0:T(8,128)(2,1)S(1)}, u32[]{:S(2)}, u32[]{:S(2)}) collective-permute-start(bf16[4,32,1024]{2,1,0:T(8,128)(2,1)S(1)} %bitcast.5), channel_id=1, source_target_pairs={{0,96},{16,112},{32,0},{48,16},{64,32},{80,48},{96,64},{112,80},{1... | collective-permute-start | bytes 786440 | tf_op jit(solution)/shard_map/ppermute | solution.py:337
  54.6 9.5 %collective-permute-start.4 = (bf16[4,32,1024]{2,1,0:T(8,128)(2,1)S(1)}, bf16[4,32,1024]{2,1,0:T(8,128)(2,1)S(1)}, u32[]{:S(2)}, u32[]{:S(2)}) collective-permute-start(bf16[4,32,1024]{2,1,0:T(8,128)(2,1)S(1)} %bitcast.6), channel_id=1, source_target_pairs={{0,32},{16,48},{32,64},{48,80},{64,96},{80,112},{96,0},{112,16},{1... | collective-permute-start | bytes 786440 | tf_op jit(solution)/shard_map/ppermute | solution.py:336
  58.4 8.1 %collective-permute-start.7 = (bf16[2,32,1024]{2,1,0:T(8,128)(2,1)S(1)}, bf16[2,32,1024]{2,1,0:T(8,128)(2,1)S(1)}, u32[]{:S(2)}, u32[]{:S(2)}) collective-permute-start(bf16[2,32,1024]{2,1,0:T(8,128)(2,1)S(1)} %slice.23), channel_id=1, source_target_pairs={{0,96},{16,112},{32,0},{48,16},{64,32},{80,48},{96,64},{112,80},{1... | collective-permute-start | bytes 393224 | tf_op jit(solution)/shard_map/ppermute | solution.py:340
  64.1 26.6 %copy-start = (bf16[128,1024]{1,0:T(8,128)(2,1)S(1)}, bf16[128,1024]{1,0:T(8,128)(2,1)}, u32[]{:S(2)}) copy-start(bf16[128,1024]{1,0:T(8,128)(2,1)} %out_grad_ref.3) | copy-start | bytes 786436
  64.1 8.2 %collective-permute-start.5 = (bf16[2,32,1024]{2,1,0:T(8,128)(2,1)S(1)}, bf16[2,32,1024]{2,1,0:T(8,128)(2,1)S(1)}, u32[]{:S(2)}, u32[]{:S(2)}) collective-permute-start(bf16[2,32,1024]{2,1,0:T(8,128)(2,1)S(1)} %slice.22), channel_id=1, source_target_pairs={{0,32},{16,48},{32,64},{48,80},{64,96},{80,112},{96,0},{112,16},{1... | collective-permute-start | bytes 393224 | tf_op jit(solution)/shard_map/ppermute | solution.py:339
  78.6 26.3 %copy-start.1 = (bf16[128,1024]{1,0:T(8,128)(2,1)S(1)}, bf16[128,1024]{1,0:T(8,128)(2,1)}, u32[]{:S(2)}) copy-start(bf16[128,1024]{1,0:T(8,128)(2,1)} %gate_ref.1) | copy-start | bytes 786436
  78.6 26.3 %all-to-all-start.2 = ((bf16[16,64,128]{2,1,0:T(8,128)(2,1)}), bf16[16,64,128]{2,1,0:T(8,128)(2,1)S(1)}, u32[]{:S(2)}, u32[]{:S(2)}) async-start(bf16[16,64,128]{2,1,0:T(8,128)(2,1)} %shard_map.111), calls=%async_computation.2 | async-start | bytes 524288 | tf_op jit(solution)/shard_map/all_to_all | solution.py:314
  90.7 3.4 %collective-permute-start.8 = (bf16[128,1024]{1,0:T(8,128)(2,1)S(1)}, bf16[128,1024]{1,0:T(8,128)(2,1)S(1)}, u32[]{:S(2)}, u32[]{:S(2)}) collective-permute-start(bf16[128,1024]{1,0:T(8,128)(2,1)S(1)} %copy-done), channel_id=1, source_target_pairs={{0,16},{16,0},{32,48},{48,32},{64,80},{80,64},{96,112},{112,96},{1... | collective-permute-start | bytes 786440 | tf_op jit(solution)/shard_map/ppermute | solution.py:379
  95.6 3.4 %collective-permute-start.9 = (f32[16,32,128]{2,1,0:T(8,128)S(1)}, f32[16,32,128]{2,1,0:T(8,128)S(1)}, u32[]{:S(2)}, u32[]{:S(2)}) collective-permute-start(f32[16,32,128]{2,1,0:T(8,128)S(1)} %get-tuple-element.31), channel_id=1, source_target_pairs={{0,16},{16,0},{32,48},{48,32},{64,80},{80,64},{96,112},{112,96},{1... | collective-permute-start | bytes 786440 | tf_op jit(solution)/shard_map/ppermute | solution.py:387
  106.8 24.7 %all-to-all-start.3 = ((bf16[16,64,128]{2,1,0:T(8,128)(2,1)}), bf16[16,64,128]{2,1,0:T(8,128)(2,1)S(1)}, u32[]{:S(2)}, u32[]{:S(2)}) async-start(bf16[16,64,128]{2,1,0:T(8,128)(2,1)} %get-tuple-element.32), calls=%async_computation.3 | async-start | bytes 524288 | tf_op jit(solution)/shard_map/all_to_all | solution.py:314
  113.0 3.2 %collective-permute-start.10 = (bf16[16,32,128]{2,1,0:T(8,128)(2,1)S(1)}, bf16[16,32,128]{2,1,0:T(8,128)(2,1)S(1)}, u32[]{:S(2)}, u32[]{:S(2)}) collective-permute-start(bf16[16,32,128]{2,1,0:T(8,128)(2,1)S(1)} %get-tuple-element.34), channel_id=1, source_target_pairs={{0,16},{16,0},{32,48},{48,32},{64,80},{80,64},{96,112},{112,96},{1... | collective-permute-start | bytes 393224 | tf_op jit(solution)/shard_map/ppermute | solution.py:413
  131.5 17.4 %all-to-all-start.4 = ((bf16[16,32,1024]{2,1,0:T(8,128)(2,1)}), bf16[16,32,1024]{2,1,0:T(8,128)(2,1)S(1)}, u32[]{:S(2)}, u32[]{:S(2)}) async-start(bf16[16,32,1024]{2,1,0:T(8,128)(2,1)} %shard_map.115), calls=%async_computation.4 | async-start | bytes 2097152 | tf_op jit(solution)/shard_map/all_to_all | solution.py:314
  202.3 18.5 %all-to-all-start.6 = ((bf16[16,16,128]{2,1,0:T(8,128)(2,1)}), bf16[16,16,128]{2,1,0:T(8,128)(2,1)S(1)}, u32[]{:S(2)}, u32[]{:S(2)}) async-start(bf16[16,16,128]{2,1,0:T(8,128)(2,1)} %broadcast_in_dim.15), calls=%async_computation.6 | async-start | bytes 131072 | tf_op jit(solution)/shard_map/all_to_all | solution.py:314

commit v3 on v2

--- a/solution.py
+++ b/solution.py
@@ -1,4 +1,3 @@
-import functools
 import math
 
 import jax
@@ -11,11 +10,12 @@
 DH = 64
 LANES = 128
 TILE = 256
+SUM_ROWS = 16
 BF16 = jnp.bfloat16
 F32 = jnp.float32
 VMEM = pl.BlockSpec(memory_space=pltpu.VMEM)
 SMEM = pl.BlockSpec(memory_space=pltpu.SMEM)
-LIMIT = 48 * 1024 * 1024
+LIMIT = 16 * 1024 * 1024
 
 
 def call(kernel, out_shape, in_specs, scratch=(), flops=0, nbytes=0):
@@ -30,6 +30,15 @@
         compiler_params=pltpu.CompilerParams(vmem_limit_bytes=LIMIT),
         cost_estimate=pl.CostEstimate(flops=flops, bytes_accessed=nbytes, transcendentals=0),
     )
+
+
+def spread_kernel(w_ref, out_ref):
+    count, width = w_ref.shape
+    weight = w_ref[...].astype(F32)
+    pieces = [weight[:, j * LANES : (j + 1) * LANES] for j in range(width // LANES)]
+    rows = jnp.concatenate(pieces, axis=0).astype(BF16)
+    for chunk in range(out_ref.shape[0]):
+        out_ref[chunk] = rows
 
 
 def pack_kernel(q_hbm, k_hbm, v_hbm, out_ref, rows_ref, sems):
@@ -48,13 +57,26 @@
             out_ref[2 * pair + 1, i * DH : (i + 1) * DH, :] = both[DH:]
 
 
-def unpack_kernel(count, x_ref, *out_refs):
-    heads = x_ref.shape[0]
-    for pair in range(heads // 2):
-        for i in range(count):
+def unpack_kernel(x_ref, q_ref, k_ref, v_ref, proj_ref):
+    for pair in range(x_ref.shape[0] // 2):
+        for i, out_ref in enumerate((q_ref, k_ref, v_ref)):
             rows = slice(i * DH, (i + 1) * DH)
             both = jnp.concatenate([x_ref[2 * pair, rows, :], x_ref[2 * pair + 1, rows, :]], axis=0)
-            out_refs[i][:, pair * 2 * DH : (pair + 1) * 2 * DH] = both.T
+            out_ref[:, pair * 2 * DH : (pair + 1) * 2 * DH] = both.T
+    for row, col, chunk in proj_tiles(proj_ref.shape):
+        proj_ref[row, col] = x_ref[chunk, 3 * DH :, :].astype(F32)
+
+
+def proj_tiles(shape):
+    rows, width = shape
+    per_row = width // LANES
+    for i in range(rows // SUM_ROWS):
+        for j in range(per_row):
+            yield (
+                slice(i * SUM_ROWS, (i + 1) * SUM_ROWS),
+                slice(j * LANES, (j + 1) * LANES),
+                i * per_row + j,
+            )
 
 
 def user_edges(len_ref):
@@ -202,6 +224,9 @@
         total = (total * scale).astype(BF16)
         out_ref[2 * row_block, 0:DH, :] = total[:, :LANES]
         out_ref[2 * row_block + 1, 0:DH, :] = total[:, LANES:]
+    total = jnp.sum(g_ref[:, DH:, :].astype(F32), axis=0).astype(BF16)
+    for chunk in range(out_ref.shape[0]):
+        out_ref[chunk, 3 * DH :, :] = total
     for block in range(blocks):
         k_grad = (k_acc[block] * scale).astype(BF16)
         v_grad = v_acc[block].astype(BF16)
@@ -230,33 +255,43 @@
             theirs_ref[x * side + y] = product[i * rows : (i + 1) * rows, tokens:]
 
 
-def norm_kernel(
-    len_ref,
-    place_ref,
-    o_ref,
-    mine_ref,
-    recv_ref,
-    gate_ref,
-    grad_ref,
-    gated_mine_ref,
-    gated_other_ref,
-    gate_grad_ref,
-    normed_grad_ref,
-):
+def norm_stats(o_ref):
     heads, _, tokens = o_ref.shape
-    width = heads * DH
-    half = DH // 2
-    even = place_ref[1] == 0
+    share = 1.0 / (heads * DH)
     total = jnp.zeros((DH, tokens), F32)
     for head in range(heads):
         total = total + o_ref[head].astype(F32)
-    mean = jnp.sum(total, axis=0, keepdims=True) * (1.0 / width)
+    mean = jnp.sum(total, axis=0, keepdims=True) * share
     total = jnp.zeros((DH, tokens), F32)
     for head in range(heads):
         centred = o_ref[head].astype(F32) - mean
         total = total + centred * centred
-    var = jnp.sum(total, axis=0, keepdims=True) * (1.0 / width)
-    rstd = lax.rsqrt(var + 1e-05)
+    var = jnp.sum(total, axis=0, keepdims=True) * share
+    return mean, lax.rsqrt(var + 1e-05)
+
+
+def gated_kernel(place_ref, o_ref, gate_ref, mine_ref, other_ref):
+    half = DH // 2
+    even = place_ref[1] == 0
+    mean, rstd = norm_stats(o_ref)
+    for pair in range(o_ref.shape[0] // 2):
+        gates = gate_ref[:, pair * 2 * DH : (pair + 1) * 2 * DH].T.astype(F32)
+        for i in range(2):
+            head = 2 * pair + i
+            normed = (o_ref[head].astype(F32) - mean) * rstd
+            gated = normed * gates[i * DH : (i + 1) * DH]
+            low, high = gated[:half], gated[half:]
+            mine_ref[head] = jnp.where(even, low, high).astype(BF16)
+            other_ref[head] = jnp.where(even, high, low).astype(BF16)
+
+
+def norm_kernel(
+    len_ref, place_ref, o_ref, mine_ref, recv_ref, gate_ref, grad_ref, gate_grad_ref, normed_grad_ref
+):
+    heads, _, tokens = o_ref.shape
+    width = heads * DH
+    even = place_ref[1] == 0
+    mean, rstd = norm_stats(o_ref)
     first = jnp.zeros((DH, tokens), F32)
     second = jnp.zeros((DH, tokens), F32)
     for pair in range(heads // 2):
@@ -270,13 +305,8 @@
             gated_grad = jnp.concatenate(
                 [jnp.where(even, mine, recv), jnp.where(even, recv, mine)], axis=0
             )
-            gate = gates[i * DH : (i + 1) * DH]
-            gated = normed * gate
-            low, high = gated[:half], gated[half:]
-            gated_mine_ref[head] = jnp.where(even, low, high).astype(BF16)
-            gated_other_ref[head] = jnp.where(even, high, low).astype(BF16)
             gate_grads.append((gated_grad * normed).astype(BF16))
-            normed_grad = gated_grad * gate
+            normed_grad = gated_grad * gates[i * DH : (i + 1) * DH]
             first = first + normed_grad
             second = second + normed_grad * normed
             normed_grad_ref[head] = normed_grad
@@ -306,8 +336,12 @@
             out_ref[part, :, cols] = product.astype(BF16).reshape(step, rows, 256)
 
 
-def sum_kernel(x_ref, out_ref):
-    out_ref[...] = jnp.sum(x_ref[...].astype(F32), axis=0).astype(BF16)
+def sum_kernel(x_ref, grad_ref, out_ref):
+    _, rows, width = x_ref.shape
+    out_ref[:, :DH, :] = grad_ref[...]
+    for row, col, chunk in proj_tiles((rows, width)):
+        tile = jnp.sum(x_ref[:, row, col].astype(F32), axis=0)
+        out_ref[chunk, DH:, :] = tile.astype(BF16)
 
 
 def exchange(array, axis, groups=None):
@@ -360,8 +394,10 @@
     ).astype(jnp.int32)
     in_hbm = pl.BlockSpec(memory_space=pltpu.HBM)
 
-    block = proj_weight.reshape(1, w_rows, LANES)
-    block = exchange(jnp.broadcast_to(block, (ctx, w_rows, LANES)), "ctx")
+    block = call(
+        spread_kernel, shape((ctx, w_rows, LANES), BF16), [VMEM], nbytes=tokens * width
+    )(proj_weight)
+    block = exchange(block, "ctx")
     qkv = call(
         pack_kernel,
         shape((heads, 3 * DH, tokens), BF16),
@@ -372,6 +408,7 @@
     block, qkv = lax.optimization_barrier((block, qkv))
     qkv = exchange(qkv, "ctx")
 
+    block = block.reshape(ctx, width // LANES, out_rows // ctx, LANES).transpose(0, 2, 1, 3)
     block = block.reshape(out_rows, width)
     column = jnp.concatenate(ring_blocks(block, "x"), axis=0).reshape(SIDE, out_rows, width)
     weights = ring_blocks(column, "y")
@@ -396,20 +433,12 @@
     )(user_lengths, qkv)
     attn_out = exchange(attn_out, "ctx")
 
-    grad, gated_mine, gated_other, gate_grad = call(
-        norm_kernel,
-        [
-            shape((heads, DH, tokens), BF16),
-            shape((heads, DH // 2, tokens), BF16),
-            shape((heads, DH // 2, tokens), BF16),
-            shape((tokens, width), BF16),
-        ],
-        [SMEM, SMEM, VMEM, VMEM, VMEM, VMEM],
-        [pltpu.VMEM((heads, DH, tokens), F32)],
-        nbytes=18 * tokens * width,
-    )(user_lengths, place, attn_out, mine, received, gate_rows)
-    grad = exchange(grad, "ctx")
-
+    gated_mine, gated_other = call(
+        gated_kernel,
+        [shape((heads, DH // 2, tokens), BF16)] * 2,
+        [SMEM, VMEM, VMEM],
+        nbytes=6 * tokens * width,
+    )(place, attn_out, gate_rows)
     other = lax.ppermute(gated_other, "dp", partner)
     partial = call(
         proj_kernel,
@@ -419,10 +448,24 @@
         nbytes=2 * width * width,
     )(gated_mine, other, out_grad, other_grad)
     partial = exchange(partial, "dp", same_core)
+    grad, gate_grad = call(
+        norm_kernel,
+        [shape((heads, DH, tokens), BF16), shape((tokens, width), BF16)],
+        [SMEM, SMEM, VMEM, VMEM, VMEM, VMEM],
+        [pltpu.VMEM((heads, DH, tokens), F32)],
+        nbytes=18 * tokens * width,
+    )(user_lengths, place, attn_out, mine, received, gate_rows)
+    grad = call(
+        sum_kernel,
+        shape((ctx, DH + w_rows, tokens), BF16),
+        [VMEM, VMEM],
+        nbytes=width * width + 4 * tokens * width,
+    )(partial, grad)
+    grad = exchange(grad, "ctx")
 
     grads = call(
         backward_kernel,
-        shape((ctx, 3 * DH, tokens), BF16),
+        shape((ctx, 3 * DH + w_rows, tokens), BF16),
         [SMEM, VMEM, VMEM],
         [
             pltpu.VMEM((blocks, TILE, DH), BF16),
@@ -435,16 +478,10 @@
         flops=3 * group * group * DH * 2,
         nbytes=7 * group * DH * 2,
     )(user_lengths, qkv, grad)
-    own = call(sum_kernel, shape((out_rows, width), BF16), [VMEM], nbytes=width * width)(partial)
-    own = own.reshape(ctx, w_rows, LANES)
-    grads = exchange(jnp.concatenate([grads, own], axis=1), "ctx")
-    summed = jnp.sum(grads[:, 3 * DH :, :].astype(F32), axis=0).astype(BF16)
-    proj = exchange(jnp.broadcast_to(summed[None], (ctx, w_rows, LANES)), "ctx")
-    proj_grad = proj.reshape(out_rows, width).astype(F32)
-
-    query_grad, key_grad, value_grad = call(
-        functools.partial(unpack_kernel, 3),
-        [shape((tokens, width), BF16)] * 3,
+    grads = exchange(grads, "ctx")
+    query_grad, key_grad, value_grad, proj_grad = call(
+        unpack_kernel,
+        [shape((tokens, width), BF16)] * 3 + [shape((out_rows, width), F32)],
         [VMEM],
         nbytes=6 * tokens * width * 2,
     )(grads)

time: 223 us -> 219 us (0.982)
  blocking collectives: 52.5 us -> 74.1 us
  waiting for transfers between devices: 57.5 us -> 40.5 us
  starting transfers between devices: 83.6 us -> 71.9 us
  Pallas kernels: 21.2 us -> 23.6 us
    all_to_all x1 -> x2, blocking collectives: 52.5 us -> 74.1 us  [exchange(): lax.all_to_all(array, axis, split_axis=0, concat_axis=0, tiled=True, axis...]
    all_to_all x6 -> x4, waiting for transfers between devices: 43.5 us -> 27.8 us  [exchange(): lax.all_to_all(array, axis, split_axis=0, concat_axis=0, tiled=True, axis...]
    all_to_all x6 -> x4, starting transfers between devices: 49.1 us -> 37.7 us  [exchange(): lax.all_to_all(array, axis, split_axis=0, concat_axis=0, tiled=True, axis...]
    unnamed x16 -> x27, local copies, waits for them, and re-layouts: 2.88 us -> 6.08 us
    pallas_call x4 -> x6, Pallas kernels: 10.7 us -> 12.6 us  [the longest x1 8.05 us: local(): call(backward_kernel, shape((ctx, 3 * DH + w_rows, tokens), BF16), [SMEM,...]
  transfers between devices with their start and end apart: 17 -> 15, of which waited for: 13 -> 10; matrix products, arithmetic and copies ran while one was open for 0% -> 0% of each run, Pallas kernels for 6% -> 3%
where the time goes in v3:
time: 219 us; the launch traced here: 217 us
  blocking collectives  74.1 us (34%)
  starting transfers between devices  71.9 us (33%)
  waiting for transfers between devices  40.5 us (18%)
  Pallas kernels  23.6 us (11%)
  local copies, waits for them, and re-layouts  6.13 us (3%)
    all_to_all x2, blocking collectives, exchange(): lax.all_to_all(array, axis, split_axis=0, concat_axis=0, tiled=True, axis...  74.1 us
    all_to_all x4, starting transfers between devices, exchange(): lax.all_to_all(array, axis, split_axis=0, concat_axis=0, tiled=True, axis...  37.7 us
    all_to_all x4, waiting for transfers between devices, exchange(): lax.all_to_all(array, axis, split_axis=0, concat_axis=0, tiled=True, axis...  27.8 us
    pallas_call x1, Pallas kernels, local(): call(backward_kernel, shape((ctx, 3 * DH + w_rows, tokens), BF16), [SMEM,...  8.05 us
    ppermute x2, starting transfers between devices, ring_blocks(): back_three = lax.ppermute(block, 'dp', down)  7.66 us
    ppermute x2, starting transfers between devices, ring_blocks(): high = lax.ppermute(back_three[half:], 'dp', down)  7.51 us
    ppermute x2, waiting for transfers between devices, ring_blocks(): low = lax.ppermute(back_one[:half], 'dp', up)  7.17 us
    ppermute x2, starting transfers between devices, ring_blocks(): low = lax.ppermute(back_one[:half], 'dp', up)  7.05 us
  transfers between devices with their start and end apart: 15, of which 10 were waited for; matrix products, arithmetic and copies ran while one was open for 0% of the time, Pallas kernels for 3%

profile of v3, /device:TPU:6, one launch (start us, length us, event | category | flops | bytes accessed | tf_op | source)
XLA Modules:
  0.0 217.2 jit_solution(13513812023985678546)
XLA Ops:
  2.0 15.2 %all-to-all-start = ((bf16[16,16,128]{2,1,0:T(8,128)(2,1)}), bf16[16,16,128]{2,1,0:T(8,128)(2,1)S(1)}, u32[]{:S(2)}, u32[]{:S(2)}) async-start(bf16[16,16,128]{2,1,0:T(8,128)(2,1)} %shard_map.110), calls=%async_computation | async-start | bytes 131072 | tf_op jit(solution)/shard_map/all_to_all | solution.py:348
  20.0 1.4 shard_map.111
  21.4 8.5 %all-to-all-done = bf16[16,16,128]{2,1,0:T(8,128)(2,1)S(1)} async-done(((bf16[16,16,128]{2,1,0:T(8,128)(2,1)}), bf16[16,16,128]{2,1,0:T(8,128)(2,1)S(1)}, u32[]{:S(2)}, u32[]{:S(2)}) %all-to-all-start) | async-done | bytes 65568 | tf_op jit(solution)/shard_map/all_to_all | solution.py:348
  29.9 3.6 %all-to-all-start.1 = ((bf16[16,192,128]{2,1,0:T(8,128)(2,1)}), bf16[16,192,128]{2,1,0:T(8,128)(2,1)S(1)}, u32[]{:S(2)}, u32[]{:S(2)}) async-start(bf16[16,192,128]{2,1,0:T(8,128)(2,1)} %shard_map.111), calls=%async_computation.1 | async-start | bytes 1572864 | tf_op jit(solution)/shard_map/all_to_all | solution.py:348
  33.5 2.7 %collective-permute-start.2 = (bf16[32,1024]{1,0:T(8,128)(2,1)S(1)}, bf16[32,1024]{1,0:T(8,128)(2,1)S(1)}, u32[]{:S(2)}, u32[]{:S(2)}) collective-permute-start(bf16[32,1024]{1,0:T(8,128)(2,1)S(1)} %bitcast.21), channel_id=1, source_target_pairs={{0,384},{16,400},{32,416},{48,432},{64,448},{80,464},{96,480},{112... | collective-permute-start | bytes 196616 | tf_op jit(solution)/shard_map/ppermute | solution.py:371
  36.3 4.3 %collective-permute-start = (bf16[32,1024]{1,0:T(8,128)(2,1)S(1)}, bf16[32,1024]{1,0:T(8,128)(2,1)S(1)}, u32[]{:S(2)}, u32[]{:S(2)}) collective-permute-start(bf16[32,1024]{1,0:T(8,128)(2,1)S(1)} %bitcast.22), channel_id=1, source_target_pairs={{0,128},{16,144},{32,160},{48,176},{64,192},{80,208},{96,224},{112... | collective-permute-start | bytes 196616 | tf_op jit(solution)/shard_map/ppermute | solution.py:370
  40.9 1.9 collective-permute-start.3
  42.9 5.1 %collective-permute-start.1 = (bf16[16,1024]{1,0:T(8,128)(2,1)S(1)}, bf16[16,1024]{1,0:T(8,128)(2,1)S(1)}, u32[]{:S(2)}, u32[]{:S(2)}) collective-permute-start(bf16[16,1024]{1,0:T(8,128)(2,1)S(1)} %slice.16), channel_id=1, source_target_pairs={{0,128},{16,144},{32,160},{48,176},{64,192},{80,208},{96,224},{112... | collective-permute-start | bytes 98312 | tf_op jit(solution)/shard_map/ppermute | solution.py:373
  48.0 1.6 collective-permute-done.1
  49.6 4.9 %collective-permute-start.6 = (bf16[4,32,1024]{2,1,0:T(8,128)(2,1)S(1)}, bf16[4,32,1024]{2,1,0:T(8,128)(2,1)S(1)}, u32[]{:S(2)}, u32[]{:S(2)}) collective-permute-start(bf16[4,32,1024]{2,1,0:T(8,128)(2,1)S(1)} %bitcast.15), channel_id=1, source_target_pairs={{0,96},{16,112},{32,0},{48,16},{64,32},{80,48},{96,64},{112,80},{1... | collective-permute-start | bytes 786440 | tf_op jit(solution)/shard_map/ppermute | solution.py:371
  54.5 1.9 collective-permute-start.4
  56.5 1.9 collective-permute-done.6.w3_ref
  58.4 5.6 %collective-permute-start.7 = (bf16[2,32,1024]{2,1,0:T(8,128)(2,1)S(1)}, bf16[2,32,1024]{2,1,0:T(8,128)(2,1)S(1)}, u32[]{:S(2)}, u32[]{:S(2)}) collective-permute-start(bf16[2,32,1024]{2,1,0:T(8,128)(2,1)S(1)} %slice.19), channel_id=1, source_target_pairs={{0,96},{16,112},{32,0},{48,16},{64,32},{80,48},{96,64},{112,80},{1... | collective-permute-start | bytes 393224 | tf_op jit(solution)/shard_map/ppermute | solution.py:374
  64.1 1.9 collective-permute-start.5
  66.6 5.6 %collective-permute-done.5.w2_low_ref = bf16[2,32,1024]{2,1,0:T(8,128)(2,1)S(1)} collective-permute-done((bf16[2,32,1024]{2,1,0:T(8,128)(2,1)S(1)}, bf16[2,32,1024]{2,1,0:T(8,128)(2,1)S(1)}, u32[]{:S(2)}, u32[]{:S(2)}) %collective-permute-start.5) | collective-permute-done | bytes 131104 | tf_op jit(solution)/shard_map/ppermute | solution.py:373
  72.8 6.7 %shard_map.112 = bf16[16,64,128]{2,1,0:T(8,128)(2,1)} custom-call(s32[1,4]{1,0:T(1,128)S(1)} %copy-done.10, bf16[16,192,128]{2,1,0:T(8,128)(2,1)S(1)} %all-to-all-done.1.qkv_ref), custom_call_target="tpu_custom_call" | custom-call | flops 536870912 | bytes 1310720 | tf_op jit(solution)/shard_map/pallas_call | solution.py:426
  79.5 12.1 %all-to-all-start.2 = ((bf16[16,64,128]{2,1,0:T(8,128)(2,1)}), bf16[16,64,128]{2,1,0:T(8,128)(2,1)S(1)}, u32[]{:S(2)}, u32[]{:S(2)}) async-start(bf16[16,64,128]{2,1,0:T(8,128)(2,1)} %shard_map.112), calls=%async_computation.2 | async-start | bytes 524288 | tf_op jit(solution)/shard_map/all_to_all | solution.py:348
  91.6 1.9 collective-permute-start.9
  93.7 11.8 %all-to-all-done.2.o_ref = bf16[16,64,128]{2,1,0:T(8,128)(2,1)S(1)} async-done(((bf16[16,64,128]{2,1,0:T(8,128)(2,1)}), bf16[16,64,128]{2,1,0:T(8,128)(2,1)S(1)}, u32[]{:S(2)}, u32[]{:S(2)}) %all-to-all-start.2) | async-done | bytes 262176 | tf_op jit(solution)/shard_map/all_to_all | solution.py:348
  106.3 1.9 collective-permute-start.8
  108.2 1.3 collective-permute-done.8.other_ref
  109.5 1.4 shard_map.114
  110.9 6.8 %all-to-all-start.3 = ((bf16[16,32,1024]{2,1,0:T(8,128)(2,1)}), bf16[16,32,1024]{2,1,0:T(8,128)(2,1)S(1)}, u32[]{:S(2)}, u32[]{:S(2)}) async-start(bf16[16,32,1024]{2,1,0:T(8,128)(2,1)} %shard_map.114), calls=%async_computation.3 | async-start | bytes 2097152 | tf_op jit(solution)/shard_map/all_to_all | solution.py:348
  119.6 1.5 shard_map.115
  121.1 1.9 collective-permute-start.10
  123.0 1.5 collective-permute-done.10.recv_ref
  124.5 1.8 shard_map.116
  126.3 7.5 %all-to-all-done.3.x_ref = bf16[16,32,1024]{2,1,0:T(8,128)(2,1)S(1)} async-done(((bf16[16,32,1024]{2,1,0:T(8,128)(2,1)}), bf16[16,32,1024]{2,1,0:T(8,128)(2,1)S(1)}, u32[]{:S(2)}, u32[]{:S(2)}) %all-to-all-start.3) | async-done | bytes 1048608 | tf_op jit(solution)/shard_map/all_to_all | solution.py:348
  134.0 25.4 %all_to_all.30.g_ref = bf16[16,80,128]{2,1,0:T(8,128)(2,1)S(1)} all-to-all(bf16[16,80,128]{2,1,0:T(8,128)(2,1)S(1)} %shard_map.117), channel_id=1, replica_groups=mesh['dp'=32,'ctx'=16] {'ctx'}, dimensions={0} | all-to-all | bytes 655360 | tf_op jit(solution)/shard_map/all_to_all | solution.py:348
  159.4 8.0 %shard_map.118 = bf16[16,208,128]{2,1,0:T(8,128)(2,1)S(1)} custom-call(s32[1,4]{1,0:T(1,128)S(1)} %copy-done.10, bf16[16,192,128]{2,1,0:T(8,128)(2,1)S(1)} %all-to-all-done.1.qkv_ref, bf16[16,80,128]{2,1,0:T(8,128)(2,1)S(1)} %all_to_all.30.g_ref), custom_call_target="tpu_custom_call" | custom-call | flops 1610612736 | bytes 1835008 | tf_op jit(solution)/shard_map/pallas_call | solution.py:466
  167.4 48.7 %all_to_all.31.x_ref = bf16[16,208,128]{2,1,0:T(8,128)(2,1)S(1)} all-to-all(bf16[16,208,128]{2,1,0:T(8,128)(2,1)S(1)} %shard_map.118), channel_id=1, replica_groups=mesh['dp'=32,'ctx'=16] {'ctx'}, dimensions={0} | all-to-all | bytes 1703936 | tf_op jit(solution)/shard_map/all_to_all | solution.py:348
  216.1 1.1 shard_map.119
  (44 shorter events, 8.6 us)
Async XLA Ops:
  0.6 0.7 copy-start.9
  2.0 27.9 %all-to-all-start = ((bf16[16,16,128]{2,1,0:T(8,128)(2,1)}), bf16[16,16,128]{2,1,0:T(8,128)(2,1)S(1)}, u32[]{:S(2)}, u32[]{:S(2)}) async-start(bf16[16,16,128]{2,1,0:T(8,128)(2,1)} %shard_map.110), calls=%async_computation | async-start | bytes 131072 | tf_op jit(solution)/shard_map/all_to_all | solution.py:348
  17.2 1.0 copy-start.4
  18.1 0.9 copy-start.5
  19.1 0.9 copy-start.6
  29.9 42.9 %all-to-all-start.1 = ((bf16[16,192,128]{2,1,0:T(8,128)(2,1)}), bf16[16,192,128]{2,1,0:T(8,128)(2,1)S(1)}, u32[]{:S(2)}, u32[]{:S(2)}) async-start(bf16[16,192,128]{2,1,0:T(8,128)(2,1)} %shard_map.111), calls=%async_computation.1 | async-start | bytes 1572864 | tf_op jit(solution)/shard_map/all_to_all | solution.py:348
  33.5 7.4 %collective-permute-start.2 = (bf16[32,1024]{1,0:T(8,128)(2,1)S(1)}, bf16[32,1024]{1,0:T(8,128)(2,1)S(1)}, u32[]{:S(2)}, u32[]{:S(2)}) collective-permute-start(bf16[32,1024]{1,0:T(8,128)(2,1)S(1)} %bitcast.21), channel_id=1, source_target_pairs={{0,384},{16,400},{32,416},{48,432},{64,448},{80,464},{96,480},{112... | collective-permute-start | bytes 196616 | tf_op jit(solution)/shard_map/ppermute | solution.py:371
  36.3 6.5 %collective-permute-start = (bf16[32,1024]{1,0:T(8,128)(2,1)S(1)}, bf16[32,1024]{1,0:T(8,128)(2,1)S(1)}, u32[]{:S(2)}, u32[]{:S(2)}) collective-permute-start(bf16[32,1024]{1,0:T(8,128)(2,1)S(1)} %bitcast.22), channel_id=1, source_target_pairs={{0,128},{16,144},{32,160},{48,176},{64,192},{80,208},{96,224},{112... | collective-permute-start | bytes 196616 | tf_op jit(solution)/shard_map/ppermute | solution.py:370
  40.9 8.7 %collective-permute-start.3 = (bf16[16,1024]{1,0:T(8,128)(2,1)S(1)}, bf16[16,1024]{1,0:T(8,128)(2,1)S(1)}, u32[]{:S(2)}, u32[]{:S(2)}) collective-permute-start(bf16[16,1024]{1,0:T(8,128)(2,1)S(1)} %slice.17), channel_id=1, source_target_pairs={{0,384},{16,400},{32,416},{48,432},{64,448},{80,464},{96,480},{112... | collective-permute-start | bytes 98312 | tf_op jit(solution)/shard_map/ppermute | solution.py:374
  42.9 6.7 %collective-permute-start.1 = (bf16[16,1024]{1,0:T(8,128)(2,1)S(1)}, bf16[16,1024]{1,0:T(8,128)(2,1)S(1)}, u32[]{:S(2)}, u32[]{:S(2)}) collective-permute-start(bf16[16,1024]{1,0:T(8,128)(2,1)S(1)} %slice.16), channel_id=1, source_target_pairs={{0,128},{16,144},{32,160},{48,176},{64,192},{80,208},{96,224},{112... | collective-permute-start | bytes 98312 | tf_op jit(solution)/shard_map/ppermute | solution.py:373
  49.6 14.5 %copy-start.2 = (bf16[128,1024]{1,0:T(8,128)(2,1)}, bf16[128,1024]{1,0:T(8,128)(2,1)S(1)}, u32[]{:S(2)}) copy-start(bf16[128,1024]{1,0:T(8,128)(2,1)S(1)} %constant_dynamic-update-slice_fusion) | copy-start | bytes 786436
  49.6 8.8 %collective-permute-start.6 = (bf16[4,32,1024]{2,1,0:T(8,128)(2,1)S(1)}, bf16[4,32,1024]{2,1,0:T(8,128)(2,1)S(1)}, u32[]{:S(2)}, u32[]{:S(2)}) collective-permute-start(bf16[4,32,1024]{2,1,0:T(8,128)(2,1)S(1)} %bitcast.15), channel_id=1, source_target_pairs={{0,96},{16,112},{32,0},{48,16},{64,32},{80,48},{96,64},{112,80},{1... | collective-permute-start | bytes 786440 | tf_op jit(solution)/shard_map/ppermute | solution.py:371
  54.5 9.5 %collective-permute-start.4 = (bf16[4,32,1024]{2,1,0:T(8,128)(2,1)S(1)}, bf16[4,32,1024]{2,1,0:T(8,128)(2,1)S(1)}, u32[]{:S(2)}, u32[]{:S(2)}) collective-permute-start(bf16[4,32,1024]{2,1,0:T(8,128)(2,1)S(1)} %bitcast.16), channel_id=1, source_target_pairs={{0,32},{16,48},{32,64},{48,80},{64,96},{80,112},{96,0},{112,16},{1... | collective-permute-start | bytes 786440 | tf_op jit(solution)/shard_map/ppermute | solution.py:370
  58.4 14.4 %copy-start.10 = (s32[1,4]{1,0:T(1,128)S(1)}, s32[1,4]{1,0:T(1,128)}, u32[]{:S(2)}) copy-start(s32[1,4]{1,0:T(1,128)} %len_ref.5) | copy-start | bytes 52
  58.4 8.1 %collective-permute-start.7 = (bf16[2,32,1024]{2,1,0:T(8,128)(2,1)S(1)}, bf16[2,32,1024]{2,1,0:T(8,128)(2,1)S(1)}, u32[]{:S(2)}, u32[]{:S(2)}) collective-permute-start(bf16[2,32,1024]{2,1,0:T(8,128)(2,1)S(1)} %slice.19), channel_id=1, source_target_pairs={{0,96},{16,112},{32,0},{48,16},{64,32},{80,48},{96,64},{112,80},{1... | collective-permute-start | bytes 393224 | tf_op jit(solution)/shard_map/ppermute | solution.py:374
  64.1 8.1 %collective-permute-start.5 = (bf16[2,32,1024]{2,1,0:T(8,128)(2,1)S(1)}, bf16[2,32,1024]{2,1,0:T(8,128)(2,1)S(1)}, u32[]{:S(2)}, u32[]{:S(2)}) collective-permute-start(bf16[2,32,1024]{2,1,0:T(8,128)(2,1)S(1)} %slice.18), channel_id=1, source_target_pairs={{0,32},{16,48},{32,64},{48,80},{64,96},{80,112},{96,0},{112,16},{1... | collective-permute-start | bytes 393224 | tf_op jit(solution)/shard_map/ppermute | solution.py:373
  72.2 0.7 copy-start.7
  79.5 12.1 %copy-start.1 = (bf16[128,1024]{1,0:T(8,128)(2,1)S(1)}, bf16[128,1024]{1,0:T(8,128)(2,1)}, u32[]{:S(2)}) copy-start(bf16[128,1024]{1,0:T(8,128)(2,1)} %out_grad_ref.3) | copy-start | bytes 786436
  79.5 25.9 %copy-start = (bf16[128,1024]{1,0:T(8,128)(2,1)S(1)}, bf16[128,1024]{1,0:T(8,128)(2,1)}, u32[]{:S(2)}) copy-start(bf16[128,1024]{1,0:T(8,128)(2,1)} %gate_ref.3) | copy-start | bytes 786436
  79.5 25.9 %all-to-all-start.2 = ((bf16[16,64,128]{2,1,0:T(8,128)(2,1)}), bf16[16,64,128]{2,1,0:T(8,128)(2,1)S(1)}, u32[]{:S(2)}, u32[]{:S(2)}) async-start(bf16[16,64,128]{2,1,0:T(8,128)(2,1)} %shard_map.112), calls=%async_computation.2 | async-start | bytes 524288 | tf_op jit(solution)/shard_map/all_to_all | solution.py:348
  91.6 16.6 %collective-permute-start.9 = (bf16[128,1024]{1,0:T(8,128)(2,1)S(1)}, bf16[128,1024]{1,0:T(8,128)(2,1)S(1)}, u32[]{:S(2)}, u32[]{:S(2)}) collective-permute-start(bf16[128,1024]{1,0:T(8,128)(2,1)S(1)} %copy-done.1), channel_id=1, source_target_pairs={{0,16},{16,0},{32,48},{48,32},{64,80},{80,64},{96,112},{112,96},{1... | collective-permute-start | bytes 786440 | tf_op jit(solution)/shard_map/ppermute | solution.py:416
  106.3 3.2 %collective-permute-start.8 = (bf16[16,32,128]{2,1,0:T(8,128)(2,1)S(1)}, bf16[16,32,128]{2,1,0:T(8,128)(2,1)S(1)}, u32[]{:S(2)}, u32[]{:S(2)}) collective-permute-start(bf16[16,32,128]{2,1,0:T(8,128)(2,1)S(1)} %get-tuple-element.27), channel_id=1, source_target_pairs={{0,16},{16,0},{32,48},{48,32},{64,80},{80,64},{96,112},{112,96},{1... | collective-permute-start | bytes 393224 | tf_op jit(solution)/shard_map/ppermute | solution.py:442
  110.9 22.8 %all-to-all-start.3 = ((bf16[16,32,1024]{2,1,0:T(8,128)(2,1)}), bf16[16,32,1024]{2,1,0:T(8,128)(2,1)S(1)}, u32[]{:S(2)}, u32[]{:S(2)}) async-start(bf16[16,32,1024]{2,1,0:T(8,128)(2,1)} %shard_map.114), calls=%async_computation.3 | async-start | bytes 2097152 | tf_op jit(solution)/shard_map/all_to_all | solution.py:348
  117.7 0.9 copy-start.3
  118.7 0.9 copy-start.8
  121.1 3.4 %collective-permute-start.10 = (f32[16,32,128]{2,1,0:T(8,128)S(1)}, f32[16,32,128]{2,1,0:T(8,128)S(1)}, u32[]{:S(2)}, u32[]{:S(2)}) collective-permute-start(f32[16,32,128]{2,1,0:T(8,128)S(1)} %get-tuple-element.34), channel_id=1, source_target_pairs={{0,16},{16,0},{32,48},{48,32},{64,80},{80,64},{96,112},{112,96},{1... | collective-permute-start | bytes 786440 | tf_op jit(solution)/shard_map/ppermute | solution.py:424

commit v4 on v3

--- a/solution.py
+++ b/solution.py
@@ -142,88 +142,115 @@
     return gate, (half + half) * gate
 
 
+def row_pair(ref, pair, rows):
+    return [lane_pair(ref, 2 * pair + i, rows) for i in range(2)]
+
+
 def forward_kernel(len_ref, qkv_ref, out_ref, k_nat, attn_ref):
     ends = user_edges(len_ref)
     natural(qkv_ref, K_ROWS, k_nat)
-    for row_block in range(k_nat.shape[0]):
-        q_t = lane_pair(qkv_ref, row_block, Q_ROWS)
-        positions, starts = block_rows(row_block, ends)
-        first = first_block(row_block, ends)
-
-        def score(col, diagonal, q_t=q_t, positions=positions, starts=starts):
-            raw = jnp.dot(k_nat[col], q_t, preferred_element_type=F32)
+    for pair in range(k_nat.shape[0] // 2):
+        low, high = 2 * pair, 2 * pair + 1
+        q_t = row_pair(qkv_ref, pair, Q_ROWS)
+        places = [block_rows(row, ends) for row in (low, high)]
+        first = first_block(low, ends)
+
+        def score(i, col, diagonal, q_t=q_t, places=places):
+            raw = jnp.dot(k_nat[col], q_t[i], preferred_element_type=F32)
             _, silu = gate_and_silu(raw)
+            positions, starts = places[i]
             allowed = tile_allowed(diagonal, col, starts, positions)
             return jnp.where(allowed, silu, 0.0).astype(BF16)
 
         def product(col, attn):
             return jnp.dot(lane_pair(qkv_ref, col, V_ROWS), attn, preferred_element_type=F32)
 
-        def step(i, total, row_block=row_block, score=score):
-            col = row_block - 1 - i
-            before = attn_ref[...]
-            attn = score(col, False)
-            total = total + product(col + 1, before)
-            attn_ref[...] = attn
-            return total
-
-        attn_ref[...] = score(row_block, True)
-        total = lax.fori_loop(0, row_block - first, step, jnp.zeros((DH, TILE), F32))
-        total = total + product(first, attn_ref[...])
-        total = total * user_inverse(positions, ends, len_ref)
-        out_ref[2 * row_block] = total[:, :LANES].astype(BF16)
-        out_ref[2 * row_block + 1] = total[:, LANES:].astype(BF16)
-
-
-def backward_kernel(len_ref, qkv_ref, g_ref, out_ref, k_nat, v_nat, k_acc, v_acc, attn_ref, slope_ref):
-    blocks = k_nat.shape[0]
+        def step(i, totals, low=low, score=score):
+            col = low - 1 - i
+            before = attn_ref[0], attn_ref[1]
+            attn_low = score(0, col, False)
+            total_low = totals[0] + product(col + 1, before[0])
+            attn_high = score(1, col, False)
+            total_high = totals[1] + product(col + 1, before[1])
+            attn_ref[0] = attn_low
+            attn_ref[1] = attn_high
+            return total_low, total_high
+
+        diagonal = score(1, high, True)
+        attn_ref[0] = score(0, low, True)
+        totals = jnp.zeros((DH, TILE), F32), product(high, diagonal)
+        attn_ref[1] = score(1, low, False)
+        totals = lax.fori_loop(0, low - first, step, totals)
+        for i, row in enumerate((low, high)):
+            total = totals[i] + product(first, attn_ref[i])
+            total = total * user_inverse(places[i][0], ends, len_ref)
+            out_ref[2 * row] = total[:, :LANES].astype(BF16)
+            out_ref[2 * row + 1] = total[:, LANES:].astype(BF16)
+
+
+def backward_kernel(
+    len_ref, qkv_ref, g_ref, out_ref, k_nat, v_nat, k_acc, v_acc, attn_ref, grad_ref
+):
+    blocks = v_nat.shape[0]
     scale = 1.0 / math.sqrt(DH)
     ends = user_edges(len_ref)
     natural(qkv_ref, K_ROWS, k_nat)
     natural(qkv_ref, V_ROWS, v_nat)
     k_acc[...] = jnp.zeros_like(k_acc)
     v_acc[...] = jnp.zeros_like(v_acc)
-    for row_block in range(blocks):
-        q_t = lane_pair(qkv_ref, row_block, Q_ROWS)
-        g_t = lane_pair(g_ref, row_block, slice(0, DH))
-        positions, starts = block_rows(row_block, ends)
-        first = first_block(row_block, ends)
-
-        def score(col, diagonal, q_t=q_t, g_t=g_t, positions=positions, starts=starts):
-            raw = jnp.dot(k_nat[col], q_t, preferred_element_type=F32)
-            attn_grad = jnp.dot(v_nat[col], g_t, preferred_element_type=F32)
+    for pair in range(blocks // 2):
+        low, high = 2 * pair, 2 * pair + 1
+        q_t = row_pair(qkv_ref, pair, Q_ROWS)
+        g_t = row_pair(g_ref, pair, slice(0, DH))
+        places = [block_rows(row, ends) for row in (low, high)]
+        first = first_block(low, ends)
+
+        def score(i, col, diagonal, q_t=q_t, g_t=g_t, places=places):
+            raw = jnp.dot(k_nat[col], q_t[i], preferred_element_type=F32)
+            attn_grad = jnp.dot(v_nat[col], g_t[i], preferred_element_type=F32)
             gate, silu = gate_and_silu(raw)
             score_grad = attn_grad * (gate + silu * (1.0 - gate))
+            positions, starts = places[i]
             allowed = tile_allowed(diagonal, col, starts, positions)
             return (
                 jnp.where(allowed, silu, 0.0).astype(BF16),
                 jnp.where(allowed, score_grad, 0.0).astype(BF16),
             )
 
-        def product(col, attn, score_grad, q_t=q_t, g_t=g_t):
-            v_acc[col] += lax.dot_general(g_t, attn, CONTRACT_LANES, preferred_element_type=F32)
+        def product(i, col, attn, score_grad, q_t=q_t, g_t=g_t):
+            v_acc[col] += lax.dot_general(g_t[i], attn, CONTRACT_LANES, preferred_element_type=F32)
             k_acc[col] += lax.dot_general(
-                q_t, score_grad, CONTRACT_LANES, preferred_element_type=F32
+                q_t[i], score_grad, CONTRACT_LANES, preferred_element_type=F32
             )
             return jnp.dot(lane_pair(qkv_ref, col, K_ROWS), score_grad, preferred_element_type=F32)
 
-        def step(i, total, row_block=row_block, score=score, product=product):
-            col = row_block - 1 - i
-            before = attn_ref[...], slope_ref[...]
-            attn, score_grad = score(col, False)
-            total = total + product(col + 1, *before)
-            attn_ref[...] = attn
-            slope_ref[...] = score_grad
-            return total
-
-        attn, score_grad = score(row_block, True)
-        attn_ref[...] = attn
-        slope_ref[...] = score_grad
-        total = lax.fori_loop(0, row_block - first, step, jnp.zeros((DH, TILE), F32))
-        total = total + product(first, attn_ref[...], slope_ref[...])
-        total = (total * scale).astype(BF16)
-        out_ref[2 * row_block, 0:DH, :] = total[:, :LANES]
-        out_ref[2 * row_block + 1, 0:DH, :] = total[:, LANES:]
+        def keep(i, tile):
+            attn_ref[i], grad_ref[i] = tile
+
+        def kept(i):
+            return attn_ref[i], grad_ref[i]
+
+        def step(i, totals, low=low, score=score, product=product):
+            col = low - 1 - i
+            before = kept(0), kept(1)
+            tile_low = score(0, col, False)
+            total_low = totals[0] + product(0, col + 1, *before[0])
+            tile_high = score(1, col, False)
+            total_high = totals[1] + product(1, col + 1, *before[1])
+            keep(0, tile_low)
+            keep(1, tile_high)
+            return total_low, total_high
+
+        diagonal = score(1, high, True)
+        keep(0, score(0, low, True))
+        totals = jnp.zeros((DH, TILE), F32), product(1, high, *diagonal)
+        keep(1, score(1, low, False))
+        totals = lax.fori_loop(0, low - first, step, totals)
+        for i, row in enumerate((low, high)):
+            total = totals[i] + product(i, first, *kept(i))
+            total = (total * scale).astype(BF16)
+            out_ref[2 * row, 0:DH, :] = total[:, :LANES]
+            out_ref[2 * row + 1, 0:DH, :] = total[:, LANES:]
     total = jnp.sum(g_ref[:, DH:, :].astype(F32), axis=0).astype(BF16)
     for chunk in range(out_ref.shape[0]):
         out_ref[chunk, 3 * DH :, :] = total
@@ -365,14 +392,20 @@
     return moves
 
 
+def ring_near(block, axis):
+    return tuple(lax.ppermute(block, "dp", plane_shift(axis, step)) for step in (1, -1))
+
+
+def ring_far(back_one, back_three, axis):
+    half = back_one.shape[0] // 2
+    low = lax.ppermute(back_one[:half], "dp", plane_shift(axis, 1))
+    high = lax.ppermute(back_three[half:], "dp", plane_shift(axis, -1))
+    return low, high
+
+
 def ring_blocks(block, axis):
-    up, down = plane_shift(axis, 1), plane_shift(axis, -1)
-    back_one = lax.ppermute(block, "dp", up)
-    back_three = lax.ppermute(block, "dp", down)
-    half = block.shape[0] // 2
-    low = lax.ppermute(back_one[:half], "dp", up)
-    high = lax.ppermute(back_three[half:], "dp", down)
-    return block, back_one, low, high, back_three
+    back_one, back_three = ring_near(block, axis)
+    return (block, back_one) + ring_far(back_one, back_three, axis) + (back_three,)
 
 
 def local(query_rows, key_rows, value_rows, gate_rows, out_grad, proj_weight, user_lengths):
@@ -411,27 +444,30 @@
     block = block.reshape(ctx, width // LANES, out_rows // ctx, LANES).transpose(0, 2, 1, 3)
     block = block.reshape(out_rows, width)
     column = jnp.concatenate(ring_blocks(block, "x"), axis=0).reshape(SIDE, out_rows, width)
-    weights = ring_blocks(column, "y")
-    qkv, weights = lax.optimization_barrier((qkv, weights))
-    other_grad = lax.ppermute(out_grad, "dp", partner)
+    column, own_grad = lax.optimization_barrier((column, out_grad))
+    near = ring_near(column, "y")
+    other_grad = lax.ppermute(own_grad, "dp", partner)
+    qkv, near, other_grad = lax.optimization_barrier((qkv, near, other_grad))
+    far = ring_far(*near, "y")
+    attn_out = call(
+        forward_kernel,
+        shape((ctx, DH, tokens), BF16),
+        [SMEM, VMEM],
+        [pltpu.VMEM((blocks, TILE, DH), BF16), pltpu.VMEM((2, TILE, TILE), BF16)],
+        flops=group * group * DH * 2,
+        nbytes=5 * group * DH * 2,
+    )(user_lengths, qkv)
+    attn_out = exchange(attn_out, "ctx")
+    attn_out, far = lax.optimization_barrier((attn_out, far))
+
     mine, theirs = call(
         project_kernel,
         [shape((heads, DH // 2, tokens), F32)] * 2,
         [SMEM] + [VMEM] * 7,
         flops=2 * tokens * width * width,
         nbytes=2 * width * width,
-    )(place, *weights, out_grad, other_grad)
+    )(place, column, near[0], *far, near[1], out_grad, other_grad)
     received = lax.ppermute(theirs, "dp", partner)
-
-    attn_out = call(
-        forward_kernel,
-        shape((ctx, DH, tokens), BF16),
-        [SMEM, VMEM],
-        [pltpu.VMEM((blocks, TILE, DH), BF16), pltpu.VMEM((TILE, TILE), BF16)],
-        flops=group * group * DH * 2,
-        nbytes=5 * group * DH * 2,
-    )(user_lengths, qkv)
-    attn_out = exchange(attn_out, "ctx")
 
     gated_mine, gated_other = call(
         gated_kernel,
@@ -472,8 +508,8 @@
             pltpu.VMEM((blocks, TILE, DH), BF16),
             pltpu.VMEM((blocks, DH, TILE), F32),
             pltpu.VMEM((blocks, DH, TILE), F32),
-            pltpu.VMEM((TILE, TILE), BF16),
-            pltpu.VMEM((TILE, TILE), BF16),
+            pltpu.VMEM((2, TILE, TILE), BF16),
+            pltpu.VMEM((2, TILE, TILE), BF16),
         ],
         flops=3 * group * group * DH * 2,
         nbytes=7 * group * DH * 2,

time: 219 us -> 215 us (0.982)
  starting transfers between devices: 71.9 us -> 67.8 us
  waiting for transfers between devices: 40.5 us -> 44.4 us
  Pallas kernels: 23.6 us -> 20.4 us
    ppermute x9, waiting for transfers between devices: 9.94 us -> 16.4 us  [the longest x4 9.17 us: ring_near(): lax.ppermute(block, 'dp', plane_shift(axis, step))]
    all_to_all x4, waiting for transfers between devices: 27.8 us -> 25.2 us  [exchange(): lax.all_to_all(array, axis, split_axis=0, concat_axis=0, tiled=True, axis...]
    all_to_all x4, starting transfers between devices: 37.7 us -> 35.1 us  [exchange(): lax.all_to_all(array, axis, split_axis=0, concat_axis=0, tiled=True, axis...]
  transfers between devices with their start and end apart: 15 -> 15, of which waited for: 10 -> 12; matrix products, arithmetic and copies ran while one was open for 0% -> 0% of each run, Pallas kernels for 3% -> 2%
where the time goes in v4:
time: 215 us; the launch traced here: 213 us
  blocking collectives  73.1 us (34%)
  starting transfers between devices  67.8 us (32%)
  waiting for transfers between devices  44.4 us (21%)
  Pallas kernels  20.4 us (9%)
  local copies, waits for them, and re-layouts  6.17 us (3%)
    all_to_all x2, blocking collectives, exchange(): lax.all_to_all(array, axis, split_axis=0, concat_axis=0, tiled=True, axis...  73.1 us
    all_to_all x4, starting transfers between devices, exchange(): lax.all_to_all(array, axis, split_axis=0, concat_axis=0, tiled=True, axis...  35.1 us
    all_to_all x4, waiting for transfers between devices, exchange(): lax.all_to_all(array, axis, split_axis=0, concat_axis=0, tiled=True, axis...  25.2 us
    ppermute x4, starting transfers between devices, ring_near(): lax.ppermute(block, 'dp', plane_shift(axis, step))  13.9 us
    ppermute x4, waiting for transfers between devices, ring_near(): lax.ppermute(block, 'dp', plane_shift(axis, step))  9.17 us
    ppermute x2, starting transfers between devices, ring_far(): low = lax.ppermute(back_one[:half], 'dp', plane_shift(axis, 1))  7.46 us
    pallas_call x1, Pallas kernels, local(): call(backward_kernel, shape((ctx, 3 * DH + w_rows, tokens), BF16), [SMEM,...  6.48 us
    ppermute x2, waiting for transfers between devices, ring_far(): low = lax.ppermute(back_one[:half], 'dp', plane_shift(axis, 1))  6.3 us
  transfers between devices with their start and end apart: 15, of which 12 were waited for; matrix products, arithmetic and copies ran while one was open for 0% of the time, Pallas kernels for 2%

profile of v4, /device:TPU:6, one launch (start us, length us, event | category | flops | bytes accessed | tf_op | source)
XLA Modules:
  0.0 212.9 jit_solution(16628836040496180108)
XLA Ops:
  2.0 15.2 %all-to-all-start = ((bf16[16,16,128]{2,1,0:T(8,128)(2,1)}), bf16[16,16,128]{2,1,0:T(8,128)(2,1)S(1)}, u32[]{:S(2)}, u32[]{:S(2)}) async-start(bf16[16,16,128]{2,1,0:T(8,128)(2,1)} %shard_map.110), calls=%async_computation | async-start | bytes 131072 | tf_op jit(solution)/shard_map/all_to_all | solution.py:375
  20.0 1.4 shard_map.111
  21.4 8.5 %all-to-all-done = bf16[16,16,128]{2,1,0:T(8,128)(2,1)S(1)} async-done(((bf16[16,16,128]{2,1,0:T(8,128)(2,1)}), bf16[16,16,128]{2,1,0:T(8,128)(2,1)S(1)}, u32[]{:S(2)}, u32[]{:S(2)}) %all-to-all-start) | async-done | bytes 65568 | tf_op jit(solution)/shard_map/all_to_all | solution.py:375
  29.9 3.6 %all-to-all-start.1 = ((bf16[16,192,128]{2,1,0:T(8,128)(2,1)}), bf16[16,192,128]{2,1,0:T(8,128)(2,1)S(1)}, u32[]{:S(2)}, u32[]{:S(2)}) async-start(bf16[16,192,128]{2,1,0:T(8,128)(2,1)} %shard_map.111), calls=%async_computation.1 | async-start | bytes 1572864 | tf_op jit(solution)/shard_map/all_to_all | solution.py:375
  33.5 2.7 %collective-permute-start.2 = (bf16[32,1024]{1,0:T(8,128)(2,1)S(1)}, bf16[32,1024]{1,0:T(8,128)(2,1)S(1)}, u32[]{:S(2)}, u32[]{:S(2)}) collective-permute-start(bf16[32,1024]{1,0:T(8,128)(2,1)S(1)} %bitcast.21), channel_id=1, source_target_pairs={{0,384},{16,400},{32,416},{48,432},{64,448},{80,464},{96,480},{112... | collective-permute-start | bytes 196616 | tf_op jit(solution)/shard_map/ppermute | solution.py:396
  36.3 4.3 %collective-permute-start = (bf16[32,1024]{1,0:T(8,128)(2,1)S(1)}, bf16[32,1024]{1,0:T(8,128)(2,1)S(1)}, u32[]{:S(2)}, u32[]{:S(2)}) collective-permute-start(bf16[32,1024]{1,0:T(8,128)(2,1)S(1)} %bitcast.22), channel_id=1, source_target_pairs={{0,128},{16,144},{32,160},{48,176},{64,192},{80,208},{96,224},{112... | collective-permute-start | bytes 196616 | tf_op jit(solution)/shard_map/ppermute | solution.py:396
  40.9 1.9 collective-permute-start.3
  42.9 5.1 %collective-permute-start.1 = (bf16[16,1024]{1,0:T(8,128)(2,1)S(1)}, bf16[16,1024]{1,0:T(8,128)(2,1)S(1)}, u32[]{:S(2)}, u32[]{:S(2)}) collective-permute-start(bf16[16,1024]{1,0:T(8,128)(2,1)S(1)} %slice.16), channel_id=1, source_target_pairs={{0,128},{16,144},{32,160},{48,176},{64,192},{80,208},{96,224},{112... | collective-permute-start | bytes 98312 | tf_op jit(solution)/shard_map/ppermute | solution.py:401
  48.0 1.6 collective-permute-done.1
  49.6 1.9 collective-permute-start.6
  51.6 4.9 %collective-permute-start.5 = (bf16[4,32,1024]{2,1,0:T(8,128)(2,1)S(1)}, bf16[4,32,1024]{2,1,0:T(8,128)(2,1)S(1)}, u32[]{:S(2)}, u32[]{:S(2)}) collective-permute-start(bf16[4,32,1024]{2,1,0:T(8,128)(2,1)S(1)} %bitcast.15), channel_id=1, source_target_pairs={{0,96},{16,112},{32,0},{48,16},{64,32},{80,48},{96,64},{112,80},{1... | collective-permute-start | bytes 786440 | tf_op jit(solution)/shard_map/ppermute | solution.py:396
  56.5 1.9 collective-permute-start.4
  59.1 3.6 %collective-permute-done.5.w3_ref = bf16[4,32,1024]{2,1,0:T(8,128)(2,1)S(1)} collective-permute-done((bf16[4,32,1024]{2,1,0:T(8,128)(2,1)S(1)}, bf16[4,32,1024]{2,1,0:T(8,128)(2,1)S(1)}, u32[]{:S(2)}, u32[]{:S(2)}) %collective-permute-start.5) | collective-permute-done | bytes 262176 | tf_op jit(solution)/shard_map/ppermute | solution.py:396
  62.7 5.3 %collective-permute-done.4.w1_ref = bf16[4,32,1024]{2,1,0:T(8,128)(2,1)S(1)} collective-permute-done((bf16[4,32,1024]{2,1,0:T(8,128)(2,1)S(1)}, bf16[4,32,1024]{2,1,0:T(8,128)(2,1)S(1)}, u32[]{:S(2)}, u32[]{:S(2)}) %collective-permute-start.4) | collective-permute-done | bytes 262176 | tf_op jit(solution)/shard_map/ppermute | solution.py:396
  68.0 3.8 %all-to-all-done.1.qkv_ref = bf16[16,192,128]{2,1,0:T(8,128)(2,1)S(1)} async-done(((bf16[16,192,128]{2,1,0:T(8,128)(2,1)}), bf16[16,192,128]{2,1,0:T(8,128)(2,1)S(1)}, u32[]{:S(2)}, u32[]{:S(2)}) %all-to-all-start.1) | async-done | bytes 786464 | tf_op jit(solution)/shard_map/all_to_all | solution.py:375
  71.8 5.1 %shard_map.112 = bf16[16,64,128]{2,1,0:T(8,128)(2,1)} custom-call(s32[1,4]{1,0:T(1,128)S(1)} %copy-done.10, bf16[16,192,128]{2,1,0:T(8,128)(2,1)S(1)} %all-to-all-done.1.qkv_ref), custom_call_target="tpu_custom_call" | custom-call | flops 536870912 | bytes 1310720 | tf_op jit(solution)/shard_map/pallas_call | solution.py:452
  76.9 8.2 %all-to-all-start.2 = ((bf16[16,64,128]{2,1,0:T(8,128)(2,1)}), bf16[16,64,128]{2,1,0:T(8,128)(2,1)S(1)}, u32[]{:S(2)}, u32[]{:S(2)}) async-start(bf16[16,64,128]{2,1,0:T(8,128)(2,1)} %shard_map.112), calls=%async_computation.2 | async-start | bytes 524288 | tf_op jit(solution)/shard_map/all_to_all | solution.py:375
  85.2 3.6 %collective-permute-start.8 = (bf16[2,32,1024]{2,1,0:T(8,128)(2,1)S(1)}, bf16[2,32,1024]{2,1,0:T(8,128)(2,1)S(1)}, u32[]{:S(2)}, u32[]{:S(2)}) collective-permute-start(bf16[2,32,1024]{2,1,0:T(8,128)(2,1)S(1)} %slice.15), channel_id=1, source_target_pairs={{0,96},{16,112},{32,0},{48,16},{64,32},{80,48},{96,64},{112,80},{1... | collective-permute-start | bytes 393224 | tf_op jit(solution)/shard_map/ppermute | solution.py:402
  88.8 2.3 %collective-permute-start.7 = (bf16[2,32,1024]{2,1,0:T(8,128)(2,1)S(1)}, bf16[2,32,1024]{2,1,0:T(8,128)(2,1)S(1)}, u32[]{:S(2)}, u32[]{:S(2)}) collective-permute-start(bf16[2,32,1024]{2,1,0:T(8,128)(2,1)S(1)} %slice.14), channel_id=1, source_target_pairs={{0,32},{16,48},{32,64},{48,80},{64,96},{80,112},{96,0},{112,16},{1... | collective-permute-start | bytes 393224 | tf_op jit(solution)/shard_map/ppermute | solution.py:401
  92.2 4.7 %collective-permute-done.7.w2_low_ref = bf16[2,32,1024]{2,1,0:T(8,128)(2,1)S(1)} collective-permute-done((bf16[2,32,1024]{2,1,0:T(8,128)(2,1)S(1)}, bf16[2,32,1024]{2,1,0:T(8,128)(2,1)S(1)}, u32[]{:S(2)}, u32[]{:S(2)}) %collective-permute-start.7) | collective-permute-done | bytes 131104 | tf_op jit(solution)/shard_map/ppermute | solution.py:401
  96.9 5.8 %all-to-all-done.2.o_ref = bf16[16,64,128]{2,1,0:T(8,128)(2,1)S(1)} async-done(((bf16[16,64,128]{2,1,0:T(8,128)(2,1)}), bf16[16,64,128]{2,1,0:T(8,128)(2,1)S(1)}, u32[]{:S(2)}, u32[]{:S(2)}) %all-to-all-start.2) | async-done | bytes 262176 | tf_op jit(solution)/shard_map/all_to_all | solution.py:375
  103.5 1.9 collective-permute-start.9
  106.8 1.4 shard_map.114
  108.2 8.1 %all-to-all-start.3 = ((bf16[16,32,1024]{2,1,0:T(8,128)(2,1)}), bf16[16,32,1024]{2,1,0:T(8,128)(2,1)S(1)}, u32[]{:S(2)}, u32[]{:S(2)}) async-start(bf16[16,32,1024]{2,1,0:T(8,128)(2,1)} %shard_map.114), calls=%async_computation.3 | async-start | bytes 2097152 | tf_op jit(solution)/shard_map/all_to_all | solution.py:375
  118.2 1.5 shard_map.115
  119.6 1.9 collective-permute-start.10
  121.6 1.5 collective-permute-done.10.recv_ref
  123.1 1.8 shard_map.116
  124.9 7.1 %all-to-all-done.3.x_ref = bf16[16,32,1024]{2,1,0:T(8,128)(2,1)S(1)} async-done(((bf16[16,32,1024]{2,1,0:T(8,128)(2,1)}), bf16[16,32,1024]{2,1,0:T(8,128)(2,1)S(1)}, u32[]{:S(2)}, u32[]{:S(2)}) %all-to-all-start.3) | async-done | bytes 1048608 | tf_op jit(solution)/shard_map/all_to_all | solution.py:375
  132.2 25.2 %all_to_all.30.g_ref = bf16[16,80,128]{2,1,0:T(8,128)(2,1)S(1)} all-to-all(bf16[16,80,128]{2,1,0:T(8,128)(2,1)S(1)} %shard_map.117), channel_id=1, replica_groups=mesh['dp'=32,'ctx'=16] {'ctx'}, dimensions={0} | all-to-all | bytes 655360 | tf_op jit(solution)/shard_map/all_to_all | solution.py:375
  157.4 6.5 %shard_map.118 = bf16[16,208,128]{2,1,0:T(8,128)(2,1)S(1)} custom-call(s32[1,4]{1,0:T(1,128)S(1)} %copy-done.10, bf16[16,192,128]{2,1,0:T(8,128)(2,1)S(1)} %all-to-all-done.1.qkv_ref, bf16[16,80,128]{2,1,0:T(8,128)(2,1)S(1)} %all_to_all.30.g_ref), custom_call_target="tpu_custom_call" | custom-call | flops 1610612736 | bytes 1835008 | tf_op jit(solution)/shard_map/pallas_call | solution.py:502
  163.9 47.9 %all_to_all.31.x_ref = bf16[16,208,128]{2,1,0:T(8,128)(2,1)S(1)} all-to-all(bf16[16,208,128]{2,1,0:T(8,128)(2,1)S(1)} %shard_map.118), channel_id=1, replica_groups=mesh['dp'=32,'ctx'=16] {'ctx'}, dimensions={0} | all-to-all | bytes 1703936 | tf_op jit(solution)/shard_map/all_to_all | solution.py:375
  (44 shorter events, 11.5 us)
Async XLA Ops:
  0.6 0.7 copy-start.9
  2.0 27.9 %all-to-all-start = ((bf16[16,16,128]{2,1,0:T(8,128)(2,1)}), bf16[16,16,128]{2,1,0:T(8,128)(2,1)S(1)}, u32[]{:S(2)}, u32[]{:S(2)}) async-start(bf16[16,16,128]{2,1,0:T(8,128)(2,1)} %shard_map.110), calls=%async_computation | async-start | bytes 131072 | tf_op jit(solution)/shard_map/all_to_all | solution.py:375
  17.2 1.0 copy-start.4
  18.1 0.9 copy-start.5
  19.1 0.9 copy-start.6
  29.9 41.9 %all-to-all-start.1 = ((bf16[16,192,128]{2,1,0:T(8,128)(2,1)}), bf16[16,192,128]{2,1,0:T(8,128)(2,1)S(1)}, u32[]{:S(2)}, u32[]{:S(2)}) async-start(bf16[16,192,128]{2,1,0:T(8,128)(2,1)} %shard_map.111), calls=%async_computation.1 | async-start | bytes 1572864 | tf_op jit(solution)/shard_map/all_to_all | solution.py:375
  33.5 7.4 %collective-permute-start.2 = (bf16[32,1024]{1,0:T(8,128)(2,1)S(1)}, bf16[32,1024]{1,0:T(8,128)(2,1)S(1)}, u32[]{:S(2)}, u32[]{:S(2)}) collective-permute-start(bf16[32,1024]{1,0:T(8,128)(2,1)S(1)} %bitcast.21), channel_id=1, source_target_pairs={{0,384},{16,400},{32,416},{48,432},{64,448},{80,464},{96,480},{112... | collective-permute-start | bytes 196616 | tf_op jit(solution)/shard_map/ppermute | solution.py:396
  36.3 6.5 %collective-permute-start = (bf16[32,1024]{1,0:T(8,128)(2,1)S(1)}, bf16[32,1024]{1,0:T(8,128)(2,1)S(1)}, u32[]{:S(2)}, u32[]{:S(2)}) collective-permute-start(bf16[32,1024]{1,0:T(8,128)(2,1)S(1)} %bitcast.22), channel_id=1, source_target_pairs={{0,128},{16,144},{32,160},{48,176},{64,192},{80,208},{96,224},{112... | collective-permute-start | bytes 196616 | tf_op jit(solution)/shard_map/ppermute | solution.py:396
  40.6 9.0 %copy-start.1 = (bf16[128,1024]{1,0:T(8,128)(2,1)S(1)}, bf16[128,1024]{1,0:T(8,128)(2,1)}, u32[]{:S(2)}) copy-start(bf16[128,1024]{1,0:T(8,128)(2,1)} %out_grad_ref.3) | copy-start | bytes 786436
  40.9 8.7 %collective-permute-start.3 = (bf16[16,1024]{1,0:T(8,128)(2,1)S(1)}, bf16[16,1024]{1,0:T(8,128)(2,1)S(1)}, u32[]{:S(2)}, u32[]{:S(2)}) collective-permute-start(bf16[16,1024]{1,0:T(8,128)(2,1)S(1)} %slice.17), channel_id=1, source_target_pairs={{0,384},{16,400},{32,416},{48,432},{64,448},{80,464},{96,480},{112... | collective-permute-start | bytes 98312 | tf_op jit(solution)/shard_map/ppermute | solution.py:402
  42.9 6.7 %collective-permute-start.1 = (bf16[16,1024]{1,0:T(8,128)(2,1)S(1)}, bf16[16,1024]{1,0:T(8,128)(2,1)S(1)}, u32[]{:S(2)}, u32[]{:S(2)}) collective-permute-start(bf16[16,1024]{1,0:T(8,128)(2,1)S(1)} %slice.16), channel_id=1, source_target_pairs={{0,128},{16,144},{32,160},{48,176},{64,192},{80,208},{96,224},{112... | collective-permute-start | bytes 98312 | tf_op jit(solution)/shard_map/ppermute | solution.py:401
  49.6 22.2 %copy-start.10 = (s32[1,4]{1,0:T(1,128)S(1)}, s32[1,4]{1,0:T(1,128)}, u32[]{:S(2)}) copy-start(s32[1,4]{1,0:T(1,128)} %len_ref.5) | copy-start | bytes 52
  49.6 9.5 %collective-permute-start.6 = (bf16[128,1024]{1,0:T(8,128)(2,1)S(1)}, bf16[128,1024]{1,0:T(8,128)(2,1)S(1)}, u32[]{:S(2)}, u32[]{:S(2)}) collective-permute-start(bf16[128,1024]{1,0:T(8,128)(2,1)S(1)} %copy-done.1), channel_id=1, source_target_pairs={{0,16},{16,0},{32,48},{48,32},{64,80},{80,64},{96,112},{112,96},{1... | collective-permute-start | bytes 786440 | tf_op jit(solution)/shard_map/ppermute | solution.py:449
  51.6 11.1 %collective-permute-start.5 = (bf16[4,32,1024]{2,1,0:T(8,128)(2,1)S(1)}, bf16[4,32,1024]{2,1,0:T(8,128)(2,1)S(1)}, u32[]{:S(2)}, u32[]{:S(2)}) collective-permute-start(bf16[4,32,1024]{2,1,0:T(8,128)(2,1)S(1)} %bitcast.15), channel_id=1, source_target_pairs={{0,96},{16,112},{32,0},{48,16},{64,32},{80,48},{96,64},{112,80},{1... | collective-permute-start | bytes 786440 | tf_op jit(solution)/shard_map/ppermute | solution.py:396
  56.5 11.5 %collective-permute-start.4 = (bf16[4,32,1024]{2,1,0:T(8,128)(2,1)S(1)}, bf16[4,32,1024]{2,1,0:T(8,128)(2,1)S(1)}, u32[]{:S(2)}, u32[]{:S(2)}) collective-permute-start(bf16[4,32,1024]{2,1,0:T(8,128)(2,1)S(1)} %bitcast.16), channel_id=1, source_target_pairs={{0,32},{16,48},{32,64},{48,80},{64,96},{80,112},{96,0},{112,16},{1... | collective-permute-start | bytes 786440 | tf_op jit(solution)/shard_map/ppermute | solution.py:396
  58.4 0.7 copy-start.2
  76.9 25.8 %all-to-all-start.2 = ((bf16[16,64,128]{2,1,0:T(8,128)(2,1)}), bf16[16,64,128]{2,1,0:T(8,128)(2,1)S(1)}, u32[]{:S(2)}, u32[]{:S(2)}) async-start(bf16[16,64,128]{2,1,0:T(8,128)(2,1)} %shard_map.112), calls=%async_computation.2 | async-start | bytes 524288 | tf_op jit(solution)/shard_map/all_to_all | solution.py:375
  85.1 17.6 %copy-start = (bf16[128,1024]{1,0:T(8,128)(2,1)S(1)}, bf16[128,1024]{1,0:T(8,128)(2,1)}, u32[]{:S(2)}) copy-start(bf16[128,1024]{1,0:T(8,128)(2,1)} %gate_ref.3) | copy-start | bytes 786436
  85.2 7.0 %collective-permute-start.8 = (bf16[2,32,1024]{2,1,0:T(8,128)(2,1)S(1)}, bf16[2,32,1024]{2,1,0:T(8,128)(2,1)S(1)}, u32[]{:S(2)}, u32[]{:S(2)}) collective-permute-start(bf16[2,32,1024]{2,1,0:T(8,128)(2,1)S(1)} %slice.15), channel_id=1, source_target_pairs={{0,96},{16,112},{32,0},{48,16},{64,32},{80,48},{96,64},{112,80},{1... | collective-permute-start | bytes 393224 | tf_op jit(solution)/shard_map/ppermute | solution.py:402
  88.8 8.1 %collective-permute-start.7 = (bf16[2,32,1024]{2,1,0:T(8,128)(2,1)S(1)}, bf16[2,32,1024]{2,1,0:T(8,128)(2,1)S(1)}, u32[]{:S(2)}, u32[]{:S(2)}) collective-permute-start(bf16[2,32,1024]{2,1,0:T(8,128)(2,1)S(1)} %slice.14), channel_id=1, source_target_pairs={{0,32},{16,48},{32,64},{48,80},{64,96},{80,112},{96,0},{112,16},{1... | collective-permute-start | bytes 393224 | tf_op jit(solution)/shard_map/ppermute | solution.py:401
  96.9 6.6 %copy-start.7 = (bf16[2,32,1024]{2,1,0:T(8,128)(2,1)}, bf16[2,32,1024]{2,1,0:T(8,128)(2,1)S(1)}, u32[]{:S(2)}) copy-start(bf16[2,32,1024]{2,1,0:T(8,128)(2,1)S(1)} %collective-permute-done.7.w2_low_ref) | copy-start | bytes 393220
  103.5 3.2 %collective-permute-start.9 = (bf16[16,32,128]{2,1,0:T(8,128)(2,1)S(1)}, bf16[16,32,128]{2,1,0:T(8,128)(2,1)S(1)}, u32[]{:S(2)}, u32[]{:S(2)}) collective-permute-start(bf16[16,32,128]{2,1,0:T(8,128)(2,1)S(1)} %get-tuple-element.35), channel_id=1, source_target_pairs={{0,16},{16,0},{32,48},{48,32},{64,80},{80,64},{96,112},{112,96},{1... | collective-permute-start | bytes 393224 | tf_op jit(solution)/shard_map/ppermute | solution.py:478
  108.2 23.8 %all-to-all-start.3 = ((bf16[16,32,1024]{2,1,0:T(8,128)(2,1)}), bf16[16,32,1024]{2,1,0:T(8,128)(2,1)S(1)}, u32[]{:S(2)}, u32[]{:S(2)}) async-start(bf16[16,32,1024]{2,1,0:T(8,128)(2,1)} %shard_map.114), calls=%async_computation.3 | async-start | bytes 2097152 | tf_op jit(solution)/shard_map/all_to_all | solution.py:375
  116.3 0.9 copy-start.3
  117.3 0.9 copy-start.8
  119.6 3.4 %collective-permute-start.10 = (f32[16,32,128]{2,1,0:T(8,128)S(1)}, f32[16,32,128]{2,1,0:T(8,128)S(1)}, u32[]{:S(2)}, u32[]{:S(2)}) collective-permute-start(f32[16,32,128]{2,1,0:T(8,128)S(1)} %get-tuple-element.40), channel_id=1, source_target_pairs={{0,16},{16,0},{32,48},{48,32},{64,80},{80,64},{96,112},{112,96},{1... | collective-permute-start | bytes 786440 | tf_op jit(solution)/shard_map/ppermute | solution.py:470

commit v5 on v4

--- a/solution.py
+++ b/solution.py
@@ -79,11 +79,18 @@
             )
 
 
-def user_edges(len_ref):
+PLACE = 4
+
+
+def place_of(info_ref, i):
+    return info_ref[info_ref.shape[0] - PLACE + i]
+
+
+def user_edges(info_ref):
     ends = []
     total = 0
-    for i in range(len_ref.shape[1]):
-        total = total + len_ref[0, i]
+    for i in range(info_ref.shape[0] - PLACE):
+        total = total + info_ref[i]
         ends.append(total)
     return ends
 
@@ -95,10 +102,10 @@
     return start
 
 
-def user_inverse(position, ends, len_ref):
-    length = jnp.full(position.shape, len_ref[0, 0], jnp.int32)
+def user_inverse(position, ends, info_ref):
+    length = jnp.full(position.shape, info_ref[0], jnp.int32)
     for i, end in enumerate(ends[:-1]):
-        length = jnp.where(position >= end, len_ref[0, i + 1], length)
+        length = jnp.where(position >= end, info_ref[i + 1], length)
     return 1.0 / length.astype(F32)
 
 
@@ -146,8 +153,8 @@
     return [lane_pair(ref, 2 * pair + i, rows) for i in range(2)]
 
 
-def forward_kernel(len_ref, qkv_ref, out_ref, k_nat, attn_ref):
-    ends = user_edges(len_ref)
+def forward_kernel(info_ref, qkv_ref, out_ref, k_nat, attn_ref):
+    ends = user_edges(info_ref)
     natural(qkv_ref, K_ROWS, k_nat)
     for pair in range(k_nat.shape[0] // 2):
         low, high = 2 * pair, 2 * pair + 1
@@ -183,17 +190,17 @@
         totals = lax.fori_loop(0, low - first, step, totals)
         for i, row in enumerate((low, high)):
             total = totals[i] + product(first, attn_ref[i])
-            total = total * user_inverse(places[i][0], ends, len_ref)
+            total = total * user_inverse(places[i][0], ends, info_ref)
             out_ref[2 * row] = total[:, :LANES].astype(BF16)
             out_ref[2 * row + 1] = total[:, LANES:].astype(BF16)
 
 
 def backward_kernel(
-    len_ref, qkv_ref, g_ref, out_ref, k_nat, v_nat, k_acc, v_acc, attn_ref, grad_ref
+    info_ref, qkv_ref, g_ref, out_ref, k_nat, v_nat, k_acc, v_acc, attn_ref, grad_ref
 ):
     blocks = v_nat.shape[0]
     scale = 1.0 / math.sqrt(DH)
-    ends = user_edges(len_ref)
+    ends = user_edges(info_ref)
     natural(qkv_ref, K_ROWS, k_nat)
     natural(qkv_ref, V_ROWS, v_nat)
     k_acc[...] = jnp.zeros_like(k_acc)
@@ -264,7 +271,7 @@
 
 
 def project_kernel(
-    place_ref, w0_ref, w1_ref, w2_low_ref, w2_high_ref, w3_ref, out_grad_ref, other_grad_ref, mine_ref, theirs_ref
+    info_ref, w0_ref, w1_ref, w2_low_ref, w2_high_ref, w3_ref, out_grad_ref, other_grad_ref, mine_ref, theirs_ref
 ):
     side, rows, width = w0_ref.shape
     tokens = out_grad_ref.shape[0]
@@ -275,9 +282,9 @@
         product = lax.dot_general(
             ref[...].reshape(count * rows, width), both, CONTRACT_LANES, preferred_element_type=F32
         )
-        y = lax.rem(place_ref[3] + side - y_back, side)
+        y = lax.rem(place_of(info_ref, 3) + side - y_back, side)
         for i in range(count):
-            x = lax.rem(place_ref[2] + side - x_first - i, side)
+            x = lax.rem(place_of(info_ref, 2) + side - x_first - i, side)
             mine_ref[x * side + y] = product[i * rows : (i + 1) * rows, :tokens]
             theirs_ref[x * side + y] = product[i * rows : (i + 1) * rows, tokens:]
 
@@ -297,9 +304,9 @@
     return mean, lax.rsqrt(var + 1e-05)
 
 
-def gated_kernel(place_ref, o_ref, gate_ref, mine_ref, other_ref):
+def gated_kernel(info_ref, o_ref, gate_ref, mine_ref, other_ref):
     half = DH // 2
-    even = place_ref[1] == 0
+    even = place_of(info_ref, 1) == 0
     mean, rstd = norm_stats(o_ref)
     for pair in range(o_ref.shape[0] // 2):
         gates = gate_ref[:, pair * 2 * DH : (pair + 1) * 2 * DH].T.astype(F32)
@@ -313,11 +320,11 @@
 
 
 def norm_kernel(
-    len_ref, place_ref, o_ref, mine_ref, recv_ref, gate_ref, grad_ref, gate_grad_ref, normed_grad_ref
+    info_ref, o_ref, mine_ref, recv_ref, gate_ref, grad_ref, gate_grad_ref, normed_grad_ref
 ):
     heads, _, tokens = o_ref.shape
     width = heads * DH
-    even = place_ref[1] == 0
+    even = place_of(info_ref, 1) == 0
     mean, rstd = norm_stats(o_ref)
     first = jnp.zeros((DH, tokens), F32)
     second = jnp.zeros((DH, tokens), F32)
@@ -340,8 +347,8 @@
         gate_grad_ref[:, cols] = jnp.concatenate(gate_grads, axis=0).T
     first = jnp.sum(first, axis=0, keepdims=True) * (1.0 / width)
     second = jnp.sum(second, axis=0, keepdims=True) * (1.0 / width)
-    position = place_ref[0] * tokens + lax.broadcasted_iota(jnp.int32, (1, tokens), 1)
-    weight = rstd * user_inverse(position, user_edges(len_ref), len_ref)
+    position = place_of(info_ref, 0) * tokens + lax.broadcasted_iota(jnp.int32, (1, tokens), 1)
+    weight = rstd * user_inverse(position, user_edges(info_ref), info_ref)
     for head in range(heads):
         normed = (o_ref[head].astype(F32) - mean) * rstd
         grad_ref[head] = ((normed_grad_ref[head] - first - normed * second) * weight).astype(BF16)
@@ -403,11 +410,6 @@
     return low, high
 
 
-def ring_blocks(block, axis):
-    back_one, back_three = ring_near(block, axis)
-    return (block, back_one) + ring_far(back_one, back_three, axis) + (back_three,)
-
-
 def local(query_rows, key_rows, value_rows, gate_rows, out_grad, proj_weight, user_lengths):
     ctx = lax.axis_size("ctx")
     dp = lax.axis_size("dp")
@@ -422,9 +424,8 @@
     partner = [(i, i ^ 1) for i in range(dp)]
     same_core = [[2 * i + core for i in range(chips)] for core in range(2)]
     chip = lax.axis_index("dp") // 2
-    place = jnp.stack(
-        [lax.axis_index("ctx"), lax.rem(lax.axis_index("dp"), 2), chip // SIDE, lax.rem(chip, SIDE)]
-    ).astype(jnp.int32)
+    place = [lax.axis_index("ctx"), lax.rem(lax.axis_index("dp"), 2), chip // SIDE, lax.rem(chip, SIDE)]
+    info = jnp.concatenate([user_lengths[0], jnp.stack(place).astype(jnp.int32)])
     in_hbm = pl.BlockSpec(memory_space=pltpu.HBM)
 
     block = call(
@@ -443,7 +444,10 @@
 
     block = block.reshape(ctx, width // LANES, out_rows // ctx, LANES).transpose(0, 2, 1, 3)
     block = block.reshape(out_rows, width)
-    column = jnp.concatenate(ring_blocks(block, "x"), axis=0).reshape(SIDE, out_rows, width)
+    column = [block] + [
+        lax.ppermute(block, "dp", plane_shift("x", step)) for step in range(1, SIDE)
+    ]
+    column = jnp.concatenate(column, axis=0).reshape(SIDE, out_rows, width)
     column, own_grad = lax.optimization_barrier((column, out_grad))
     near = ring_near(column, "y")
     other_grad = lax.ppermute(own_grad, "dp", partner)
@@ -456,7 +460,7 @@
         [pltpu.VMEM((blocks, TILE, DH), BF16), pltpu.VMEM((2, TILE, TILE), BF16)],
         flops=group * group * DH * 2,
         nbytes=5 * group * DH * 2,
-    )(user_lengths, qkv)
+    )(info, qkv)
     attn_out = exchange(attn_out, "ctx")
     attn_out, far = lax.optimization_barrier((attn_out, far))
 
@@ -466,7 +470,7 @@
         [SMEM] + [VMEM] * 7,
         flops=2 * tokens * width * width,
         nbytes=2 * width * width,
-    )(place, column, near[0], *far, near[1], out_grad, other_grad)
+    )(info, column, near[0], *far, near[1], out_grad, other_grad)
     received = lax.ppermute(theirs, "dp", partner)
 
     gated_mine, gated_other = call(
@@ -474,7 +478,7 @@
         [shape((heads, DH // 2, tokens), BF16)] * 2,
         [SMEM, VMEM, VMEM],
         nbytes=6 * tokens * width,
-    )(place, attn_out, gate_rows)
+    )(info, attn_out, gate_rows)
     other = lax.ppermute(gated_other, "dp", partner)
     partial = call(
         proj_kernel,
@@ -487,10 +491,10 @@
     grad, gate_grad = call(
         norm_kernel,
         [shape((heads, DH, tokens), BF16), shape((tokens, width), BF16)],
-        [SMEM, SMEM, VMEM, VMEM, VMEM, VMEM],
+        [SMEM, VMEM, VMEM, VMEM, VMEM],
         [pltpu.VMEM((heads, DH, tokens), F32)],
         nbytes=18 * tokens * width,
-    )(user_lengths, place, attn_out, mine, received, gate_rows)
+    )(info, attn_out, mine, received, gate_rows)
     grad = call(
         sum_kernel,
         shape((ctx, DH + w_rows, tokens), BF16),
@@ -513,7 +517,7 @@
         ],
         flops=3 * group * group * DH * 2,
         nbytes=7 * group * DH * 2,
-    )(user_lengths, qkv, grad)
+    )(info, qkv, grad)
     grads = exchange(grads, "ctx")
     query_grad, key_grad, value_grad, proj_grad = call(
         unpack_kernel,

time: 215 us -> 215 us (level)
  starting transfers between devices: 67.8 us -> 64 us
  waiting for transfers between devices: 44.4 us -> 48 us
    ppermute x0 -> x3, starting transfers between devices: none -> 9.89 us  [local(): lax.ppermute(block, 'dp', plane_shift('x', step))]
    ppermute x4 -> x2, starting transfers between devices: 13.9 us -> 6.84 us  [ring_near(): lax.ppermute(block, 'dp', plane_shift(axis, step))]
    ppermute x2 -> x1, starting transfers between devices: 7.46 us -> 1.92 us  [ring_far(): low = lax.ppermute(back_one[:half], 'dp', plane_shift(axis, 1))]
    all_to_all x4, waiting for transfers between devices: 25.2 us -> 27.9 us  [exchange(): lax.all_to_all(array, axis, split_axis=0, concat_axis=0, tiled=True, axis...]
    ppermute x0 -> x3, waiting for transfers between devices: none -> 2.28 us  [local(): lax.ppermute(block, 'dp', plane_shift('x', step))]
    ppermute x2 -> x1, starting transfers between devices: 5.56 us -> 4.75 us  [ring_far(): high = lax.ppermute(back_three[half:], 'dp', plane_shift(axis, -1))]
    ppermute x2 -> x1, waiting for transfers between devices: 6.3 us -> 5.56 us  [ring_far(): low = lax.ppermute(back_one[:half], 'dp', plane_shift(axis, 1))]
    unnamed x27 -> x23, local copies, waits for them, and re-layouts: 6.13 us -> 6.71 us
  transfers between devices with their start and end apart: 15 -> 14, of which waited for: 12 -> 12; matrix products, arithmetic and copies ran while one was open for 0% -> 0% of each run, Pallas kernels for 2% -> 2%
where the time goes in v5:
time: 215 us; the launch traced here: 212 us
  blocking collectives  72.6 us (34%)
  starting transfers between devices  64 us (30%)
  waiting for transfers between devices  48 us (22%)
  Pallas kernels  19.7 us (9%)
  local copies, waits for them, and re-layouts  6.82 us (3%)
    all_to_all x2, blocking collectives, exchange(): lax.all_to_all(array, axis, split_axis=0, concat_axis=0, tiled=True, axis...  72.6 us
    all_to_all x4, starting transfers between devices, exchange(): lax.all_to_all(array, axis, split_axis=0, concat_axis=0, tiled=True, axis...  34.9 us
    all_to_all x4, waiting for transfers between devices, exchange(): lax.all_to_all(array, axis, split_axis=0, concat_axis=0, tiled=True, axis...  27.9 us
    ppermute x3, starting transfers between devices, local(): lax.ppermute(block, 'dp', plane_shift('x', step))  9.89 us
    ppermute x2, waiting for transfers between devices, ring_near(): lax.ppermute(block, 'dp', plane_shift(axis, step))  8.83 us
    ppermute x2, starting transfers between devices, ring_near(): lax.ppermute(block, 'dp', plane_shift(axis, step))  6.84 us
    unnamed x23, local copies, waits for them, and re-layouts  6.71 us
    pallas_call x1, Pallas kernels, local(): call(backward_kernel, shape((ctx, 3 * DH + w_rows, tokens), BF16), [SMEM,...  6.06 us
  transfers between devices with their start and end apart: 14, of which 12 were waited for; matrix products, arithmetic and copies ran while one was open for 0% of the time, Pallas kernels for 2%

profile of v5, /device:TPU:6, one launch (start us, length us, event | category | flops | bytes accessed | tf_op | source)
XLA Modules:
  0.0 212.0 jit_solution(16477278410429320053)
XLA Ops:
  2.0 15.2 %all-to-all-start = ((bf16[16,16,128]{2,1,0:T(8,128)(2,1)}), bf16[16,16,128]{2,1,0:T(8,128)(2,1)S(1)}, u32[]{:S(2)}, u32[]{:S(2)}) async-start(bf16[16,16,128]{2,1,0:T(8,128)(2,1)} %shard_map.110), calls=%async_computation | async-start | bytes 131072 | tf_op jit(solution)/shard_map/all_to_all | solution.py:382
  20.0 1.4 shard_map.111
  21.4 8.5 %all-to-all-done = bf16[16,16,128]{2,1,0:T(8,128)(2,1)S(1)} async-done(((bf16[16,16,128]{2,1,0:T(8,128)(2,1)}), bf16[16,16,128]{2,1,0:T(8,128)(2,1)S(1)}, u32[]{:S(2)}, u32[]{:S(2)}) %all-to-all-start) | async-done | bytes 65568 | tf_op jit(solution)/shard_map/all_to_all | solution.py:382
  29.9 3.6 %all-to-all-start.1 = ((bf16[16,192,128]{2,1,0:T(8,128)(2,1)}), bf16[16,192,128]{2,1,0:T(8,128)(2,1)S(1)}, u32[]{:S(2)}, u32[]{:S(2)}) async-start(bf16[16,192,128]{2,1,0:T(8,128)(2,1)} %shard_map.111), calls=%async_computation.1 | async-start | bytes 1572864 | tf_op jit(solution)/shard_map/all_to_all | solution.py:382
  33.6 2.9 %collective-permute-start.2 = (bf16[32,1024]{1,0:T(8,128)(2,1)S(1)}, bf16[32,1024]{1,0:T(8,128)(2,1)S(1)}, u32[]{:S(2)}, u32[]{:S(2)}) collective-permute-start(bf16[32,1024]{1,0:T(8,128)(2,1)S(1)} %bitcast.19), channel_id=1, source_target_pairs={{0,384},{16,400},{32,416},{48,432},{64,448},{80,464},{96,480},{112... | collective-permute-start | bytes 196616 | tf_op jit(solution)/shard_map/ppermute | solution.py:448
  36.4 3.0 %collective-permute-start.1 = (bf16[32,1024]{1,0:T(8,128)(2,1)S(1)}, bf16[32,1024]{1,0:T(8,128)(2,1)S(1)}, u32[]{:S(2)}, u32[]{:S(2)}) collective-permute-start(bf16[32,1024]{1,0:T(8,128)(2,1)S(1)} %bitcast.20), channel_id=1, source_target_pairs={{0,256},{16,272},{32,288},{48,304},{64,320},{80,336},{96,352},{112... | collective-permute-start | bytes 196616 | tf_op jit(solution)/shard_map/ppermute | solution.py:448
  39.5 4.0 %collective-permute-start = (bf16[32,1024]{1,0:T(8,128)(2,1)S(1)}, bf16[32,1024]{1,0:T(8,128)(2,1)S(1)}, u32[]{:S(2)}, u32[]{:S(2)}) collective-permute-start(bf16[32,1024]{1,0:T(8,128)(2,1)S(1)} %bitcast.21), channel_id=1, source_target_pairs={{0,128},{16,144},{32,160},{48,176},{64,192},{80,208},{96,224},{112... | collective-permute-start | bytes 196616 | tf_op jit(solution)/shard_map/ppermute | solution.py:448
  44.1 1.7 collective-permute-done
  45.8 1.9 collective-permute-start.5
  47.7 4.9 %collective-permute-start.4 = (bf16[4,32,1024]{2,1,0:T(8,128)(2,1)S(1)}, bf16[4,32,1024]{2,1,0:T(8,128)(2,1)S(1)}, u32[]{:S(2)}, u32[]{:S(2)}) collective-permute-start(bf16[4,32,1024]{2,1,0:T(8,128)(2,1)S(1)} %bitcast.14), channel_id=1, source_target_pairs={{0,96},{16,112},{32,0},{48,16},{64,32},{80,48},{96,64},{112,80},{1... | collective-permute-start | bytes 786440 | tf_op jit(solution)/shard_map/ppermute | solution.py:403
  52.7 1.9 collective-permute-start.3
  55.4 3.5 %collective-permute-done.4.w3_ref = bf16[4,32,1024]{2,1,0:T(8,128)(2,1)S(1)} collective-permute-done((bf16[4,32,1024]{2,1,0:T(8,128)(2,1)S(1)}, bf16[4,32,1024]{2,1,0:T(8,128)(2,1)S(1)}, u32[]{:S(2)}, u32[]{:S(2)}) %collective-permute-start.4) | collective-permute-done | bytes 262176 | tf_op jit(solution)/shard_map/ppermute | solution.py:403
  58.9 5.3 %collective-permute-done.3.w1_ref = bf16[4,32,1024]{2,1,0:T(8,128)(2,1)S(1)} collective-permute-done((bf16[4,32,1024]{2,1,0:T(8,128)(2,1)S(1)}, bf16[4,32,1024]{2,1,0:T(8,128)(2,1)S(1)}, u32[]{:S(2)}, u32[]{:S(2)}) %collective-permute-start.3) | collective-permute-done | bytes 262176 | tf_op jit(solution)/shard_map/ppermute | solution.py:403
  64.2 7.6 %all-to-all-done.1.qkv_ref = bf16[16,192,128]{2,1,0:T(8,128)(2,1)S(1)} async-done(((bf16[16,192,128]{2,1,0:T(8,128)(2,1)}), bf16[16,192,128]{2,1,0:T(8,128)(2,1)S(1)}, u32[]{:S(2)}, u32[]{:S(2)}) %all-to-all-start.1) | async-done | bytes 786464 | tf_op jit(solution)/shard_map/all_to_all | solution.py:382
  71.8 4.8 %shard_map.112 = bf16[16,64,128]{2,1,0:T(8,128)(2,1)} custom-call(s32[8]{0:T(128)S(1)} %concatenate.6.info_ref, bf16[16,192,128]{2,1,0:T(8,128)(2,1)S(1)} %all-to-all-done.1.qkv_ref), custom_call_target="tpu_custom_call" | custom-call | flops 536870912 | bytes 1310720 | tf_op jit(solution)/shard_map/pallas_call | solution.py:456
  76.6 7.7 %all-to-all-start.2 = ((bf16[16,64,128]{2,1,0:T(8,128)(2,1)}), bf16[16,64,128]{2,1,0:T(8,128)(2,1)S(1)}, u32[]{:S(2)}, u32[]{:S(2)}) async-start(bf16[16,64,128]{2,1,0:T(8,128)(2,1)} %shard_map.112), calls=%async_computation.2 | async-start | bytes 524288 | tf_op jit(solution)/shard_map/all_to_all | solution.py:382
  84.4 4.7 %collective-permute-start.7 = (bf16[2,32,1024]{2,1,0:T(8,128)(2,1)S(1)}, bf16[2,32,1024]{2,1,0:T(8,128)(2,1)S(1)}, u32[]{:S(2)}, u32[]{:S(2)}) collective-permute-start(bf16[2,32,1024]{2,1,0:T(8,128)(2,1)S(1)} %slice.7), channel_id=1, source_target_pairs={{0,96},{16,112},{32,0},{48,16},{64,32},{80,48},{96,64},{112,80},{1... | collective-permute-start | bytes 393224 | tf_op jit(solution)/shard_map/ppermute | solution.py:409
  89.1 1.9 collective-permute-start.6
  91.6 5.6 %collective-permute-done.6.w2_low_ref = bf16[2,32,1024]{2,1,0:T(8,128)(2,1)S(1)} collective-permute-done((bf16[2,32,1024]{2,1,0:T(8,128)(2,1)S(1)}, bf16[2,32,1024]{2,1,0:T(8,128)(2,1)S(1)}, u32[]{:S(2)}, u32[]{:S(2)}) %collective-permute-start.6) | collective-permute-done | bytes 131104 | tf_op jit(solution)/shard_map/ppermute | solution.py:408
  97.9 4.7 %all-to-all-done.2.o_ref = bf16[16,64,128]{2,1,0:T(8,128)(2,1)S(1)} async-done(((bf16[16,64,128]{2,1,0:T(8,128)(2,1)}), bf16[16,64,128]{2,1,0:T(8,128)(2,1)S(1)}, u32[]{:S(2)}, u32[]{:S(2)}) %all-to-all-start.2) | async-done | bytes 262176 | tf_op jit(solution)/shard_map/all_to_all | solution.py:382
  103.4 1.9 collective-permute-start.8
  105.3 1.3 collective-permute-done.8.other_ref
  106.6 1.4 shard_map.114
  108.0 8.4 %all-to-all-start.3 = ((bf16[16,32,1024]{2,1,0:T(8,128)(2,1)}), bf16[16,32,1024]{2,1,0:T(8,128)(2,1)S(1)}, u32[]{:S(2)}, u32[]{:S(2)}) async-start(bf16[16,32,1024]{2,1,0:T(8,128)(2,1)} %shard_map.114), calls=%async_computation.3 | async-start | bytes 2097152 | tf_op jit(solution)/shard_map/all_to_all | solution.py:382
  118.3 1.5 shard_map.115
  119.7 1.9 collective-permute-start.9
  121.7 1.5 collective-permute-done.9.recv_ref
  123.2 1.8 shard_map.116
  125.0 7.1 %all-to-all-done.3.x_ref = bf16[16,32,1024]{2,1,0:T(8,128)(2,1)S(1)} async-done(((bf16[16,32,1024]{2,1,0:T(8,128)(2,1)}), bf16[16,32,1024]{2,1,0:T(8,128)(2,1)S(1)}, u32[]{:S(2)}, u32[]{:S(2)}) %all-to-all-start.3) | async-done | bytes 1048608 | tf_op jit(solution)/shard_map/all_to_all | solution.py:382
  132.3 24.7 %all_to_all.30.g_ref = bf16[16,80,128]{2,1,0:T(8,128)(2,1)S(1)} all-to-all(bf16[16,80,128]{2,1,0:T(8,128)(2,1)S(1)} %shard_map.117), channel_id=1, replica_groups=mesh['dp'=32,'ctx'=16] {'ctx'}, dimensions={0} | all-to-all | bytes 655360 | tf_op jit(solution)/shard_map/all_to_all | solution.py:382
  156.9 6.1 %shard_map.118 = bf16[16,208,128]{2,1,0:T(8,128)(2,1)S(1)} custom-call(s32[8]{0:T(128)S(1)} %concatenate.6.info_ref, bf16[16,192,128]{2,1,0:T(8,128)(2,1)S(1)} %all-to-all-done.1.qkv_ref, bf16[16,80,128]{2,1,0:T(8,128)(2,1)S(1)} %all_to_all.30.g_ref), custom_call_target="tpu_custom_call" | custom-call | flops 1610612736 | bytes 1835008 | tf_op jit(solution)/shard_map/pallas_call | solution.py:506
  163.0 47.9 %all_to_all.31.x_ref = bf16[16,208,128]{2,1,0:T(8,128)(2,1)S(1)} all-to-all(bf16[16,208,128]{2,1,0:T(8,128)(2,1)S(1)} %shard_map.118), channel_id=1, replica_groups=mesh['dp'=32,'ctx'=16] {'ctx'}, dimensions={0} | all-to-all | bytes 1703936 | tf_op jit(solution)/shard_map/all_to_all | solution.py:382
  (36 shorter events, 10.8 us)
Async XLA Ops:
  0.6 0.7 copy-start.9
  2.0 27.9 %all-to-all-start = ((bf16[16,16,128]{2,1,0:T(8,128)(2,1)}), bf16[16,16,128]{2,1,0:T(8,128)(2,1)S(1)}, u32[]{:S(2)}, u32[]{:S(2)}) async-start(bf16[16,16,128]{2,1,0:T(8,128)(2,1)} %shard_map.110), calls=%async_computation | async-start | bytes 131072 | tf_op jit(solution)/shard_map/all_to_all | solution.py:382
  17.2 1.0 copy-start.4
  18.1 0.9 copy-start.5
  19.1 0.9 copy-start.6
  29.9 41.9 %all-to-all-start.1 = ((bf16[16,192,128]{2,1,0:T(8,128)(2,1)}), bf16[16,192,128]{2,1,0:T(8,128)(2,1)S(1)}, u32[]{:S(2)}, u32[]{:S(2)}) async-start(bf16[16,192,128]{2,1,0:T(8,128)(2,1)} %shard_map.111), calls=%async_computation.1 | async-start | bytes 1572864 | tf_op jit(solution)/shard_map/all_to_all | solution.py:382
  33.5 12.2 %copy-start = (bf16[128,1024]{1,0:T(8,128)(2,1)S(1)}, bf16[128,1024]{1,0:T(8,128)(2,1)}, u32[]{:S(2)}) copy-start(bf16[128,1024]{1,0:T(8,128)(2,1)} %out_grad_ref.3) | copy-start | bytes 786436
  33.6 9.9 %collective-permute-start.2 = (bf16[32,1024]{1,0:T(8,128)(2,1)S(1)}, bf16[32,1024]{1,0:T(8,128)(2,1)S(1)}, u32[]{:S(2)}, u32[]{:S(2)}) collective-permute-start(bf16[32,1024]{1,0:T(8,128)(2,1)S(1)} %bitcast.19), channel_id=1, source_target_pairs={{0,384},{16,400},{32,416},{48,432},{64,448},{80,464},{96,480},{112... | collective-permute-start | bytes 196616 | tf_op jit(solution)/shard_map/ppermute | solution.py:448
  36.4 7.7 %collective-permute-start.1 = (bf16[32,1024]{1,0:T(8,128)(2,1)S(1)}, bf16[32,1024]{1,0:T(8,128)(2,1)S(1)}, u32[]{:S(2)}, u32[]{:S(2)}) collective-permute-start(bf16[32,1024]{1,0:T(8,128)(2,1)S(1)} %bitcast.20), channel_id=1, source_target_pairs={{0,256},{16,272},{32,288},{48,304},{64,320},{80,336},{96,352},{112... | collective-permute-start | bytes 196616 | tf_op jit(solution)/shard_map/ppermute | solution.py:448
  39.5 6.3 %collective-permute-start = (bf16[32,1024]{1,0:T(8,128)(2,1)S(1)}, bf16[32,1024]{1,0:T(8,128)(2,1)S(1)}, u32[]{:S(2)}, u32[]{:S(2)}) collective-permute-start(bf16[32,1024]{1,0:T(8,128)(2,1)S(1)} %bitcast.21), channel_id=1, source_target_pairs={{0,128},{16,144},{32,160},{48,176},{64,192},{80,208},{96,224},{112... | collective-permute-start | bytes 196616 | tf_op jit(solution)/shard_map/ppermute | solution.py:448
  45.8 9.6 %collective-permute-start.5 = (bf16[128,1024]{1,0:T(8,128)(2,1)S(1)}, bf16[128,1024]{1,0:T(8,128)(2,1)S(1)}, u32[]{:S(2)}, u32[]{:S(2)}) collective-permute-start(bf16[128,1024]{1,0:T(8,128)(2,1)S(1)} %copy-done), channel_id=1, source_target_pairs={{0,16},{16,0},{32,48},{48,32},{64,80},{80,64},{96,112},{112,96},{1... | collective-permute-start | bytes 786440 | tf_op jit(solution)/shard_map/ppermute | solution.py:453
  47.7 11.1 %collective-permute-start.4 = (bf16[4,32,1024]{2,1,0:T(8,128)(2,1)S(1)}, bf16[4,32,1024]{2,1,0:T(8,128)(2,1)S(1)}, u32[]{:S(2)}, u32[]{:S(2)}) collective-permute-start(bf16[4,32,1024]{2,1,0:T(8,128)(2,1)S(1)} %bitcast.14), channel_id=1, source_target_pairs={{0,96},{16,112},{32,0},{48,16},{64,32},{80,48},{96,64},{112,80},{1... | collective-permute-start | bytes 786440 | tf_op jit(solution)/shard_map/ppermute | solution.py:403
  52.7 11.5 %collective-permute-start.3 = (bf16[4,32,1024]{2,1,0:T(8,128)(2,1)S(1)}, bf16[4,32,1024]{2,1,0:T(8,128)(2,1)S(1)}, u32[]{:S(2)}, u32[]{:S(2)}) collective-permute-start(bf16[4,32,1024]{2,1,0:T(8,128)(2,1)S(1)} %bitcast.15), channel_id=1, source_target_pairs={{0,32},{16,48},{32,64},{48,80},{64,96},{80,112},{96,0},{112,16},{1... | collective-permute-start | bytes 786440 | tf_op jit(solution)/shard_map/ppermute | solution.py:403
  54.6 0.7 copy-start.10
  64.2 20.1 %copy-start.2 = (bf16[4,32,1024]{2,1,0:T(8,128)(2,1)}, bf16[4,32,1024]{2,1,0:T(8,128)(2,1)S(1)}, u32[]{:S(2)}) copy-start(bf16[4,32,1024]{2,1,0:T(8,128)(2,1)S(1)} %collective-permute-done.3.w1_ref) | copy-start | bytes 786436
  76.6 26.0 %all-to-all-start.2 = ((bf16[16,64,128]{2,1,0:T(8,128)(2,1)}), bf16[16,64,128]{2,1,0:T(8,128)(2,1)S(1)}, u32[]{:S(2)}, u32[]{:S(2)}) async-start(bf16[16,64,128]{2,1,0:T(8,128)(2,1)} %shard_map.112), calls=%async_computation.2 | async-start | bytes 524288 | tf_op jit(solution)/shard_map/all_to_all | solution.py:382
  84.3 18.3 %copy-start.1 = (bf16[128,1024]{1,0:T(8,128)(2,1)S(1)}, bf16[128,1024]{1,0:T(8,128)(2,1)}, u32[]{:S(2)}) copy-start(bf16[128,1024]{1,0:T(8,128)(2,1)} %gate_ref.3) | copy-start | bytes 786436
  84.4 7.3 %collective-permute-start.7 = (bf16[2,32,1024]{2,1,0:T(8,128)(2,1)S(1)}, bf16[2,32,1024]{2,1,0:T(8,128)(2,1)S(1)}, u32[]{:S(2)}, u32[]{:S(2)}) collective-permute-start(bf16[2,32,1024]{2,1,0:T(8,128)(2,1)S(1)} %slice.7), channel_id=1, source_target_pairs={{0,96},{16,112},{32,0},{48,16},{64,32},{80,48},{96,64},{112,80},{1... | collective-permute-start | bytes 393224 | tf_op jit(solution)/shard_map/ppermute | solution.py:409
  89.1 8.1 %collective-permute-start.6 = (bf16[2,32,1024]{2,1,0:T(8,128)(2,1)S(1)}, bf16[2,32,1024]{2,1,0:T(8,128)(2,1)S(1)}, u32[]{:S(2)}, u32[]{:S(2)}) collective-permute-start(bf16[2,32,1024]{2,1,0:T(8,128)(2,1)S(1)} %slice.6), channel_id=1, source_target_pairs={{0,32},{16,48},{32,64},{48,80},{64,96},{80,112},{96,0},{112,16},{1... | collective-permute-start | bytes 393224 | tf_op jit(solution)/shard_map/ppermute | solution.py:408
  97.2 0.7 copy-start.7
  103.4 3.2 %collective-permute-start.8 = (bf16[16,32,128]{2,1,0:T(8,128)(2,1)S(1)}, bf16[16,32,128]{2,1,0:T(8,128)(2,1)S(1)}, u32[]{:S(2)}, u32[]{:S(2)}) collective-permute-start(bf16[16,32,128]{2,1,0:T(8,128)(2,1)S(1)} %get-tuple-element.35), channel_id=1, source_target_pairs={{0,16},{16,0},{32,48},{48,32},{64,80},{80,64},{96,112},{112,96},{1... | collective-permute-start | bytes 393224 | tf_op jit(solution)/shard_map/ppermute | solution.py:482
  108.0 24.0 %all-to-all-start.3 = ((bf16[16,32,1024]{2,1,0:T(8,128)(2,1)}), bf16[16,32,1024]{2,1,0:T(8,128)(2,1)S(1)}, u32[]{:S(2)}, u32[]{:S(2)}) async-start(bf16[16,32,1024]{2,1,0:T(8,128)(2,1)} %shard_map.114), calls=%async_computation.3 | async-start | bytes 2097152 | tf_op jit(solution)/shard_map/all_to_all | solution.py:382
  116.4 0.9 copy-start.3
  117.4 0.9 copy-start.8
  119.7 3.4 %collective-permute-start.9 = (f32[16,32,128]{2,1,0:T(8,128)S(1)}, f32[16,32,128]{2,1,0:T(8,128)S(1)}, u32[]{:S(2)}, u32[]{:S(2)}) collective-permute-start(f32[16,32,128]{2,1,0:T(8,128)S(1)} %get-tuple-element.40), channel_id=1, source_target_pairs={{0,16},{16,0},{32,48},{48,32},{64,80},{80,64},{96,112},{112,96},{1... | collective-permute-start | bytes 786440 | tf_op jit(solution)/shard_map/ppermute | solution.py:474
